TPU v7x, 32 devices: a whole 2x2x4 slice. The times are simulated.
32 devices in a mesh: grp: 4 (over z), exp: 2 (over x), ten: 4 (over y, core).
Axes of the slice: x: 2, y: 2, z: 4, core: 2. Of those that a mesh axis runs over, the one named last changes fastest.
Arguments:
- tokens: bfloat16 [1024, 4096], P(('grp', 'exp', 'ten')), parts along dimension 0, may hold values from -100 to 100
- norm_gain: float32 [4096], replicated, may hold values from 0.1 to 1.9
- expert_ids: int32 [1024, 8], P(('grp', 'exp', 'ten')), parts along dimension 0, may hold values from 0 to 15, as said below
- gate_prob: float32 [1024, 8], P(('grp', 'exp', 'ten')), parts along dimension 0, may hold values from 0.05 to 1
- w_gate: bfloat16 [16, 4096, 1536], P('exp', None, 'ten'), may hold values from -0.09375 to 0.09375
- w_up: bfloat16 [16, 4096, 1536], P('exp', None, 'ten'), may hold values from -0.09375 to 0.09375
- w_down: bfloat16 [16, 1536, 4096], P('exp', 'ten'), may hold values from -0.15625 to 0.15625
Outputs:
- mixed: bfloat16 [1024, 4096], P(('grp', 'exp', 'ten')), parts along dimension 0
There are 4 independent parts, one for each index of `grp`. A program takes and returns all parts, laid end to end along the dimension named above; an argument that names none is the same for every part. Nothing has to cross between parts.
Inputs may be any that keep to these rules, and one draw needn't show every extreme that they name: `expert_ids`: each row names 8 different experts. Within the rows of one device no expert is named by more than 24 rows, and in every draw one expert is named by exactly 24 rows of every device.
All inputs are finite; a program needn't handle non-finite values.
Results may differ from a plain program's by a relative error of at most 0.012.
Values may be sent and summed in bfloat16 or wider, within the bound.
No kernel may reach another device: no remote copies, remote signals or barrier semaphores. Data moves between devices by JAX's collectives and lax.ppermute only.
A program may use at most 192 MiB of HBM per device.

v0:
```python
import jax
import jax.numpy as jnp
from jax import lax
from jax.sharding import PartitionSpec as P


def expert_pass(piece, w_gate, w_up, w_down):
    gate_part = jnp.einsum("abecd,edf->abecf", piece, w_gate, preferred_element_type=jnp.float32)
    up_part = jnp.einsum("abecd,edf->abecf", piece, w_up, preferred_element_type=jnp.float32)
    hidden = (jax.nn.silu(gate_part) * up_part).astype(jnp.bfloat16)
    return jnp.einsum("abecf,efd->abecd", hidden, w_down, preferred_element_type=jnp.float32)


def per_device(tokens, norm_gain, expert_ids, gate_prob, w_gate, w_up, w_down):
    tok_rows, width = tokens.shape
    top_count = expert_ids.shape[1]
    exp_count = lax.axis_size("exp")
    ten_count = lax.axis_size("ten")
    local_count = w_gate.shape[0]
    expert_count = local_count * exp_count
    capacity = 3 * tok_rows // 4
    floats = tokens.astype(jnp.float32)
    meansq = jnp.mean(floats * floats, axis=1, keepdims=True)
    normed = (floats * lax.rsqrt(meansq + 1e-06) * norm_gain).astype(jnp.bfloat16)
    mixing = gate_prob / jnp.sum(gate_prob, axis=1, keepdims=True)
    flat_ids = expert_ids.reshape(-1)
    member = (flat_ids[:, None] == jnp.arange(expert_count, dtype=jnp.int32)[None, :]).astype(
        jnp.int32
    )
    earlier = jnp.cumsum(member, axis=0) - member
    slot_index = jnp.sum(earlier * member, axis=1)
    target = flat_ids * capacity + slot_index
    placing = jnp.arange(expert_count * capacity, dtype=jnp.int32)[:, None] == target[None, :]
    placing = jnp.any(placing.reshape(expert_count * capacity, tok_rows, top_count), axis=2).astype(
        jnp.bfloat16
    )
    outgoing = jnp.dot(placing, normed, preferred_element_type=jnp.float32).astype(jnp.bfloat16)
    outgoing = outgoing.reshape(exp_count, local_count, capacity, width)
    arrived = lax.all_to_all(outgoing, "exp", split_axis=0, concat_axis=0, tiled=True)
    arrived = arrived.reshape(exp_count, 1, local_count, capacity, width)
    partial_value = expert_pass(
        lax.all_gather(arrived, "ten", axis=1, tiled=True), w_gate, w_up, w_down
    )
    sendback = partial_value.astype(jnp.bfloat16).reshape(
        exp_count * ten_count, local_count * capacity, width
    )
    returned = lax.all_to_all(sendback, ("exp", "ten"), split_axis=0, concat_axis=0, tiled=True)
    returned = returned.reshape(exp_count, ten_count, local_count * capacity, width)
    combined = jnp.sum(returned, axis=1, dtype=jnp.float32).astype(jnp.bfloat16)
    combined = combined.reshape(expert_count * capacity, width)
    picked = jnp.take(combined, target, axis=0).reshape(tok_rows, top_count, width)
    mixed = jnp.sum(mixing[:, :, None] * picked.astype(jnp.float32), axis=1)
    return mixed.astype(jnp.bfloat16)


def solution(mesh):
    placed = (
        P(("grp", "exp", "ten"), None),
        P(),
        P(("grp", "exp", "ten"), None),
        P(("grp", "exp", "ten"), None),
        P("exp", None, "ten"),
        P("exp", None, "ten"),
        P("exp", "ten", None),
    )
    return jax.shard_map(
        per_device,
        mesh=mesh,
        in_specs=placed,
        out_specs=P(("grp", "exp", "ten"), None),
        check_vma=False,
    )
```

profile of v0, /device:TPU:0, one launch (start us, length us, event | category | flops | bytes accessed | tf_op | source)
XLA Modules:
  0.0 368.9 jit_solution(4669418831246202869)
XLA Ops:
  6.5 0.8 copy.19
  7.3 0.1 eq.40
  7.4 0.1 reshape.105
  7.5 0.6 reduce-window.6
  8.1 0.2 slice_reduce_fusion
  8.3 0.1 fusion.27
  8.4 0.1 reduce_sum.54
  8.5 0.2 fusion.21
  8.7 1.1 fusion.18
  9.8 2.0 convolution_convert_fusion
  11.8 41.1 %all_to_all.10 = bf16[2,8,24,4096]{3,2,1,0:T(8,128)(2,1)} all-to-all(bf16[2,8,24,4096]{3,2,1,0:T(8,128)(2,1)S(1)} %bitcast.73), channel_id=1, replica_groups=mesh['grp'=4,'exp'=2,'ten'=4] {'exp'}, dimensions={0} | all-to-all | bytes 6291456 | tf_op jit(solution)/shard_map/all_to_all | solution.py:39
  53.0 0.0 all-gather.3.cloned.1.call-update
  53.0 82.9 %all-gather.3.cloned.1.call-done = bf16[2,32,24,4096]{3,2,1,0:T(8,128)(2,1)} async-done(((bf16[2,8,24,4096]{3,2,1,0:T(8,128)(2,1)}), bf16[2,32,24,4096]{3,2,1,0:T(8,128)(2,1)}) %all-gather.3.cloned.1.call-update) | async-done | bytes 12582928 | tf_op jit(solution)/shard_map/all_gather | solution.py:42
  135.9 16.6 %fusion.2 = f32[8,2,4,24,384]{4,3,2,1,0:T(8,128)} fusion(bf16[8,4096,384]{2,1,0:T(8,128)(2,1)} %param.12, bf16[2,4,8,24,4096]{4,3,2,1,0:T(8,128)(2,1)} %bitcast.76), kind=kOutput, calls=%fused_computation.3 | convolution fusion | flops 4831838208 | bytes 40108032 | tf_op jit(solution)/shard_map/abecd,edf->abecf/dot_general | solution.py:9
  152.5 20.2 %fusion.10 = bf16[2,4,8,24,384]{4,3,1,0,2:T(8,128)(2,1)S(1)} fusion(f32[8,2,4,24,384]{4,3,2,1,0:T(8,128)} %fusion.2, bf16[8,4096,384]{2,1,0:T(8,128)(2,1)} %param.11, bf16[2,4,8,24,4096]{4,3,2,1,0:T(8,128)(2,1)} %bitcast.77), kind=kOutput, calls=%fused_computation.14 | convolution fusion | flops 4835377152 | bytes 41287680 | tf_op jit(solution)/shard_map/abecd,edf->abecf/dot_general | solution.py:8
  172.7 20.6 %convert_bitcast_fusion = bf16[2,4,8,24,4096]{4,3,1,0,2:T(8,128)(2,1)} fusion(bf16[2,4,8,24,384]{4,3,1,0,2:T(8,128)(2,1)S(1)} %fusion.10, bf16[8,384,4096]{2,1,0:T(8,128)(2,1)} %param.13), kind=kOutput, calls=%fused_computation.8 | convolution fusion | flops 4838129664 | bytes 38928384 | tf_op jit(solution)/shard_map/abecf,efd->abecd/dot_general | solution.py:11
  193.3 10.7 %copy.25 = bf16[2,4,8,24,4096]{4,3,2,1,0:T(8,128)(2,1)} copy(bf16[2,4,8,24,4096]{4,3,1,0,2:T(8,128)(2,1)} %convert_bitcast_fusion) | data formatting | bytes 25165824 | tf_op jit(solution)/shard_map/convert_element_type | solution.py:44
  203.9 5.5 %all-to-all-start.1 = ((bf16[8,192,4096]{2,1,0:T(8,128)(2,1)}), bf16[8,192,4096]{2,1,0:T(8,128)(2,1)}, u32[]{:S(2)}, u32[]{:S(2)}) async-start(bf16[8,192,4096]{2,1,0:T(8,128)(2,1)} %bitcast.72), calls=%async_computation.1 | async-start | bytes 25165824 | tf_op jit(solution)/shard_map/all_to_all | solution.py:47
  209.5 0.1 mul.71
  209.6 0.1 copy.18
  209.7 137.8 %all-to-all-done.1 = bf16[8,192,4096]{2,1,0:T(8,128)(2,1)} async-done(((bf16[8,192,4096]{2,1,0:T(8,128)(2,1)}), bf16[8,192,4096]{2,1,0:T(8,128)(2,1)}, u32[]{:S(2)}, u32[]{:S(2)}) %all-to-all-start.1) | async-done | bytes 12582944 | tf_op jit(solution)/shard_map/all_to_all | solution.py:47
  347.5 7.1 %bitcast_reduce_fusion = bf16[2,192,4096]{2,1,0:T(8,128)(2,1)S(1)} fusion(bf16[8,192,4096]{2,1,0:T(8,128)(2,1)} %all-to-all-done.1), kind=kLoop, calls=%fused_computation.7 | loop fusion | flops 4718592 | bytes 15728640 | tf_op jit(solution)/shard_map/reduce_sum | solution.py:49
  354.6 3.2 gather_fusion
  357.8 4.2 %multiply_reduce_fusion = bf16[32,4096]{1,0:T(8,128)(2,1)} fusion(bf16[256,4096]{1,0:T(8,128)(2,1)} %gather_fusion, f32[32,8]{1,0:T(8,128)S(1)} %copy.18, pred[32,8]{1,0:T(8,128)(4,1)S(1)} %get-tuple-element.5), kind=kLoop, calls=%fused_computation.12 | loop fusion | flops 4063232 | bytes 2360576 | tf_op jit(solution)/shard_map/reduce_sum | solution.py:52
  (13 shorter events, 0.1 us)
Async XLA Ops:
  6.5 129.3 %all-gather.3.cloned.1.call-start = ((), (), s32[]{:S(2)}) async-start(), calls=%async_computation.2 | async-start | bytes 15728640 | tf_op jit(solution)/shard_map/all_gather | solution.py:42
  203.9 5.6 %copy-start = (f32[32,8]{0,1:T(8,128)S(1)}, f32[32,8]{0,1:T(8,128)}, u32[]{:S(2)}) copy-start(f32[32,8]{0,1:T(8,128)} %param.10) | copy-start | bytes 3076
  203.9 143.6 %all-to-all-start.1 = ((bf16[8,192,4096]{2,1,0:T(8,128)(2,1)}), bf16[8,192,4096]{2,1,0:T(8,128)(2,1)}, u32[]{:S(2)}, u32[]{:S(2)}) async-start(bf16[8,192,4096]{2,1,0:T(8,128)(2,1)} %bitcast.72), calls=%async_computation.1 | async-start | bytes 25165824 | tf_op jit(solution)/shard_map/all_to_all | solution.py:47
Sparse Core Ops, SparseCore 0:
  53.1 82.7 all-gather.2
where the time goes:
time: 369 us
  waiting for transfers between devices  221 us (60%)
  matrix products  59.4 us (16%)
  blocking collectives  41.1 us (11%)
  local copies, waits for them, and re-layouts  15.2 us (4%)
  between operations  13.5 us (4%)
  other arithmetic  13.4 us (4%)
  starting transfers between devices  5.52 us (1%)
    all_to_all x1, waiting for transfers between devices, per_device(): lax.all_to_all(sendback, ('exp', 'ten'), split_axis=0, concat_axis=0, til...  138 us
    all_gather x1, waiting for transfers between devices, per_device(): lax.all_gather(arrived, 'ten', axis=1, tiled=True)  82.9 us
    all_to_all x1, blocking collectives, per_device(): lax.all_to_all(outgoing, 'exp', split_axis=0, concat_axis=0, tiled=True)  41.1 us
    dot_general x1, matrix products, expert_pass(): jnp.einsum('abecf,efd->abecd', hidden, w_down, preferred_element_type=jnp...  20.6 us
    dot_general x1, matrix products, expert_pass(): jnp.einsum('abecd,edf->abecf', piece, w_gate, preferred_element_type=jnp....  20.2 us
    dot_general x1, matrix products, expert_pass(): jnp.einsum('abecd,edf->abecf', piece, w_up, preferred_element_type=jnp.fl...  16.6 us
    convert_element_type x1, local copies, waits for them, and re-layouts, per_device(): partial_value.astype(jnp.bfloat16)  10.7 us
  transfers between devices with their start and end apart: 2, of which 2 were waited for; matrix products, arithmetic and copies ran while one was open for 0% of the time, Pallas kernels for 0%

commit v1 on v0

v1 whole, which is shorter than its diff:
```python
import jax
import jax.numpy as jnp
from jax import lax
from jax.sharding import PartitionSpec as P


def per_device(tokens, norm_gain, expert_ids, gate_prob, w_gate, w_up, w_down):
    tok_rows, width = tokens.shape
    local_count = w_gate.shape[0]
    floats = tokens.astype(jnp.float32)
    meansq = jnp.mean(floats * floats, axis=1, keepdims=True)
    normed = (floats * lax.rsqrt(meansq + 1e-06) * norm_gain).astype(jnp.bfloat16)
    mixing = gate_prob / jnp.sum(gate_prob, axis=1, keepdims=True)
    expert_count = local_count * lax.axis_size("exp")
    chosen = expert_ids[:, :, None] == jnp.arange(expert_count, dtype=jnp.int32)
    weight = jnp.sum(jnp.where(chosen, mixing[:, :, None], 0.0), axis=1)
    rows = lax.all_gather(normed, ("exp", "ten"), axis=0, tiled=True)
    weight = lax.all_gather(weight, ("exp", "ten"), axis=0, tiled=True)
    weight = lax.dynamic_slice_in_dim(weight, lax.axis_index("exp") * local_count, local_count, axis=1)
    gate_part = jnp.einsum("td,edf->etf", rows, w_gate, preferred_element_type=jnp.float32)
    up_part = jnp.einsum("td,edf->etf", rows, w_up, preferred_element_type=jnp.float32)
    hidden = (jax.nn.silu(gate_part) * up_part * weight.T[:, :, None]).astype(jnp.bfloat16)
    part = jnp.einsum("etf,efd->td", hidden, w_down, preferred_element_type=jnp.float32)
    return lax.psum_scatter(
        part.astype(jnp.bfloat16), ("exp", "ten"), scatter_dimension=0, tiled=True
    )


def solution(mesh):
    placed = (
        P(("grp", "exp", "ten"), None),
        P(),
        P(("grp", "exp", "ten"), None),
        P(("grp", "exp", "ten"), None),
        P("exp", None, "ten"),
        P("exp", None, "ten"),
        P("exp", "ten", None),
    )
    return jax.shard_map(
        per_device,
        mesh=mesh,
        in_specs=placed,
        out_specs=P(("grp", "exp", "ten"), None),
        check_vma=False,
    )
```

time: 369 us -> 129 us (0.35)
  waiting for transfers between devices: 221 us -> 59.2 us
  blocking collectives: 41.1 us -> 10.7 us
  matrix products: 59.4 us -> 40.6 us
  local copies, waits for them, and re-layouts: 15.2 us -> 0.12 us
  other arithmetic: 13.4 us -> 5.01 us
  starting transfers between devices: 5.52 us -> 0.04 us
    all_to_all x1 -> x0, waiting for transfers between devices: 138 us -> none  [per_device(): lax.all_to_all(sendback, ('exp', 'ten'), split_axis=0, concat_axis=0, til...]
    all_gather x1, waiting for transfers between devices: 82.9 us -> 17.8 us  [per_device(): rows = lax.all_gather(normed, ('exp', 'ten'), axis=0, tiled=True)]
    reduce_scatter x0 -> x1, waiting for transfers between devices: none -> 41.4 us  [per_device(): lax.psum_scatter(part.astype(jnp.bfloat16), ('exp', 'ten'), scatter_dimen...]
    all_to_all x1 -> x0, blocking collectives: 41.1 us -> none  [per_device(): lax.all_to_all(outgoing, 'exp', split_axis=0, concat_axis=0, tiled=True)]
    dot_general x4 -> x3, matrix products: 59.4 us -> 40.6 us  [the longest x1 15.4 us: per_device(): jnp.einsum('td,edf->etf', rows, w_up, preferred_element_type=jnp.float32)]
    reduce_sum x3 -> x1, other arithmetic: 11.4 us -> 0.71 us  [per_device(): weight = jnp.sum(jnp.where(chosen, mixing[:, :, None], 0.0), axis=1)]
    all_gather x0 -> x1, blocking collectives: none -> 10.7 us  [per_device(): weight = lax.all_gather(weight, ('exp', 'ten'), axis=0, tiled=True)]
    convert_element_type x1 -> x0, local copies, waits for them, and re-layouts: 10.7 us -> none  [per_device(): partial_value.astype(jnp.bfloat16)]
  transfers between devices with their start and end apart: 2 -> 2, of which waited for: 2 -> 2; matrix products, arithmetic and copies ran while one was open for 0% -> 2% of each run, Pallas kernels for 0% -> 0%
where the time goes in v1:
time: 129 us
  waiting for transfers between devices  59.2 us (46%)
  matrix products  40.6 us (31%)
  between operations  13.4 us (10%)
  blocking collectives  10.7 us (8%)
  other arithmetic  5.01 us (4%)
    reduce_scatter x1, waiting for transfers between devices, per_device(): lax.psum_scatter(part.astype(jnp.bfloat16), ('exp', 'ten'), scatter_dimen...  41.4 us
    all_gather x1, waiting for transfers between devices, per_device(): rows = lax.all_gather(normed, ('exp', 'ten'), axis=0, tiled=True)  17.8 us
    dot_general x1, matrix products, per_device(): jnp.einsum('td,edf->etf', rows, w_up, preferred_element_type=jnp.float32)  15.4 us
    dot_general x1, matrix products, per_device(): jnp.einsum('etf,efd->td', hidden, w_down, preferred_element_type=jnp.floa...  13.4 us
    dot_general x1, matrix products, per_device(): jnp.einsum('td,edf->etf', rows, w_gate, preferred_element_type=jnp.float32)  11.8 us
    all_gather x1, blocking collectives, per_device(): weight = lax.all_gather(weight, ('exp', 'ten'), axis=0, tiled=True)  10.7 us
  transfers between devices with their start and end apart: 2, of which 2 were waited for; matrix products, arithmetic and copies ran while one was open for 2% of the time, Pallas kernels for 0%

profile of v1, /device:TPU:0, one launch (start us, length us, event | category | flops | bytes accessed | tf_op | source)
XLA Modules:
  0.0 129.1 jit_solution(12407627924592515004)
XLA Ops:
  6.5 0.0 all-gather.3.cloned.1.call-start
  6.5 1.1 fusion.16
  7.7 1.8 %fusion.18 = bf16[32,4096]{1,0:T(8,128)(2,1)} fusion(bf16[32,4096]{1,0:T(8,128)(2,1)} %param.7, f32[4096]{0:T(1024)} %param.8, f32[32]{0:T(128)S(1)} %add_rsqrt_fusion), kind=kLoop, calls=%fused_computation.20 | loop fusion | flops 524288 | bytes 540800 | tf_op jit(solution)/shard_map/convert_element_type | solution.py:12
  9.4 0.0 all-gather.3.cloned.1.call-update
  9.5 0.0 reduce-scatter.2.cloned.1.call-start
  9.5 0.7 reduce_sum.28
  10.2 0.7 broadcast_divide_fusion
  10.9 0.7 select_reduce_fusion
  11.6 10.7 %all-gather = f32[8,32,16]{1,2,0:T(8,128)S(1)} all-gather(f32[1,32,16]{1,2,0:T(8,128)S(1)} %bitcast.59), channel_id=1, replica_groups=mesh['grp'=4,'exp'=2,'ten'=4] {'exp','ten'}, dimensions={0}, use_global_device_ids=true | all-gather | bytes 18432 | tf_op jit(solution)/shard_map/all_gather | solution.py:18
  22.3 0.1 reshape.14
  22.5 17.8 %all-gather.3.cloned.1.call-done = bf16[256,4096]{1,0:T(8,128)(2,1)} async-done(((bf16[32,4096]{1,0:T(8,128)(2,1)}), bf16[256,4096]{1,0:T(8,128)(2,1)}) %all-gather.3.cloned.1.call-update) | async-done | bytes 2097168 | tf_op jit(solution)/shard_map/all_gather | solution.py:17
  40.2 0.0 copy-start
  40.2 15.4 %fusion.6 = f32[256,8,384]{2,0,1:T(8,128)S(1)} fusion(bf16[8,4096,384]{2,1,0:T(8,128)(2,1)} %param.12, bf16[256,4096]{1,0:T(8,128)(2,1)} %all-gather.3.cloned.1.call-done), kind=kOutput, calls=%fused_computation.10 | convolution fusion | flops 6442450944 | bytes 30408704 | tf_op jit(solution)/shard_map/td,edf->etf/dot_general | solution.py:21
  55.6 0.0 copy-done
  55.6 11.8 %fusion.2.clone.4 = bf16[8,256,384]{2,1,0:T(8,128)(2,1)S(1)} fusion(f32[256,8,384]{2,0,1:T(8,128)S(1)} %fusion.6, bf16[8,4096,384]{2,1,0:T(8,128)(2,1)} %param.11, bf16[256,4096]{1,0:T(8,128)(2,1)S(1)} %copy-done, f32[8,256]{1,0:T(8,128)S(1)} %dynamic-slice_bitcast_fusion), kind=kOutput, calls=%fused_computation.4.clone.clone.clone.1 | convolution fusion | flops 6447955968 | bytes 31989760 | tf_op jit(solution)/shard_map/td,edf->etf/dot_general | solution.py:20
  67.4 13.4 %fusion = bf16[256,4096]{1,0:T(8,128)(2,1)} fusion(bf16[8,384,4096]{2,1,0:T(8,128)(2,1)} %param.13, bf16[8,256,384]{2,1,0:T(8,128)(2,1)S(1)} %fusion.2.clone.4), kind=kOutput, calls=%fused_computation.1 | convolution fusion | flops 6443499520 | bytes 28835840 | tf_op jit(solution)/shard_map/etf,efd->td/dot_general | solution.py:23
  80.9 0.0 reduce-scatter.2.cloned.1.call-update
  80.9 41.4 %reduce-scatter.2.cloned.1.call-done = bf16[32,4096]{1,0:T(8,128)(2,1)} async-done(((bf16[256,4096]{1,0:T(8,128)(2,1)}), bf16[32,4096]{1,0:T(8,128)(2,1)}) %reduce-scatter.2.cloned.1.call-update) | async-done | bytes 262160 | tf_op jit(solution)/shard_map/reduce_scatter | solution.py:24
  (3 shorter events, 0.0 us)
Async XLA Ops:
  6.5 33.7 %all-gather.3.cloned.1.call-start = ((), (), s32[]{:S(2)}) async-start(), calls=%async_computation.1 | async-start | bytes 2359296 | tf_op jit(solution)/shard_map/all_gather | solution.py:17
  9.5 112.8 %reduce-scatter.2.cloned.1.call-start = ((), (), s32[]{:S(2)}) async-start(), calls=%async_computation.2 | async-start | bytes 2359296 | tf_op jit(solution)/shard_map/reduce_scatter | solution.py:24
  40.2 15.4 %copy-start = (bf16[256,4096]{1,0:T(8,128)(2,1)S(1)}, bf16[256,4096]{1,0:T(8,128)(2,1)}, u32[]{:S(2)}) copy-start(bf16[256,4096]{1,0:T(8,128)(2,1)} %all-gather.3.cloned.1.call-done) | copy-start | bytes 6291460
Sparse Core Ops, SparseCore 0:
  9.6 30.5 all-gather.2
  81.0 41.1 reduce-scatter.1

commit v2 on v1

v2 whole, which is shorter than its diff:
```python
import functools

import jax
import jax.numpy as jnp
from jax import lax
from jax.experimental import pallas as pl
from jax.experimental.pallas import tpu as pltpu
from jax.sharding import PartitionSpec as P

BF16 = jnp.bfloat16
F32 = jnp.float32
MIB = 2**20
GROUP = ("exp", "ten")
EXTRA = 128
IN_CHUNKS = 4
OUT_CHUNKS = 4
VMEM_FULL = pl.BlockSpec(memory_space=pltpu.VMEM)


def in_vmem(value):
    return pltpu.with_memory_space_constraint(value, pltpu.VMEM)


def in_hbm(value):
    return pltpu.with_memory_space_constraint(value, pltpu.HBM)


def exchange(value, size, mask):
    return lax.ppermute(value, GROUP, [(i, i ^ mask) for i in range(size)])


def after(value, other):
    return lax.optimization_barrier((value, other))[0]


def norm_body(expert_count, tok_ref, gain_ref, ids_ref, prob_ref, *outs):
    floats = tok_ref[...].astype(F32)
    meansq = jnp.mean(floats * floats, axis=1, keepdims=True)
    normed = (floats * lax.rsqrt(meansq + 1e-06) * gain_ref[...]).astype(BF16)
    prob = prob_ref[...]
    mixing = prob / jnp.sum(prob, axis=1, keepdims=True)
    lane = lax.broadcasted_iota(jnp.int32, (prob.shape[0], EXTRA), 1)
    weight = jnp.zeros((prob.shape[0], EXTRA), F32)
    for k in range(prob.shape[1]):
        weight = weight + jnp.where(
            lane % expert_count == ids_ref[:, k : k + 1], mixing[:, k : k + 1], 0.0
        )
    high = weight.astype(BF16).astype(F32)
    middle = (weight - high).astype(BF16).astype(F32)
    low = weight - high - middle
    piece = lane // expert_count
    packed = jnp.where(piece == 0, high, jnp.where(piece == 1, middle, jnp.where(piece == 2, low, 0.0)))
    step = normed.shape[1] // len(outs)
    for j, out in enumerate(outs):
        out[:, :step] = normed[:, j * step : (j + 1) * step]
    outs[-1][:, step:] = packed.astype(BF16)


def norm_call(tokens, norm_gain, expert_ids, gate_prob, expert_count):
    rows, width = tokens.shape
    step = width // IN_CHUNKS
    shapes = [
        pltpu.VMEM((rows, step + (EXTRA if j == IN_CHUNKS - 1 else 0)), BF16)
        for j in range(IN_CHUNKS)
    ]
    return pl.pallas_call(
        functools.partial(norm_body, expert_count),
        out_shape=shapes,
        in_specs=[VMEM_FULL] * 4,
        out_specs=[VMEM_FULL] * IN_CHUNKS,
    )(tokens, norm_gain.reshape(1, width), expert_ids, gate_prob)


def gate_up_body(first, last, step, hidden, expert_count, parts, *refs):
    pieces, refs = refs[:parts], refs[parts:]
    gate_ref, up_ref = refs[:2]
    total_ref = None if first else refs[2]
    out_ref, rows_ref = refs[-2:]
    expert = pl.program_id(0)

    @pl.when(expert == 0)
    def _():
        at = 0
        for piece in pieces:
            rows_ref[at : at + piece.shape[0]] = piece[...]
            at += piece.shape[0]

    weights = jnp.concatenate([gate_ref[0], up_ref[0]], axis=1)
    both = jnp.dot(rows_ref[:, :step], weights, preferred_element_type=F32)
    if not first:
        both = both + total_ref[expert]
    if not last:
        out_ref[expert] = both
        return
    gate, up = both[:, :hidden], both[:, hidden:]
    number = lax.axis_index("exp") * pl.num_programs(0) + expert
    row = lax.broadcasted_iota(jnp.int32, (EXTRA, hidden), 0)
    pick = jnp.where((row % expert_count == number) & (row < 3 * expert_count), 1.0, 0.0)
    mixing = jnp.dot(rows_ref[:, step:], pick.astype(BF16), preferred_element_type=F32)
    out_ref[...] = (gate / (1.0 + jnp.exp(-gate)) * up * mixing).astype(BF16)


def gate_up_call(j, pieces, w_gate, w_up, total, expert_count):
    first, last = j == 0, j == IN_CHUNKS - 1
    local, width, hidden = w_gate.shape
    step = width // IN_CHUNKS
    rows = sum(p.shape[0] for p in pieces)
    weight_spec = pl.BlockSpec((1, step, hidden), lambda e: (e, j, 0))
    totals = [] if first else [total]
    if last:
        out_shape = pltpu.VMEM((rows, local * hidden), BF16)
        out_spec = pl.BlockSpec((rows, hidden), lambda e: (0, e))
    else:
        out_shape = pltpu.VMEM((local, rows, 2 * hidden), F32)
        out_spec = VMEM_FULL
    return pl.pallas_call(
        functools.partial(gate_up_body, first, last, step, hidden, expert_count, len(pieces)),
        grid=(local,),
        out_shape=out_shape,
        in_specs=[VMEM_FULL] * len(pieces) + [weight_spec] * 2 + [VMEM_FULL] * len(totals),
        out_specs=out_spec,
        scratch_shapes=[pltpu.VMEM((rows, pieces[0].shape[1]), BF16)],
        input_output_aliases={} if first or last else {len(pieces) + 2: 0},
        compiler_params=pltpu.CompilerParams(vmem_limit_bytes=16 * MIB),
        cost_estimate=pl.CostEstimate(
            flops=4 * rows * step * hidden * local,
            bytes_accessed=4 * step * hidden * local,
            transcendentals=0,
        ),
    )(*[in_vmem(p) for p in pieces], in_hbm(w_gate), in_hbm(w_up), *[in_vmem(t) for t in totals])


def down_body(half, hidden_ref, weight_ref, keep_ref, send_ref):
    out = jnp.dot(hidden_ref[...], weight_ref[...], preferred_element_type=F32).astype(BF16)
    keep_ref[...] = out[:half]
    send_ref[...] = out[half:]


def down_call(j, hidden, w_down):
    rows, depth = hidden.shape
    width = w_down.shape[1]
    step = width // OUT_CHUNKS
    block = min(512, step)
    steps = step // block
    half = rows // 2
    return pl.pallas_call(
        functools.partial(down_body, half),
        grid=(steps,),
        out_shape=[pltpu.VMEM((half, step), BF16)] * 2,
        in_specs=[VMEM_FULL, pl.BlockSpec((depth, block), lambda n: (0, j * steps + n))],
        out_specs=[pl.BlockSpec((half, block), lambda n: (0, n))] * 2,
        compiler_params=pltpu.CompilerParams(vmem_limit_bytes=16 * MIB),
        cost_estimate=pl.CostEstimate(
            flops=2 * rows * depth * step, bytes_accessed=2 * depth * step, transcendentals=0
        ),
    )(in_vmem(hidden), in_hbm(w_down))


def pair_body(keep_ref, got_ref, *outs):
    rows = outs[0].shape[0]
    for k, out in enumerate(outs):
        at = slice(k * rows, (k + 1) * rows)
        out[...] = (keep_ref[at].astype(F32) + got_ref[at].astype(F32)).astype(BF16)


def pair_call(keep, got, rows):
    count = keep.shape[0] // rows
    return pl.pallas_call(
        pair_body,
        out_shape=[pltpu.VMEM((rows, keep.shape[1]), BF16)] * count,
        in_specs=[VMEM_FULL] * 2,
        out_specs=[VMEM_FULL] * count,
    )(in_vmem(keep), in_vmem(got))


def finish_body(*refs):
    ins, out_ref = refs[:-1], refs[-1]
    count = len(ins) // OUT_CHUNKS
    step = ins[0].shape[1]
    for j in range(OUT_CHUNKS):
        total = ins[j * count][...].astype(F32)
        for ref in ins[j * count + 1 : (j + 1) * count]:
            total = total + ref[...].astype(F32)
        out_ref[:, j * step : (j + 1) * step] = total.astype(BF16)


def finish_call(parts, rows, width):
    return pl.pallas_call(
        finish_body,
        out_shape=jax.ShapeDtypeStruct((rows, width), BF16),
        in_specs=[VMEM_FULL] * len(parts),
        out_specs=VMEM_FULL,
    )(*[in_vmem(p) for p in parts])


def per_device(tokens, norm_gain, expert_ids, gate_prob, w_gate, w_up, w_down):
    rows, width = tokens.shape
    local, _, hidden = w_gate.shape
    size = lax.axis_size("exp") * lax.axis_size("ten")
    expert_count = local * lax.axis_size("exp")
    far = range(2, size, 2)

    own = norm_call(tokens, norm_gain, expert_ids, gate_prob, expert_count)
    gathered = []
    for j in range(IN_CHUNKS):
        mine = own[j]
        if j >= 2:
            mine = after(mine, gathered[j - 2][-1])
        near = [mine] + [exchange(mine, size, mask) for mask in far]
        gathered.append(near + [exchange(jnp.concatenate(near, axis=0), size, 1)])
    total = None
    for j in range(IN_CHUNKS):
        total = gate_up_call(j, gathered[j], w_gate, w_up, total, expert_count)

    w_rows = w_down.reshape(local * hidden, width)
    parts = []
    for j in range(OUT_CHUNKS):
        keep, send = down_call(j, total, w_rows)
        blocks = pair_call(keep, exchange(send, size, 1), rows)
        parts += [blocks[0]] + [exchange(b, size, mask) for b, mask in zip(blocks[1:], far)]
    return finish_call(parts, rows, width)


def solution(mesh):
    placed = (
        P(("grp", "exp", "ten"), None),
        P(),
        P(("grp", "exp", "ten"), None),
        P(("grp", "exp", "ten"), None),
        P("exp", None, "ten"),
        P("exp", None, "ten"),
        P("exp", "ten", None),
    )
    return jax.shard_map(
        per_device,
        mesh=mesh,
        in_specs=placed,
        out_specs=P(("grp", "exp", "ten"), None),
        check_vma=False,
    )
```

time: 129 us -> 97.4 us (0.76)
  Pallas kernels: 0 us -> 53.6 us
  waiting for transfers between devices: 59.2 us -> 7.6 us
  matrix products: 40.6 us -> 0 us
  starting transfers between devices: 0.04 us -> 32.6 us
  between operations: 13.4 us -> 0.23 us
  blocking collectives: 10.7 us -> 0 us
  other arithmetic: 5.01 us -> 0.08 us
  local copies, waits for them, and re-layouts: 0.12 us -> 2.72 us
    pallas_call x0 -> x14, Pallas kernels: none -> 53.6 us  [the longest x4 35.7 us: gate_up_call(): pl.pallas_call(functools.partial(gate_up_body, first, last, step, hidden,...]
    reduce_scatter x1 -> x0, waiting for transfers between devices: 41.4 us -> none  [per_device(): lax.psum_scatter(part.astype(jnp.bfloat16), ('exp', 'ten'), scatter_dimen...]
    dot_general x3 -> x0, matrix products: 40.6 us -> none  [the longest x1 15.4 us: per_device(): jnp.einsum('td,edf->etf', rows, w_up, preferred_element_type=jnp.float32)]
    ppermute x0 -> x32, starting transfers between devices: none -> 32.6 us  [exchange(): return lax.ppermute(value, GROUP, [(i, i ^ mask) for i in range(size)])]
    all_gather x1 -> x0, waiting for transfers between devices: 17.8 us -> none  [per_device(): rows = lax.all_gather(normed, ('exp', 'ten'), axis=0, tiled=True)]
    all_gather x1 -> x0, blocking collectives: 10.7 us -> none  [per_device(): weight = lax.all_gather(weight, ('exp', 'ten'), axis=0, tiled=True)]
    ppermute x0 -> x32, waiting for transfers between devices: none -> 7.6 us  [exchange(): return lax.ppermute(value, GROUP, [(i, i ^ mask) for i in range(size)])]
    unnamed x3 -> x2, local copies, waits for them, and re-layouts: 0.09 us -> 2.72 us
  transfers between devices with their start and end apart: 2 -> 32, of which waited for: 2 -> 6; matrix products, arithmetic and copies ran while one was open for 2% -> 0% of each run, Pallas kernels for 0% -> 32%
where the time goes in v2:
time: 97.4 us; the launch traced here: 96.8 us
  Pallas kernels  53.6 us (55%)
  starting transfers between devices  32.6 us (33%)
  waiting for transfers between devices  7.6 us (8%)
  local copies, waits for them, and re-layouts  2.72 us (3%)
    pallas_call x4, Pallas kernels, gate_up_call(): pl.pallas_call(functools.partial(gate_up_body, first, last, step, hidden,...  35.7 us
    ppermute x32, starting transfers between devices, exchange(): return lax.ppermute(value, GROUP, [(i, i ^ mask) for i in range(size)])  32.6 us
    pallas_call x4, Pallas kernels, down_call(): pl.pallas_call(functools.partial(down_body, half), grid=(steps,), out_sha...  15.6 us
    ppermute x32, waiting for transfers between devices, exchange(): return lax.ppermute(value, GROUP, [(i, i ^ mask) for i in range(size)])  7.6 us
    unnamed x2, local copies, waits for them, and re-layouts  2.72 us
  transfers between devices with their start and end apart: 32, of which 6 were waited for; matrix products, arithmetic and copies ran while one was open for 0% of the time, Pallas kernels for 32%

profile of v2, /device:TPU:0, one launch (start us, length us, event | category | flops | bytes accessed | tf_op | source)
XLA Modules:
  0.0 96.8 jit_solution(18205443692381902913)
XLA Ops:
  3.9 4.0 %collective-permute-start.10 = (bf16[32,1024]{1,0:T(8,128)(2,1)S(1)}, bf16[32,1024]{1,0:T(8,128)(2,1)S(1)}, u32[]{:S(2)}, u32[]{:S(2)}) collective-permute-start(bf16[32,1024]{1,0:T(8,128)(2,1)S(1)} %get-tuple-element.39.refs_0_), channel_id=1, source_target_pairs={{0,6},{1,7},{2,4},{3,5},{4,2},{5,3},{6,0},{7,1},{8,14},{9,15},{10,... | collective-permute-start | bytes 196616 | tf_op jit(solution)/shard_map/ppermute | solution.py:29
  8.5 1.9 %collective-permute-start = (bf16[32,1024]{1,0:T(8,128)(2,1)S(1)}, bf16[32,1024]{1,0:T(8,128)(2,1)S(1)}, u32[]{:S(2)}, u32[]{:S(2)}) collective-permute-start(bf16[32,1024]{1,0:T(8,128)(2,1)S(1)} %get-tuple-element.36.refs_0_), channel_id=1, source_target_pairs={{0,2},{1,3},{2,0},{3,1},{4,6},{5,7},{6,4},{7,5},{8,10},{9,11},{10,... | collective-permute-start | bytes 196616 | tf_op jit(solution)/shard_map/ppermute | solution.py:29
  10.5 1.5 %collective-permute-start.1 = (bf16[32,1024]{1,0:T(8,128)(2,1)S(1)}, bf16[32,1024]{1,0:T(8,128)(2,1)S(1)}, u32[]{:S(2)}, u32[]{:S(2)}) collective-permute-start(bf16[32,1024]{1,0:T(8,128)(2,1)S(1)} %get-tuple-element.36.refs_0_), channel_id=1, source_target_pairs={{0,4},{1,5},{2,6},{3,7},{4,0},{5,1},{6,2},{7,3},{8,12},{9,13},{10,... | collective-permute-start | bytes 196616 | tf_op jit(solution)/shard_map/ppermute | solution.py:29
  12.0 1.4 %collective-permute-start.2 = (bf16[32,1024]{1,0:T(8,128)(2,1)S(1)}, bf16[32,1024]{1,0:T(8,128)(2,1)S(1)}, u32[]{:S(2)}, u32[]{:S(2)}) collective-permute-start(bf16[32,1024]{1,0:T(8,128)(2,1)S(1)} %get-tuple-element.36.refs_0_), channel_id=1, source_target_pairs={{0,6},{1,7},{2,4},{3,5},{4,2},{5,3},{6,0},{7,1},{8,14},{9,15},{10,... | collective-permute-start | bytes 196616 | tf_op jit(solution)/shard_map/ppermute | solution.py:29
  14.7 2.4 %collective-permute-done.2.refs_3_ = bf16[32,1024]{1,0:T(8,128)(2,1)S(1)} collective-permute-done((bf16[32,1024]{1,0:T(8,128)(2,1)S(1)}, bf16[32,1024]{1,0:T(8,128)(2,1)S(1)}, u32[]{:S(2)}, u32[]{:S(2)}) %collective-permute-start.2) | collective-permute-done | bytes 65568 | tf_op jit(solution)/shard_map/ppermute | solution.py:29
  19.3 1.5 %collective-permute-start.14 = (bf16[32,1024]{1,0:T(8,128)(2,1)S(1)}, bf16[32,1024]{1,0:T(8,128)(2,1)S(1)}, u32[]{:S(2)}, u32[]{:S(2)}) collective-permute-start(bf16[32,1024]{1,0:T(8,128)(2,1)S(1)} %get-tuple-element.40.refs_0_), channel_id=1, source_target_pairs={{0,6},{1,7},{2,4},{3,5},{4,2},{5,3},{6,0},{7,1},{8,14},{9,15},{10,... | collective-permute-start | bytes 196616 | tf_op jit(solution)/shard_map/ppermute | solution.py:29
  21.4 1.4 %collective-permute-start.5 = (bf16[32,1152]{1,0:T(8,128)(2,1)S(1)}, bf16[32,1152]{1,0:T(8,128)(2,1)S(1)}, u32[]{:S(2)}, u32[]{:S(2)}) collective-permute-start(bf16[32,1152]{1,0:T(8,128)(2,1)S(1)} %get-tuple-element.37.refs_0_), channel_id=1, source_target_pairs={{0,4},{1,5},{2,6},{3,7},{4,0},{5,1},{6,2},{7,3},{8,12},{9,13},{10,... | collective-permute-start | bytes 221192 | tf_op jit(solution)/shard_map/ppermute | solution.py:29
  22.8 8.8 %shard_map.74.refs_7_ = f32[8,256,768]{2,1,0:T(8,128)S(1)} custom-call(bf16[32,1024]{1,0:T(8,128)(2,1)S(1)} %get-tuple-element.39.refs_0_, bf16[32,1024]{1,0:T(8,128)(2,1)S(1)} %collective-permute-done.8.refs_1_, bf16[32,1024]{1,0:T(8,128)(2,1)S(1)} %collective-permute-done.9.refs_2_, bf16[32,1024]{1,0:T(8,128)(2,1)S(1)} %collective-permute-done.10.refs_3_, ...), custom_call_target="tpu_custom_call" | custom-call | flops 3221225472 | bytes 12582912 | tf_op jit(solution)/shard_map/pallas_call | solution.py:116
  31.6 1.6 %collective-permute-start.6 = (bf16[32,1152]{1,0:T(8,128)(2,1)S(1)}, bf16[32,1152]{1,0:T(8,128)(2,1)S(1)}, u32[]{:S(2)}, u32[]{:S(2)}) collective-permute-start(bf16[32,1152]{1,0:T(8,128)(2,1)S(1)} %get-tuple-element.37.refs_0_), channel_id=1, source_target_pairs={{0,6},{1,7},{2,4},{3,5},{4,2},{5,3},{6,0},{7,1},{8,14},{9,15},{10,... | collective-permute-start | bytes 221192 | tf_op jit(solution)/shard_map/ppermute | solution.py:29
  33.3 8.8 %shard_map.75.refs_7_ = f32[8,256,768]{2,1,0:T(8,128)S(1)} custom-call(bf16[32,1024]{1,0:T(8,128)(2,1)S(1)} %get-tuple-element.36.refs_0_, bf16[32,1024]{1,0:T(8,128)(2,1)S(1)} %collective-permute-done.refs_1_, bf16[32,1024]{1,0:T(8,128)(2,1)S(1)} %collective-permute-done.1.refs_2_, ...), custom_call_target="tpu_custom_call", output_to_operand_aliasing={{}: (7, {})} | custom-call | flops 3221225472 | bytes 12582912 | tf_op jit(solution)/shard_map/pallas_call | solution.py:116
  42.7 8.8 %shard_map.76.refs_7_ = f32[8,256,768]{2,1,0:T(8,128)S(1)} custom-call(bf16[32,1024]{1,0:T(8,128)(2,1)S(1)} %get-tuple-element.40.refs_0_, bf16[32,1024]{1,0:T(8,128)(2,1)S(1)} %collective-permute-done.12.refs_1_, bf16[32,1024]{1,0:T(8,128)(2,1)S(1)} %collective-permute-done.13.refs_2_, ...), custom_call_target="tpu_custom_call", output_to_operand_aliasing={{}: (7, {})} | custom-call | flops 3221225472 | bytes 12582912 | tf_op jit(solution)/shard_map/pallas_call | solution.py:116
  51.5 9.2 %shard_map.77.hidden_ref = bf16[256,3072]{1,0:T(8,128)(2,1)S(1)} custom-call(bf16[32,1152]{1,0:T(8,128)(2,1)S(1)} %get-tuple-element.37.refs_0_, bf16[32,1152]{1,0:T(8,128)(2,1)S(1)} %collective-permute-done.4.refs_1_, bf16[32,1152]{1,0:T(8,128)(2,1)S(1)} %collective-permute-done.5.refs_2_, bf16[32,1152]{1,0:T(8,128)(2,1)S(1)} %collective-permute-done.6.refs_3_, ...), custom_call_target="tpu_custom_call" | custom-call | flops 3221225472 | bytes 12582912 | tf_op jit(solution)/shard_map/pallas_call | solution.py:116
  60.8 3.9 %shard_map.84 = (bf16[128,1024]{1,0:T(8,128)(2,1)S(1)}, bf16[128,1024]{1,0:T(8,128)(2,1)S(1)}) custom-call(bf16[256,3072]{1,0:T(8,128)(2,1)S(1)} %shard_map.77.hidden_ref, bf16[3072,4096]{1,0:T(8,128)(2,1)} %bitcast.2), custom_call_target="tpu_custom_call" | custom-call | flops 1610612736 | bytes 6291456 | tf_op jit(solution)/shard_map/pallas_call | solution.py:146
  64.7 3.9 %shard_map.82 = (bf16[128,1024]{1,0:T(8,128)(2,1)S(1)}, bf16[128,1024]{1,0:T(8,128)(2,1)S(1)}) custom-call(bf16[256,3072]{1,0:T(8,128)(2,1)S(1)} %shard_map.77.hidden_ref, bf16[3072,4096]{1,0:T(8,128)(2,1)} %bitcast.3), custom_call_target="tpu_custom_call" | custom-call | flops 1610612736 | bytes 6291456 | tf_op jit(solution)/shard_map/pallas_call | solution.py:146
  68.6 3.9 %shard_map.80 = (bf16[128,1024]{1,0:T(8,128)(2,1)S(1)}, bf16[128,1024]{1,0:T(8,128)(2,1)S(1)}) custom-call(bf16[256,3072]{1,0:T(8,128)(2,1)S(1)} %shard_map.77.hidden_ref, bf16[3072,4096]{1,0:T(8,128)(2,1)} %bitcast.4), custom_call_target="tpu_custom_call" | custom-call | flops 1610612736 | bytes 6291456 | tf_op jit(solution)/shard_map/pallas_call | solution.py:146
  73.2 3.9 %shard_map.78 = (bf16[128,1024]{1,0:T(8,128)(2,1)S(1)}, bf16[128,1024]{1,0:T(8,128)(2,1)S(1)}) custom-call(bf16[256,3072]{1,0:T(8,128)(2,1)S(1)} %shard_map.77.hidden_ref, bf16[3072,4096]{1,0:T(8,128)(2,1)} %bitcast.5), custom_call_target="tpu_custom_call" | custom-call | flops 1610612736 | bytes 6291456 | tf_op jit(solution)/shard_map/pallas_call | solution.py:146
  79.7 1.5 %collective-permute-start.31 = (bf16[32,1024]{1,0:T(8,128)(2,1)S(1)}, bf16[32,1024]{1,0:T(8,128)(2,1)S(1)}, u32[]{:S(2)}, u32[]{:S(2)}) collective-permute-start(bf16[32,1024]{1,0:T(8,128)(2,1)S(1)} %get-tuple-element.64), channel_id=1, source_target_pairs={{0,6},{1,7},{2,4},{3,5},{4,2},{5,3},{6,0},{7,1},{8,14},{9,15},{10,... | collective-permute-start | bytes 196616 | tf_op jit(solution)/shard_map/ppermute | solution.py:29
  82.0 1.5 %collective-permute-start.26 = (bf16[32,1024]{1,0:T(8,128)(2,1)S(1)}, bf16[32,1024]{1,0:T(8,128)(2,1)S(1)}, u32[]{:S(2)}, u32[]{:S(2)}) collective-permute-start(bf16[32,1024]{1,0:T(8,128)(2,1)S(1)} %get-tuple-element.57), channel_id=1, source_target_pairs={{0,4},{1,5},{2,6},{3,7},{4,0},{5,1},{6,2},{7,3},{8,12},{9,13},{10,... | collective-permute-start | bytes 196616 | tf_op jit(solution)/shard_map/ppermute | solution.py:29
  83.5 1.5 %collective-permute-start.27 = (bf16[32,1024]{1,0:T(8,128)(2,1)S(1)}, bf16[32,1024]{1,0:T(8,128)(2,1)S(1)}, u32[]{:S(2)}, u32[]{:S(2)}) collective-permute-start(bf16[32,1024]{1,0:T(8,128)(2,1)S(1)} %get-tuple-element.58), channel_id=1, source_target_pairs={{0,6},{1,7},{2,4},{3,5},{4,2},{5,3},{6,0},{7,1},{8,14},{9,15},{10,... | collective-permute-start | bytes 196616 | tf_op jit(solution)/shard_map/ppermute | solution.py:29
  85.7 1.5 %collective-permute-start.22 = (bf16[32,1024]{1,0:T(8,128)(2,1)S(1)}, bf16[32,1024]{1,0:T(8,128)(2,1)S(1)}, u32[]{:S(2)}, u32[]{:S(2)}) collective-permute-start(bf16[32,1024]{1,0:T(8,128)(2,1)S(1)} %get-tuple-element.51), channel_id=1, source_target_pairs={{0,4},{1,5},{2,6},{3,7},{4,0},{5,1},{6,2},{7,3},{8,12},{9,13},{10,... | collective-permute-start | bytes 196616 | tf_op jit(solution)/shard_map/ppermute | solution.py:29
  87.1 1.5 %collective-permute-start.23 = (bf16[32,1024]{1,0:T(8,128)(2,1)S(1)}, bf16[32,1024]{1,0:T(8,128)(2,1)S(1)}, u32[]{:S(2)}, u32[]{:S(2)}) collective-permute-start(bf16[32,1024]{1,0:T(8,128)(2,1)S(1)} %get-tuple-element.52), channel_id=1, source_target_pairs={{0,6},{1,7},{2,4},{3,5},{4,2},{5,3},{6,0},{7,1},{8,14},{9,15},{10,... | collective-permute-start | bytes 196616 | tf_op jit(solution)/shard_map/ppermute | solution.py:29
  89.2 1.4 %collective-permute-start.18 = (bf16[32,1024]{1,0:T(8,128)(2,1)S(1)}, bf16[32,1024]{1,0:T(8,128)(2,1)S(1)}, u32[]{:S(2)}, u32[]{:S(2)}) collective-permute-start(bf16[32,1024]{1,0:T(8,128)(2,1)S(1)} %get-tuple-element.45), channel_id=1, source_target_pairs={{0,4},{1,5},{2,6},{3,7},{4,0},{5,1},{6,2},{7,3},{8,12},{9,13},{10,... | collective-permute-start | bytes 196616 | tf_op jit(solution)/shard_map/ppermute | solution.py:29
  90.8 1.4 %collective-permute-start.19 = (bf16[32,1024]{1,0:T(8,128)(2,1)S(1)}, bf16[32,1024]{1,0:T(8,128)(2,1)S(1)}, u32[]{:S(2)}, u32[]{:S(2)}) collective-permute-start(bf16[32,1024]{1,0:T(8,128)(2,1)S(1)} %get-tuple-element.46), channel_id=1, source_target_pairs={{0,6},{1,7},{2,4},{3,5},{4,2},{5,3},{6,0},{7,1},{8,14},{9,15},{10,... | collective-permute-start | bytes 196616 | tf_op jit(solution)/shard_map/ppermute | solution.py:29
  93.5 2.5 %collective-permute-done.19.refs_3_ = bf16[32,1024]{1,0:T(8,128)(2,1)S(1)} collective-permute-done((bf16[32,1024]{1,0:T(8,128)(2,1)S(1)}, bf16[32,1024]{1,0:T(8,128)(2,1)S(1)}, u32[]{:S(2)}, u32[]{:S(2)}) %collective-permute-start.19) | collective-permute-done | bytes 65568 | tf_op jit(solution)/shard_map/ppermute | solution.py:29
  (60 shorter events, 16.8 us)
Async XLA Ops:
  3.9 8.0 %collective-permute-start.10 = (bf16[32,1024]{1,0:T(8,128)(2,1)S(1)}, bf16[32,1024]{1,0:T(8,128)(2,1)S(1)}, u32[]{:S(2)}, u32[]{:S(2)}) collective-permute-start(bf16[32,1024]{1,0:T(8,128)(2,1)S(1)} %get-tuple-element.39.refs_0_), channel_id=1, source_target_pairs={{0,6},{1,7},{2,4},{3,5},{4,2},{5,3},{6,0},{7,1},{8,14},{9,15},{10,... | collective-permute-start | bytes 196616 | tf_op jit(solution)/shard_map/ppermute | solution.py:29
  7.9 5.5 %collective-permute-start.8 = (bf16[32,1024]{1,0:T(8,128)(2,1)S(1)}, bf16[32,1024]{1,0:T(8,128)(2,1)S(1)}, u32[]{:S(2)}, u32[]{:S(2)}) collective-permute-start(bf16[32,1024]{1,0:T(8,128)(2,1)S(1)} %get-tuple-element.39.refs_0_), channel_id=1, source_target_pairs={{0,2},{1,3},{2,0},{3,1},{4,6},{5,7},{6,4},{7,5},{8,10},{9,11},{10,... | collective-permute-start | bytes 196616 | tf_op jit(solution)/shard_map/ppermute | solution.py:29
  12.0 5.2 %collective-permute-start.2 = (bf16[32,1024]{1,0:T(8,128)(2,1)S(1)}, bf16[32,1024]{1,0:T(8,128)(2,1)S(1)}, u32[]{:S(2)}, u32[]{:S(2)}) collective-permute-start(bf16[32,1024]{1,0:T(8,128)(2,1)S(1)} %get-tuple-element.36.refs_0_), channel_id=1, source_target_pairs={{0,6},{1,7},{2,4},{3,5},{4,2},{5,3},{6,0},{7,1},{8,14},{9,15},{10,... | collective-permute-start | bytes 196616 | tf_op jit(solution)/shard_map/ppermute | solution.py:29
  17.2 14.3 %collective-permute-start.12 = (bf16[32,1024]{1,0:T(8,128)(2,1)S(1)}, bf16[32,1024]{1,0:T(8,128)(2,1)S(1)}, u32[]{:S(2)}, u32[]{:S(2)}) collective-permute-start(bf16[32,1024]{1,0:T(8,128)(2,1)S(1)} %get-tuple-element.40.refs_0_), channel_id=1, source_target_pairs={{0,2},{1,3},{2,0},{3,1},{4,6},{5,7},{6,4},{7,5},{8,10},{9,11},{10,... | collective-permute-start | bytes 196616 | tf_op jit(solution)/shard_map/ppermute | solution.py:29
  17.9 15.3 %collective-permute-start.13 = (bf16[32,1024]{1,0:T(8,128)(2,1)S(1)}, bf16[32,1024]{1,0:T(8,128)(2,1)S(1)}, u32[]{:S(2)}, u32[]{:S(2)}) collective-permute-start(bf16[32,1024]{1,0:T(8,128)(2,1)S(1)} %get-tuple-element.40.refs_0_), channel_id=1, source_target_pairs={{0,4},{1,5},{2,6},{3,7},{4,0},{5,1},{6,2},{7,3},{8,12},{9,13},{10,... | collective-permute-start | bytes 196616 | tf_op jit(solution)/shard_map/ppermute | solution.py:29
  19.3 13.9 %collective-permute-start.14 = (bf16[32,1024]{1,0:T(8,128)(2,1)S(1)}, bf16[32,1024]{1,0:T(8,128)(2,1)S(1)}, u32[]{:S(2)}, u32[]{:S(2)}) collective-permute-start(bf16[32,1024]{1,0:T(8,128)(2,1)S(1)} %get-tuple-element.40.refs_0_), channel_id=1, source_target_pairs={{0,6},{1,7},{2,4},{3,5},{4,2},{5,3},{6,0},{7,1},{8,14},{9,15},{10,... | collective-permute-start | bytes 196616 | tf_op jit(solution)/shard_map/ppermute | solution.py:29
  20.8 21.3 %collective-permute-start.4 = (bf16[32,1152]{1,0:T(8,128)(2,1)S(1)}, bf16[32,1152]{1,0:T(8,128)(2,1)S(1)}, u32[]{:S(2)}, u32[]{:S(2)}) collective-permute-start(bf16[32,1152]{1,0:T(8,128)(2,1)S(1)} %get-tuple-element.37.refs_0_), channel_id=1, source_target_pairs={{0,2},{1,3},{2,0},{3,1},{4,6},{5,7},{6,4},{7,5},{8,10},{9,11},{10,... | collective-permute-start | bytes 221192 | tf_op jit(solution)/shard_map/ppermute | solution.py:29
  21.4 20.7 %collective-permute-start.5 = (bf16[32,1152]{1,0:T(8,128)(2,1)S(1)}, bf16[32,1152]{1,0:T(8,128)(2,1)S(1)}, u32[]{:S(2)}, u32[]{:S(2)}) collective-permute-start(bf16[32,1152]{1,0:T(8,128)(2,1)S(1)} %get-tuple-element.37.refs_0_), channel_id=1, source_target_pairs={{0,4},{1,5},{2,6},{3,7},{4,0},{5,1},{6,2},{7,3},{8,12},{9,13},{10,... | collective-permute-start | bytes 221192 | tf_op jit(solution)/shard_map/ppermute | solution.py:29
  31.6 10.5 %collective-permute-start.6 = (bf16[32,1152]{1,0:T(8,128)(2,1)S(1)}, bf16[32,1152]{1,0:T(8,128)(2,1)S(1)}, u32[]{:S(2)}, u32[]{:S(2)}) collective-permute-start(bf16[32,1152]{1,0:T(8,128)(2,1)S(1)} %get-tuple-element.37.refs_0_), channel_id=1, source_target_pairs={{0,6},{1,7},{2,4},{3,5},{4,2},{5,3},{6,0},{7,1},{8,14},{9,15},{10,... | collective-permute-start | bytes 221192 | tf_op jit(solution)/shard_map/ppermute | solution.py:29
  33.2 9.5 %collective-permute-start.15 = (bf16[128,1024]{1,0:T(8,128)(2,1)S(1)}, bf16[128,1024]{1,0:T(8,128)(2,1)S(1)}, u32[]{:S(2)}, u32[]{:S(2)}) collective-permute-start(bf16[128,1024]{1,0:T(8,128)(2,1)S(1)} %pad_maximum_fusion.3), channel_id=1, source_target_pairs={{0,1},{1,0},{2,3},{3,2},{4,5},{5,4},{6,7},{7,6},{8,9},{9,8},{10,11... | collective-permute-start | bytes 786440 | tf_op jit(solution)/shard_map/ppermute | solution.py:29
  42.2 9.4 %collective-permute-start.7 = (bf16[128,1152]{1,0:T(8,128)(2,1)S(1)}, bf16[128,1152]{1,0:T(8,128)(2,1)S(1)}, u32[]{:S(2)}, u32[]{:S(2)}) collective-permute-start(bf16[128,1152]{1,0:T(8,128)(2,1)S(1)} %pad_maximum_fusion), channel_id=1, source_target_pairs={{0,1},{1,0},{2,3},{3,2},{4,5},{5,4},{6,7},{7,6},{8,9},{9,8},{10,11... | collective-permute-start | bytes 884744 | tf_op jit(solution)/shard_map/ppermute | solution.py:29
  72.5 5.1 %collective-permute-start.28 = (bf16[128,1024]{1,0:T(8,128)(2,1)S(1)}, bf16[128,1024]{1,0:T(8,128)(2,1)S(1)}, u32[]{:S(2)}, u32[]{:S(2)}) collective-permute-start(bf16[128,1024]{1,0:T(8,128)(2,1)S(1)} %get-tuple-element.60), channel_id=1, source_target_pairs={{0,1},{1,0},{2,3},{3,2},{4,5},{5,4},{6,7},{7,6},{8,9},{9,8},{10,11... | collective-permute-start | bytes 786440 | tf_op jit(solution)/shard_map/ppermute | solution.py:29
  72.7 7.1 %collective-permute-start.24 = (bf16[128,1024]{1,0:T(8,128)(2,1)S(1)}, bf16[128,1024]{1,0:T(8,128)(2,1)S(1)}, u32[]{:S(2)}, u32[]{:S(2)}) collective-permute-start(bf16[128,1024]{1,0:T(8,128)(2,1)S(1)} %get-tuple-element.54), channel_id=1, source_target_pairs={{0,1},{1,0},{2,3},{3,2},{4,5},{5,4},{6,7},{7,6},{8,9},{9,8},{10,11... | collective-permute-start | bytes 786440 | tf_op jit(solution)/shard_map/ppermute | solution.py:29
  73.1 8.2 %collective-permute-start.20 = (bf16[128,1024]{1,0:T(8,128)(2,1)S(1)}, bf16[128,1024]{1,0:T(8,128)(2,1)S(1)}, u32[]{:S(2)}, u32[]{:S(2)}) collective-permute-start(bf16[128,1024]{1,0:T(8,128)(2,1)S(1)} %get-tuple-element.48), channel_id=1, source_target_pairs={{0,1},{1,0},{2,3},{3,2},{4,5},{5,4},{6,7},{7,6},{8,9},{9,8},{10,11... | collective-permute-start | bytes 786440 | tf_op jit(solution)/shard_map/ppermute | solution.py:29
  77.7 5.8 %collective-permute-start.29 = (bf16[32,1024]{1,0:T(8,128)(2,1)S(1)}, bf16[32,1024]{1,0:T(8,128)(2,1)S(1)}, u32[]{:S(2)}, u32[]{:S(2)}) collective-permute-start(bf16[32,1024]{1,0:T(8,128)(2,1)S(1)} %get-tuple-element.62), channel_id=1, source_target_pairs={{0,2},{1,3},{2,0},{3,1},{4,6},{5,7},{6,4},{7,5},{8,10},{9,11},{10,... | collective-permute-start | bytes 196616 | tf_op jit(solution)/shard_map/ppermute | solution.py:29
  78.3 6.7 %collective-permute-start.30 = (bf16[32,1024]{1,0:T(8,128)(2,1)S(1)}, bf16[32,1024]{1,0:T(8,128)(2,1)S(1)}, u32[]{:S(2)}, u32[]{:S(2)}) collective-permute-start(bf16[32,1024]{1,0:T(8,128)(2,1)S(1)} %get-tuple-element.63), channel_id=1, source_target_pairs={{0,4},{1,5},{2,6},{3,7},{4,0},{5,1},{6,2},{7,3},{8,12},{9,13},{10,... | collective-permute-start | bytes 196616 | tf_op jit(solution)/shard_map/ppermute | solution.py:29
  79.7 5.9 %collective-permute-start.31 = (bf16[32,1024]{1,0:T(8,128)(2,1)S(1)}, bf16[32,1024]{1,0:T(8,128)(2,1)S(1)}, u32[]{:S(2)}, u32[]{:S(2)}) collective-permute-start(bf16[32,1024]{1,0:T(8,128)(2,1)S(1)} %get-tuple-element.64), channel_id=1, source_target_pairs={{0,6},{1,7},{2,4},{3,5},{4,2},{5,3},{6,0},{7,1},{8,14},{9,15},{10,... | collective-permute-start | bytes 196616 | tf_op jit(solution)/shard_map/ppermute | solution.py:29
  81.3 5.8 %collective-permute-start.25 = (bf16[32,1024]{1,0:T(8,128)(2,1)S(1)}, bf16[32,1024]{1,0:T(8,128)(2,1)S(1)}, u32[]{:S(2)}, u32[]{:S(2)}) collective-permute-start(bf16[32,1024]{1,0:T(8,128)(2,1)S(1)} %get-tuple-element.56), channel_id=1, source_target_pairs={{0,2},{1,3},{2,0},{3,1},{4,6},{5,7},{6,4},{7,5},{8,10},{9,11},{10,... | collective-permute-start | bytes 196616 | tf_op jit(solution)/shard_map/ppermute | solution.py:29
  82.0 6.6 %collective-permute-start.26 = (bf16[32,1024]{1,0:T(8,128)(2,1)S(1)}, bf16[32,1024]{1,0:T(8,128)(2,1)S(1)}, u32[]{:S(2)}, u32[]{:S(2)}) collective-permute-start(bf16[32,1024]{1,0:T(8,128)(2,1)S(1)} %get-tuple-element.57), channel_id=1, source_target_pairs={{0,4},{1,5},{2,6},{3,7},{4,0},{5,1},{6,2},{7,3},{8,12},{9,13},{10,... | collective-permute-start | bytes 196616 | tf_op jit(solution)/shard_map/ppermute | solution.py:29
  83.5 5.7 %collective-permute-start.27 = (bf16[32,1024]{1,0:T(8,128)(2,1)S(1)}, bf16[32,1024]{1,0:T(8,128)(2,1)S(1)}, u32[]{:S(2)}, u32[]{:S(2)}) collective-permute-start(bf16[32,1024]{1,0:T(8,128)(2,1)S(1)} %get-tuple-element.58), channel_id=1, source_target_pairs={{0,6},{1,7},{2,4},{3,5},{4,2},{5,3},{6,0},{7,1},{8,14},{9,15},{10,... | collective-permute-start | bytes 196616 | tf_op jit(solution)/shard_map/ppermute | solution.py:29
  85.0 5.8 %collective-permute-start.21 = (bf16[32,1024]{1,0:T(8,128)(2,1)S(1)}, bf16[32,1024]{1,0:T(8,128)(2,1)S(1)}, u32[]{:S(2)}, u32[]{:S(2)}) collective-permute-start(bf16[32,1024]{1,0:T(8,128)(2,1)S(1)} %get-tuple-element.50), channel_id=1, source_target_pairs={{0,2},{1,3},{2,0},{3,1},{4,6},{5,7},{6,4},{7,5},{8,10},{9,11},{10,... | collective-permute-start | bytes 196616 | tf_op jit(solution)/shard_map/ppermute | solution.py:29
  85.7 6.6 %collective-permute-start.22 = (bf16[32,1024]{1,0:T(8,128)(2,1)S(1)}, bf16[32,1024]{1,0:T(8,128)(2,1)S(1)}, u32[]{:S(2)}, u32[]{:S(2)}) collective-permute-start(bf16[32,1024]{1,0:T(8,128)(2,1)S(1)} %get-tuple-element.51), channel_id=1, source_target_pairs={{0,4},{1,5},{2,6},{3,7},{4,0},{5,1},{6,2},{7,3},{8,12},{9,13},{10,... | collective-permute-start | bytes 196616 | tf_op jit(solution)/shard_map/ppermute | solution.py:29
  87.1 5.7 %collective-permute-start.23 = (bf16[32,1024]{1,0:T(8,128)(2,1)S(1)}, bf16[32,1024]{1,0:T(8,128)(2,1)S(1)}, u32[]{:S(2)}, u32[]{:S(2)}) collective-permute-start(bf16[32,1024]{1,0:T(8,128)(2,1)S(1)} %get-tuple-element.52), channel_id=1, source_target_pairs={{0,6},{1,7},{2,4},{3,5},{4,2},{5,3},{6,0},{7,1},{8,14},{9,15},{10,... | collective-permute-start | bytes 196616 | tf_op jit(solution)/shard_map/ppermute | solution.py:29
  90.8 5.2 %collective-permute-start.19 = (bf16[32,1024]{1,0:T(8,128)(2,1)S(1)}, bf16[32,1024]{1,0:T(8,128)(2,1)S(1)}, u32[]{:S(2)}, u32[]{:S(2)}) collective-permute-start(bf16[32,1024]{1,0:T(8,128)(2,1)S(1)} %get-tuple-element.46), channel_id=1, source_target_pairs={{0,6},{1,7},{2,4},{3,5},{4,2},{5,3},{6,0},{7,1},{8,14},{9,15},{10,... | collective-permute-start | bytes 196616 | tf_op jit(solution)/shard_map/ppermute | solution.py:29
  (8 other events, 35.7 us)

commit v3 on v1

v3 whole, which is shorter than its diff:
```python
import functools

import jax
import jax.numpy as jnp
from jax import lax
from jax.experimental import pallas as pl
from jax.experimental.pallas import tpu as pltpu
from jax.sharding import PartitionSpec as P

BF16 = jnp.bfloat16
F32 = jnp.float32
MIB = 2**20
GROUP = ("exp", "ten")
EXTRA = 128
SLOTS = 4
OUT_CHUNKS = 2
VMEM_FULL = pl.BlockSpec(memory_space=pltpu.VMEM)
ANY_FULL = pl.BlockSpec(memory_space=pl.ANY)


def in_vmem(value):
    return pltpu.with_memory_space_constraint(value, pltpu.VMEM)


def in_hbm(value):
    return pltpu.with_memory_space_constraint(value, pltpu.HBM)


def params(rows, width):
    return pltpu.CompilerParams(vmem_limit_bytes=4 * MIB + 4 * rows * width)


def cost(flops, read):
    return pl.CostEstimate(flops=flops, bytes_accessed=read, transcendentals=0)


def exchange(value, size, mask):
    return lax.ppermute(value, GROUP, [(i, i ^ mask) for i in range(size)])


def after(value, other):
    return lax.optimization_barrier((value, other))[0]


def norm_body(expert_count, *refs):
    sources, out_ref, targets, sems = refs[:4], refs[4], refs[5:9], refs[9]
    copies = [
        pltpu.make_async_copy(source, target, sems.at[i])
        for i, (source, target) in enumerate(zip(sources, targets))
    ]
    for copy in copies:
        copy.start()
    for copy in copies:
        copy.wait()
    tok_ref, gain_ref, ids_ref, prob_ref = targets
    width = tok_ref.shape[1]
    floats = tok_ref[...].astype(F32)
    meansq = jnp.mean(floats * floats, axis=1, keepdims=True)
    out_ref[:, :width] = (floats * lax.rsqrt(meansq + 1e-06) * gain_ref[...]).astype(BF16)
    prob = prob_ref[...]
    mixing = prob / jnp.sum(prob, axis=0, keepdims=True)
    place = lax.broadcasted_iota(jnp.int32, (EXTRA, prob.shape[1]), 0)
    weight = jnp.zeros(place.shape, F32)
    for k in range(prob.shape[0]):
        weight = weight + jnp.where(
            place % expert_count == ids_ref[k : k + 1], mixing[k : k + 1], 0.0
        )
    high = weight.astype(BF16).astype(F32)
    middle = (weight - high).astype(BF16).astype(F32)
    low = weight - high - middle
    piece = place // expert_count
    packed = jnp.where(piece == 0, high, jnp.where(piece == 1, middle, jnp.where(piece == 2, low, 0.0)))
    out_ref[:, width:] = packed.T.astype(BF16)


def norm_call(tokens, norm_gain, expert_ids, gate_prob, expert_count, scoped):
    rows, width = tokens.shape
    args = (tokens, norm_gain.reshape(1, width), expert_ids.T, gate_prob.T)
    return pl.pallas_call(
        functools.partial(norm_body, expert_count),
        out_shape=pltpu.VMEM((rows, width + EXTRA), BF16),
        in_specs=[ANY_FULL] * 4,
        out_specs=VMEM_FULL,
        scratch_shapes=[pltpu.VMEM(v.shape, v.dtype) for v in args]
        + [pltpu.SemaphoreType.DMA((4,))],
        compiler_params=scoped,
    )(*[in_hbm(v) for v in args])


def fetch_body(slots, order_ref, gate_hbm, up_hbm, gate_out, up_out, done_ref, sems):
    del order_ref
    copies = []
    for e in range(slots):
        copies.append(pltpu.make_async_copy(gate_hbm.at[e], gate_out.at[e], sems.at[0, e]))
        copies.append(pltpu.make_async_copy(up_hbm.at[e], up_out.at[e], sems.at[1, e]))
    for copy in copies:
        copy.start()
    done_ref[...] = jnp.zeros_like(done_ref)
    for copy in copies:
        copy.wait()


def fetch_call(order, w_gate, w_up, scoped):
    local, width, hidden = w_gate.shape
    slots = min(SLOTS, local)
    return pl.pallas_call(
        functools.partial(fetch_body, slots),
        out_shape=[pltpu.VMEM((slots, width, hidden), BF16)] * 2 + [pltpu.VMEM((8, 128), F32)],
        in_specs=[ANY_FULL] * 3,
        out_specs=[VMEM_FULL] * 3,
        scratch_shapes=[pltpu.SemaphoreType.DMA((2, slots))],
        compiler_params=scoped,
        cost_estimate=cost(0, 8 * slots * width * hidden),
    )(order, in_hbm(w_gate), in_hbm(w_up))


def gate_up_body(expert_count, parts, *refs):
    pieces, refs = refs[:parts], refs[parts:]
    gate_hbm, up_hbm, down_hbm = refs[2:5]
    out_ref, down_ref, gate_ref, up_ref, rows_ref, sems, down_sems = refs[5:]
    slots, width, hidden = gate_ref.shape
    local = gate_hbm.shape[0]

    def copies(e):
        slot = e % slots
        return [
            pltpu.make_async_copy(gate_hbm.at[e], gate_ref.at[slot], sems.at[0, slot]),
            pltpu.make_async_copy(up_hbm.at[e], up_ref.at[slot], sems.at[1, slot]),
        ]

    def down_copy(e):
        at = slice(e * hidden, (e + 1) * hidden)
        return pltpu.make_async_copy(down_hbm.at[at], down_ref.at[at], down_sems.at[e])

    down_copy(0).start()
    down_copy(1).start()
    at = 0
    for piece in pieces:
        rows_ref[at : at + piece.shape[0]] = piece[...]
        at += piece.shape[0]

    row = lax.broadcasted_iota(jnp.int32, (EXTRA, hidden), 0)
    number = lax.axis_index("exp") * local

    def finish(e, both):
        gate, up = both[:, :hidden], both[:, hidden:]
        pick = jnp.where((row % expert_count == number + e) & (row < 3 * expert_count), 1.0, 0.0)
        mixing = jnp.dot(rows_ref[:, width:], pick.astype(BF16), preferred_element_type=F32)
        value = gate / (1.0 + jnp.exp(-gate)) * up * mixing
        out_ref[:, e * hidden : (e + 1) * hidden] = value.astype(BF16)

    for e in range(local):
        if e >= slots:
            for copy in copies(e):
                copy.wait()
        weights = jnp.concatenate([gate_ref[e % slots], up_ref[e % slots]], axis=1)
        both = jnp.dot(rows_ref[:, :width], weights, preferred_element_type=F32)
        if e + slots < local:
            for copy in copies(e + slots):
                copy.start()
        if e + 2 < local:
            down_copy(e + 2).start()
        finish(e, both)
    for e in range(local):
        down_copy(e).wait()


def gate_up_call(pieces, gate_slots, up_slots, w_gate, w_up, w_down, expert_count, scoped):
    slots, width, hidden = gate_slots.shape
    local = w_gate.shape[0]
    depth = w_down.shape[0]
    rows = sum(p.shape[0] for p in pieces)
    count = len(pieces)
    shape = pltpu.VMEM(gate_slots.shape, BF16)
    return pl.pallas_call(
        functools.partial(gate_up_body, expert_count, count),
        out_shape=[pltpu.VMEM((rows, depth), BF16), pltpu.VMEM((depth, width), BF16), shape, shape],
        in_specs=[VMEM_FULL] * (count + 2) + [ANY_FULL] * 3,
        out_specs=[VMEM_FULL] * 4,
        scratch_shapes=[
            pltpu.VMEM((rows, width + EXTRA), BF16),
            pltpu.SemaphoreType.DMA((2, slots)),
            pltpu.SemaphoreType.DMA((local,)),
        ],
        input_output_aliases={count: 2, count + 1: 3},
        compiler_params=scoped,
        cost_estimate=cost(4 * rows * width * hidden * local, 6 * width * hidden * local),
    )(
        *[in_vmem(v) for v in (*pieces, gate_slots, up_slots)],
        *[in_hbm(v) for v in (w_gate, w_up, w_down)],
    )[:2]


def down_body(half, start, hidden_ref, weight_ref, keep_ref, send_ref):
    block = 512
    for at in range(0, keep_ref.shape[1], block):
        to = slice(at, at + block)
        weights = weight_ref[:, start + at : start + at + block]
        out = jnp.dot(hidden_ref[...], weights, preferred_element_type=F32).astype(BF16)
        keep_ref[:, to] = out[:half]
        send_ref[:, to] = out[half:]


def down_call(hidden, weight, start, step, scoped):
    rows, depth = hidden.shape
    half = rows // 2
    return pl.pallas_call(
        functools.partial(down_body, half, start),
        out_shape=[pltpu.VMEM((half, step), BF16)] * 2,
        in_specs=[VMEM_FULL] * 2,
        out_specs=[VMEM_FULL] * 2,
        compiler_params=scoped,
        cost_estimate=cost(2 * rows * depth * step, 2 * depth * step),
    )(in_vmem(hidden), in_vmem(weight))


def pair_body(keep_ref, got_ref, *outs):
    rows = outs[0].shape[0]
    for k, out in enumerate(outs):
        at = slice(k * rows, (k + 1) * rows)
        out[...] = (keep_ref[at].astype(F32) + got_ref[at].astype(F32)).astype(BF16)


def pair_call(keep, got, rows, scoped):
    count = keep.shape[0] // rows
    return pl.pallas_call(
        pair_body,
        out_shape=[pltpu.VMEM((rows, keep.shape[1]), BF16)] * count,
        in_specs=[VMEM_FULL] * 2,
        out_specs=[VMEM_FULL] * count,
        compiler_params=scoped,
    )(in_vmem(keep), in_vmem(got))


def finish_body(chunks, *refs):
    ins, out_ref = refs[:-1], refs[-1]
    count = len(ins) // chunks
    step = ins[0].shape[1]
    for j in range(chunks):
        total = ins[j * count][...].astype(F32)
        for ref in ins[j * count + 1 : (j + 1) * count]:
            total = total + ref[...].astype(F32)
        out_ref[:, j * step : (j + 1) * step] = total.astype(BF16)


def finish_call(parts, chunks, rows, width, scoped):
    return pl.pallas_call(
        functools.partial(finish_body, chunks),
        out_shape=jax.ShapeDtypeStruct((rows, width), BF16),
        in_specs=[VMEM_FULL] * len(parts),
        out_specs=VMEM_FULL,
        compiler_params=scoped,
    )(*[in_vmem(p) for p in parts])


def per_device(tokens, norm_gain, expert_ids, gate_prob, w_gate, w_up, w_down):
    rows, width = tokens.shape
    local, _, hidden = w_gate.shape
    size = lax.axis_size("exp") * lax.axis_size("ten")
    expert_count = local * lax.axis_size("exp")
    far = range(2, size, 2)
    w_rows = w_down.reshape(local * hidden, width)

    scoped = params(size * rows, width)

    own = norm_call(tokens, norm_gain, expert_ids, gate_prob, expert_count, scoped)
    gate_slots, up_slots, fetched = fetch_call(own, w_gate, w_up, scoped)
    near = [own] + [after(exchange(own, size, mask), fetched) for mask in far]
    pieces = near + [exchange(piece, size, 1) for piece in near]
    mixed_hidden, weight = gate_up_call(
        pieces, gate_slots, up_slots, w_gate, w_up, w_rows, expert_count, scoped
    )
    step = width // OUT_CHUNKS
    parts = []
    for j in range(OUT_CHUNKS):
        keep, send = down_call(mixed_hidden, weight, j * step, step, scoped)
        blocks = pair_call(keep, exchange(send, size, 1), rows, scoped)
        parts += [blocks[0]] + [exchange(b, size, mask) for b, mask in zip(blocks[1:], far)]
    return finish_call(parts, OUT_CHUNKS, rows, width, scoped)


def solution(mesh):
    placed = (
        P(("grp", "exp", "ten"), None),
        P(),
        P(("grp", "exp", "ten"), None),
        P(("grp", "exp", "ten"), None),
        P("exp", None, "ten"),
        P("exp", None, "ten"),
        P("exp", "ten", None),
    )
    return jax.shard_map(
        per_device,
        mesh=mesh,
        in_specs=placed,
        out_specs=P(("grp", "exp", "ten"), None),
        check_vma=False,
    )
```

time: 129 us -> 61.5 us (0.48)
  waiting for transfers between devices: 59.2 us -> 12.1 us
  matrix products: 40.6 us -> 0 us
  Pallas kernels: 0 us -> 35.7 us
  starting transfers between devices: 0.04 us -> 13.6 us
  between operations: 13.4 us -> 0.07 us
  blocking collectives: 10.7 us -> 0 us
  other arithmetic: 5.01 us -> 0 us
    reduce_scatter x1 -> x0, waiting for transfers between devices: 41.4 us -> none  [per_device(): lax.psum_scatter(part.astype(jnp.bfloat16), ('exp', 'ten'), scatter_dimen...]
    dot_general x3 -> x0, matrix products: 40.6 us -> none  [the longest x1 15.4 us: per_device(): jnp.einsum('td,edf->etf', rows, w_up, preferred_element_type=jnp.float32)]
    pallas_call x0 -> x8, Pallas kernels: none -> 35.7 us  [the longest x1 17.7 us: gate_up_call(): pl.pallas_call(functools.partial(gate_up_body, expert_count, count), out_...]
    all_gather x1 -> x0, waiting for transfers between devices: 17.8 us -> none  [per_device(): rows = lax.all_gather(normed, ('exp', 'ten'), axis=0, tiled=True)]
    ppermute x0 -> x15, starting transfers between devices: none -> 13.6 us  [exchange(): return lax.ppermute(value, GROUP, [(i, i ^ mask) for i in range(size)])]
    ppermute x0 -> x15, waiting for transfers between devices: none -> 12.1 us  [exchange(): return lax.ppermute(value, GROUP, [(i, i ^ mask) for i in range(size)])]
    all_gather x1 -> x0, blocking collectives: 10.7 us -> none  [per_device(): weight = lax.all_gather(weight, ('exp', 'ten'), axis=0, tiled=True)]
    reduce_sum x3 -> x0, other arithmetic: 2.52 us -> none  [the longest x1 1.11 us: per_device(): meansq = jnp.mean(floats * floats, axis=1, keepdims=True)]
  transfers between devices with their start and end apart: 2 -> 15, of which waited for: 2 -> 8; matrix products, arithmetic and copies ran while one was open for 2% -> 0% of each run, Pallas kernels for 0% -> 20%
where the time goes in v3:
time: 61.5 us; the launch traced here: 61.4 us
  Pallas kernels  35.7 us (58%)
  starting transfers between devices  13.6 us (22%)
  waiting for transfers between devices  12.1 us (20%)
    pallas_call x1, Pallas kernels, gate_up_call(): pl.pallas_call(functools.partial(gate_up_body, expert_count, count), out_...  17.7 us
    ppermute x15, starting transfers between devices, exchange(): return lax.ppermute(value, GROUP, [(i, i ^ mask) for i in range(size)])  13.6 us
    ppermute x15, waiting for transfers between devices, exchange(): return lax.ppermute(value, GROUP, [(i, i ^ mask) for i in range(size)])  12.1 us
    pallas_call x1, Pallas kernels, fetch_call(): pl.pallas_call(functools.partial(fetch_body, slots), out_shape=[pltpu.VME...  8.89 us
    pallas_call x2, Pallas kernels, down_call(): pl.pallas_call(functools.partial(down_body, half, start), out_shape=[pltp...  6.8 us
  transfers between devices with their start and end apart: 15, of which 8 were waited for; matrix products, arithmetic and copies ran while one was open for 0% of the time, Pallas kernels for 20%

profile of v3, /device:TPU:0, one launch (start us, length us, event | category | flops | bytes accessed | tf_op | source)
XLA Modules:
  0.0 61.4 jit_solution(6039871628586717375)
XLA Ops:
  0.0 1.2 %shard_map.73.order_ref.refs_0_ = bf16[32,4224]{1,0:T(8,128)(2,1)S(1)} custom-call(bf16[32,4096]{1,0:T(8,128)(2,1)} %refs_0_.1, f32[1,4096]{1,0:T(1,128)} %bitcast.5, s32[8,32]{1,0:T(8,128)} %bitcast.6, f32[8,32]{1,0:T(8,128)} %bitcast.7), custom_call_target="tpu_custom_call" | custom-call | tf_op jit(solution)/shard_map/pallas_call | solution.py:79
  1.2 4.0 %collective-permute-start.2 = (bf16[32,4224]{1,0:T(8,128)(2,1)S(1)}, bf16[32,4224]{1,0:T(8,128)(2,1)S(1)}, u32[]{:S(2)}, u32[]{:S(2)}) collective-permute-start(bf16[32,4224]{1,0:T(8,128)(2,1)S(1)} %shard_map.73.order_ref.refs_0_), channel_id=1, source_target_pairs={{0,6},{1,7},{2,4},{3,5},{4,2},{5,3},{6,0},{7,1},{8,14},{9,15},{10,... | collective-permute-start | bytes 811016 | tf_op jit(solution)/shard_map/ppermute | solution.py:38
  5.1 0.5 collective-permute-start.1
  5.8 8.9 %shard_map.74 = (bf16[4,4096,384]{2,1,0:T(8,128)(2,1)S(1)}, bf16[4,4096,384]{2,1,0:T(8,128)(2,1)S(1)}, f32[8,128]{1,0:T(8,128)}) custom-call(bf16[32,4224]{1,0:T(8,128)(2,1)S(1)} %shard_map.73.order_ref.refs_0_, bf16[8,4096,384]{2,1,0:T(8,128)(2,1)} %refs_10_.1, bf16[8,4096,384]{2,1,0:T(8,128)(2,1)} %refs_11_.1), custom_call_target="tpu_custom_call" | custom-call | bytes 50331648 | tf_op jit(solution)/shard_map/pallas_call | solution.py:106
  14.7 3.0 %collective-permute-done.1.refs_2_ = bf16[32,4224]{1,0:T(8,128)(2,1)S(1)} collective-permute-done((bf16[32,4224]{1,0:T(8,128)(2,1)S(1)}, bf16[32,4224]{1,0:T(8,128)(2,1)S(1)}, u32[]{:S(2)}, u32[]{:S(2)}) %collective-permute-start.1) | collective-permute-done | bytes 270368 | tf_op jit(solution)/shard_map/ppermute | solution.py:38
  17.7 0.5 collective-permute-start.5
  18.2 1.0 %collective-permute-done.4.refs_5_ = bf16[32,4224]{1,0:T(8,128)(2,1)S(1)} collective-permute-done((bf16[32,4224]{1,0:T(8,128)(2,1)S(1)}, bf16[32,4224]{1,0:T(8,128)(2,1)S(1)}, u32[]{:S(2)}, u32[]{:S(2)}) %collective-permute-start.4) | collective-permute-done | bytes 270368 | tf_op jit(solution)/shard_map/ppermute | solution.py:38
  19.3 0.4 collective-permute-done.5.refs_6_
  19.6 0.4 collective-permute-done.6.refs_7_
  20.0 17.7 %shard_map.75 = (bf16[256,3072]{1,0:T(8,128)(2,1)S(1)}, bf16[3072,4096]{1,0:T(8,128)(2,1)S(1)}, bf16[4,4096,384]{2,1,0:T(8,128)(2,1)S(1)}, bf16[4,4096,384]{2,1,0:T(8,128)(2,1)S(1)}) custom-call(bf16[32,4224]{1,0:T(8,128)(2,1)S(1)} %shard_map.73.order_ref.refs_0_, ...), custom_call_target="tpu_custom_call", output_to_operand_aliasing={{2}: (8, {}), {3}: (9, {})} | custom-call | flops 12884901888 | bytes 75497472 | tf_op jit(solution)/shard_map/pallas_call | solution.py:175
  37.8 3.4 %shard_map.78 = (bf16[128,2048]{1,0:T(8,128)(2,1)S(1)}, bf16[128,2048]{1,0:T(8,128)(2,1)S(1)}) custom-call(bf16[256,3072]{1,0:T(8,128)(2,1)S(1)} %get-tuple-element.31.hidden_ref, bf16[3072,4096]{1,0:T(8,128)(2,1)S(1)} %get-tuple-element.32.weight_ref), custom_call_target="tpu_custom_call" | custom-call | flops 3221225472 | bytes 12582912 | tf_op jit(solution)/shard_map/pallas_call | solution.py:207
  41.4 3.4 %shard_map.76 = (bf16[128,2048]{1,0:T(8,128)(2,1)S(1)}, bf16[128,2048]{1,0:T(8,128)(2,1)S(1)}) custom-call(bf16[256,3072]{1,0:T(8,128)(2,1)S(1)} %get-tuple-element.31.hidden_ref, bf16[3072,4096]{1,0:T(8,128)(2,1)S(1)} %get-tuple-element.32.weight_ref), custom_call_target="tpu_custom_call" | custom-call | flops 3221225472 | bytes 12582912 | tf_op jit(solution)/shard_map/pallas_call | solution.py:207
  44.8 0.4 collective-permute-start.7
  45.4 1.5 %collective-permute-start.12 = (bf16[32,2048]{1,0:T(8,128)(2,1)S(1)}, bf16[32,2048]{1,0:T(8,128)(2,1)S(1)}, u32[]{:S(2)}, u32[]{:S(2)}) collective-permute-start(bf16[32,2048]{1,0:T(8,128)(2,1)S(1)} %get-tuple-element.42), channel_id=1, source_target_pairs={{0,2},{1,3},{2,0},{3,1},{4,6},{5,7},{6,4},{7,5},{8,10},{9,11},{10,... | collective-permute-start | bytes 393224 | tf_op jit(solution)/shard_map/ppermute | solution.py:38
  46.8 1.5 %collective-permute-start.13 = (bf16[32,2048]{1,0:T(8,128)(2,1)S(1)}, bf16[32,2048]{1,0:T(8,128)(2,1)S(1)}, u32[]{:S(2)}, u32[]{:S(2)}) collective-permute-start(bf16[32,2048]{1,0:T(8,128)(2,1)S(1)} %get-tuple-element.43), channel_id=1, source_target_pairs={{0,4},{1,5},{2,6},{3,7},{4,0},{5,1},{6,2},{7,3},{8,12},{9,13},{10,... | collective-permute-start | bytes 393224 | tf_op jit(solution)/shard_map/ppermute | solution.py:38
  48.3 0.6 collective-permute-start.14
  49.0 1.5 %collective-permute-start.8 = (bf16[32,2048]{1,0:T(8,128)(2,1)S(1)}, bf16[32,2048]{1,0:T(8,128)(2,1)S(1)}, u32[]{:S(2)}, u32[]{:S(2)}) collective-permute-start(bf16[32,2048]{1,0:T(8,128)(2,1)S(1)} %get-tuple-element.36), channel_id=1, source_target_pairs={{0,2},{1,3},{2,0},{3,1},{4,6},{5,7},{6,4},{7,5},{8,10},{9,11},{10,... | collective-permute-start | bytes 393224 | tf_op jit(solution)/shard_map/ppermute | solution.py:38
  50.5 1.5 %collective-permute-start.9 = (bf16[32,2048]{1,0:T(8,128)(2,1)S(1)}, bf16[32,2048]{1,0:T(8,128)(2,1)S(1)}, u32[]{:S(2)}, u32[]{:S(2)}) collective-permute-start(bf16[32,2048]{1,0:T(8,128)(2,1)S(1)} %get-tuple-element.37), channel_id=1, source_target_pairs={{0,4},{1,5},{2,6},{3,7},{4,0},{5,1},{6,2},{7,3},{8,12},{9,13},{10,... | collective-permute-start | bytes 393224 | tf_op jit(solution)/shard_map/ppermute | solution.py:38
  52.0 1.3 %collective-permute-start.10 = (bf16[32,2048]{1,0:T(8,128)(2,1)S(1)}, bf16[32,2048]{1,0:T(8,128)(2,1)S(1)}, u32[]{:S(2)}, u32[]{:S(2)}) collective-permute-start(bf16[32,2048]{1,0:T(8,128)(2,1)S(1)} %get-tuple-element.38), channel_id=1, source_target_pairs={{0,6},{1,7},{2,4},{3,5},{4,2},{5,3},{6,0},{7,1},{8,14},{9,15},{10,... | collective-permute-start | bytes 393224 | tf_op jit(solution)/shard_map/ppermute | solution.py:38
  53.3 2.4 %collective-permute-done.14.refs_7_ = bf16[32,2048]{1,0:T(8,128)(2,1)S(1)} collective-permute-done((bf16[32,2048]{1,0:T(8,128)(2,1)S(1)}, bf16[32,2048]{1,0:T(8,128)(2,1)S(1)}, u32[]{:S(2)}, u32[]{:S(2)}) %collective-permute-start.14) | collective-permute-done | bytes 131104 | tf_op jit(solution)/shard_map/ppermute | solution.py:38
  55.7 0.9 %collective-permute-done.8.refs_1_ = bf16[32,2048]{1,0:T(8,128)(2,1)S(1)} collective-permute-done((bf16[32,2048]{1,0:T(8,128)(2,1)S(1)}, bf16[32,2048]{1,0:T(8,128)(2,1)S(1)}, u32[]{:S(2)}, u32[]{:S(2)}) %collective-permute-start.8) | collective-permute-done | bytes 131104 | tf_op jit(solution)/shard_map/ppermute | solution.py:38
  56.6 2.2 %collective-permute-done.9.refs_2_ = bf16[32,2048]{1,0:T(8,128)(2,1)S(1)} collective-permute-done((bf16[32,2048]{1,0:T(8,128)(2,1)S(1)}, bf16[32,2048]{1,0:T(8,128)(2,1)S(1)}, u32[]{:S(2)}, u32[]{:S(2)}) %collective-permute-start.9) | collective-permute-done | bytes 131104 | tf_op jit(solution)/shard_map/ppermute | solution.py:38
  58.8 1.7 %collective-permute-done.10.refs_3_ = bf16[32,2048]{1,0:T(8,128)(2,1)S(1)} collective-permute-done((bf16[32,2048]{1,0:T(8,128)(2,1)S(1)}, bf16[32,2048]{1,0:T(8,128)(2,1)S(1)}, u32[]{:S(2)}, u32[]{:S(2)}) %collective-permute-start.10) | collective-permute-done | bytes 131104 | tf_op jit(solution)/shard_map/ppermute | solution.py:38
  60.6 0.8 %shard_map.80 = bf16[32,4096]{1,0:T(8,128)(2,1)} custom-call(bf16[32,2048]{1,0:T(8,128)(2,1)S(1)} %get-tuple-element.35.refs_0_, bf16[32,2048]{1,0:T(8,128)(2,1)S(1)} %collective-permute-done.8.refs_1_, bf16[32,2048]{1,0:T(8,128)(2,1)S(1)} %collective-permute-done.9.refs_2_, bf16[32,2048]{1,0:T(8,128)(2,1)S(1)} %collective-permute-done.10.refs_3_, ...), custom_call_target="tpu_custom_call" | custom-call | tf_op jit(solution)/shard_map/pallas_call | solution.py:247
  (14 shorter events, 0.6 us)
Async XLA Ops:
  1.2 13.5 %collective-permute-start.2 = (bf16[32,4224]{1,0:T(8,128)(2,1)S(1)}, bf16[32,4224]{1,0:T(8,128)(2,1)S(1)}, u32[]{:S(2)}, u32[]{:S(2)}) collective-permute-start(bf16[32,4224]{1,0:T(8,128)(2,1)S(1)} %shard_map.73.order_ref.refs_0_), channel_id=1, source_target_pairs={{0,6},{1,7},{2,4},{3,5},{4,2},{5,3},{6,0},{7,1},{8,14},{9,15},{10,... | collective-permute-start | bytes 811016 | tf_op jit(solution)/shard_map/ppermute | solution.py:38
  5.1 12.6 %collective-permute-start.1 = (bf16[32,4224]{1,0:T(8,128)(2,1)S(1)}, bf16[32,4224]{1,0:T(8,128)(2,1)S(1)}, u32[]{:S(2)}, u32[]{:S(2)}) collective-permute-start(bf16[32,4224]{1,0:T(8,128)(2,1)S(1)} %shard_map.73.order_ref.refs_0_), channel_id=1, source_target_pairs={{0,4},{1,5},{2,6},{3,7},{4,0},{5,1},{6,2},{7,3},{8,12},{9,13},{10,... | collective-permute-start | bytes 811016 | tf_op jit(solution)/shard_map/ppermute | solution.py:38
  5.7 12.0 %collective-permute-start = (bf16[32,4224]{1,0:T(8,128)(2,1)S(1)}, bf16[32,4224]{1,0:T(8,128)(2,1)S(1)}, u32[]{:S(2)}, u32[]{:S(2)}) collective-permute-start(bf16[32,4224]{1,0:T(8,128)(2,1)S(1)} %shard_map.73.order_ref.refs_0_), channel_id=1, source_target_pairs={{0,2},{1,3},{2,0},{3,1},{4,6},{5,7},{6,4},{7,5},{8,10},{9,11},{10,... | collective-permute-start | bytes 811016 | tf_op jit(solution)/shard_map/ppermute | solution.py:38
  5.8 12.4 %collective-permute-start.3 = (bf16[32,4224]{1,0:T(8,128)(2,1)S(1)}, bf16[32,4224]{1,0:T(8,128)(2,1)S(1)}, u32[]{:S(2)}, u32[]{:S(2)}) collective-permute-start(bf16[32,4224]{1,0:T(8,128)(2,1)S(1)} %shard_map.73.order_ref.refs_0_), channel_id=1, source_target_pairs={{0,1},{1,0},{2,3},{3,2},{4,5},{5,4},{6,7},{7,6},{8,9},{9,8},{10,11... | collective-permute-start | bytes 811016 | tf_op jit(solution)/shard_map/ppermute | solution.py:38
  17.7 1.5 %collective-permute-start.4 = (bf16[32,4224]{1,0:T(8,128)(2,1)S(1)}, bf16[32,4224]{1,0:T(8,128)(2,1)S(1)}, u32[]{:S(2)}, u32[]{:S(2)}) collective-permute-start(bf16[32,4224]{1,0:T(8,128)(2,1)S(1)} %collective-permute-done.refs_1_), channel_id=1, source_target_pairs={{0,1},{1,0},{2,3},{3,2},{4,5},{5,4},{6,7},{7,6},{8,9},{9,8},{10,11... | collective-permute-start | bytes 811016 | tf_op jit(solution)/shard_map/ppermute | solution.py:38
  17.7 1.9 %collective-permute-start.5 = (bf16[32,4224]{1,0:T(8,128)(2,1)S(1)}, bf16[32,4224]{1,0:T(8,128)(2,1)S(1)}, u32[]{:S(2)}, u32[]{:S(2)}) collective-permute-start(bf16[32,4224]{1,0:T(8,128)(2,1)S(1)} %collective-permute-done.1.refs_2_), channel_id=1, source_target_pairs={{0,1},{1,0},{2,3},{3,2},{4,5},{5,4},{6,7},{7,6},{8,9},{9,8},{10,11... | collective-permute-start | bytes 811016 | tf_op jit(solution)/shard_map/ppermute | solution.py:38
  18.2 1.8 %collective-permute-start.6 = (bf16[32,4224]{1,0:T(8,128)(2,1)S(1)}, bf16[32,4224]{1,0:T(8,128)(2,1)S(1)}, u32[]{:S(2)}, u32[]{:S(2)}) collective-permute-start(bf16[32,4224]{1,0:T(8,128)(2,1)S(1)} %collective-permute-done.2.refs_3_), channel_id=1, source_target_pairs={{0,1},{1,0},{2,3},{3,2},{4,5},{5,4},{6,7},{7,6},{8,9},{9,8},{10,11... | collective-permute-start | bytes 811016 | tf_op jit(solution)/shard_map/ppermute | solution.py:38
  41.2 4.1 %collective-permute-start.11 = (bf16[128,2048]{1,0:T(8,128)(2,1)S(1)}, bf16[128,2048]{1,0:T(8,128)(2,1)S(1)}, u32[]{:S(2)}, u32[]{:S(2)}) collective-permute-start(bf16[128,2048]{1,0:T(8,128)(2,1)S(1)} %get-tuple-element.40), channel_id=1, source_target_pairs={{0,1},{1,0},{2,3},{3,2},{4,5},{5,4},{6,7},{7,6},{8,9},{9,8},{10,11... | collective-permute-start | bytes 1572872 | tf_op jit(solution)/shard_map/ppermute | solution.py:38
  44.8 4.1 %collective-permute-start.7 = (bf16[128,2048]{1,0:T(8,128)(2,1)S(1)}, bf16[128,2048]{1,0:T(8,128)(2,1)S(1)}, u32[]{:S(2)}, u32[]{:S(2)}) collective-permute-start(bf16[128,2048]{1,0:T(8,128)(2,1)S(1)} %get-tuple-element.34), channel_id=1, source_target_pairs={{0,1},{1,0},{2,3},{3,2},{4,5},{5,4},{6,7},{7,6},{8,9},{9,8},{10,11... | collective-permute-start | bytes 1572872 | tf_op jit(solution)/shard_map/ppermute | solution.py:38
  45.4 6.7 %collective-permute-start.12 = (bf16[32,2048]{1,0:T(8,128)(2,1)S(1)}, bf16[32,2048]{1,0:T(8,128)(2,1)S(1)}, u32[]{:S(2)}, u32[]{:S(2)}) collective-permute-start(bf16[32,2048]{1,0:T(8,128)(2,1)S(1)} %get-tuple-element.42), channel_id=1, source_target_pairs={{0,2},{1,3},{2,0},{3,1},{4,6},{5,7},{6,4},{7,5},{8,10},{9,11},{10,... | collective-permute-start | bytes 393224 | tf_op jit(solution)/shard_map/ppermute | solution.py:38
  46.8 6.5 %collective-permute-start.13 = (bf16[32,2048]{1,0:T(8,128)(2,1)S(1)}, bf16[32,2048]{1,0:T(8,128)(2,1)S(1)}, u32[]{:S(2)}, u32[]{:S(2)}) collective-permute-start(bf16[32,2048]{1,0:T(8,128)(2,1)S(1)} %get-tuple-element.43), channel_id=1, source_target_pairs={{0,4},{1,5},{2,6},{3,7},{4,0},{5,1},{6,2},{7,3},{8,12},{9,13},{10,... | collective-permute-start | bytes 393224 | tf_op jit(solution)/shard_map/ppermute | solution.py:38
  48.3 7.4 %collective-permute-start.14 = (bf16[32,2048]{1,0:T(8,128)(2,1)S(1)}, bf16[32,2048]{1,0:T(8,128)(2,1)S(1)}, u32[]{:S(2)}, u32[]{:S(2)}) collective-permute-start(bf16[32,2048]{1,0:T(8,128)(2,1)S(1)} %get-tuple-element.44), channel_id=1, source_target_pairs={{0,6},{1,7},{2,4},{3,5},{4,2},{5,3},{6,0},{7,1},{8,14},{9,15},{10,... | collective-permute-start | bytes 393224 | tf_op jit(solution)/shard_map/ppermute | solution.py:38
  49.0 7.6 %collective-permute-start.8 = (bf16[32,2048]{1,0:T(8,128)(2,1)S(1)}, bf16[32,2048]{1,0:T(8,128)(2,1)S(1)}, u32[]{:S(2)}, u32[]{:S(2)}) collective-permute-start(bf16[32,2048]{1,0:T(8,128)(2,1)S(1)} %get-tuple-element.36), channel_id=1, source_target_pairs={{0,2},{1,3},{2,0},{3,1},{4,6},{5,7},{6,4},{7,5},{8,10},{9,11},{10,... | collective-permute-start | bytes 393224 | tf_op jit(solution)/shard_map/ppermute | solution.py:38
  50.5 8.3 %collective-permute-start.9 = (bf16[32,2048]{1,0:T(8,128)(2,1)S(1)}, bf16[32,2048]{1,0:T(8,128)(2,1)S(1)}, u32[]{:S(2)}, u32[]{:S(2)}) collective-permute-start(bf16[32,2048]{1,0:T(8,128)(2,1)S(1)} %get-tuple-element.37), channel_id=1, source_target_pairs={{0,4},{1,5},{2,6},{3,7},{4,0},{5,1},{6,2},{7,3},{8,12},{9,13},{10,... | collective-permute-start | bytes 393224 | tf_op jit(solution)/shard_map/ppermute | solution.py:38
  52.0 8.6 %collective-permute-start.10 = (bf16[32,2048]{1,0:T(8,128)(2,1)S(1)}, bf16[32,2048]{1,0:T(8,128)(2,1)S(1)}, u32[]{:S(2)}, u32[]{:S(2)}) collective-permute-start(bf16[32,2048]{1,0:T(8,128)(2,1)S(1)} %get-tuple-element.38), channel_id=1, source_target_pairs={{0,6},{1,7},{2,4},{3,5},{4,2},{5,3},{6,0},{7,1},{8,14},{9,15},{10,... | collective-permute-start | bytes 393224 | tf_op jit(solution)/shard_map/ppermute | solution.py:38

commit v4 on v3

--- a/solution.py
+++ b/solution.py
@@ -12,8 +12,8 @@
 MIB = 2**20
 GROUP = ("exp", "ten")
 EXTRA = 128
-SLOTS = 4
-OUT_CHUNKS = 2
+SLOTS = 5
+AHEAD = 5
 VMEM_FULL = pl.BlockSpec(memory_space=pltpu.VMEM)
 ANY_FULL = pl.BlockSpec(memory_space=pl.ANY)
 
@@ -27,7 +27,7 @@
 
 
 def params(rows, width):
-    return pltpu.CompilerParams(vmem_limit_bytes=4 * MIB + 4 * rows * width)
+    return pltpu.CompilerParams(vmem_limit_bytes=2 * MIB + 4 * rows * width)
 
 
 def cost(flops, read):
@@ -87,10 +87,10 @@
     )(*[in_hbm(v) for v in args])
 
 
-def fetch_body(slots, order_ref, gate_hbm, up_hbm, gate_out, up_out, done_ref, sems):
+def fetch_body(ahead, order_ref, gate_hbm, up_hbm, gate_out, up_out, done_ref, sems):
     del order_ref
     copies = []
-    for e in range(slots):
+    for e in range(ahead):
         copies.append(pltpu.make_async_copy(gate_hbm.at[e], gate_out.at[e], sems.at[0, e]))
         copies.append(pltpu.make_async_copy(up_hbm.at[e], up_out.at[e], sems.at[1, e]))
     for copy in copies:
@@ -103,8 +103,9 @@
 def fetch_call(order, w_gate, w_up, scoped):
     local, width, hidden = w_gate.shape
     slots = min(SLOTS, local)
-    return pl.pallas_call(
-        functools.partial(fetch_body, slots),
+    ahead = min(AHEAD, local)
+    return pl.pallas_call(
+        functools.partial(fetch_body, ahead),
         out_shape=[pltpu.VMEM((slots, width, hidden), BF16)] * 2 + [pltpu.VMEM((8, 128), F32)],
         in_specs=[ANY_FULL] * 3,
         out_specs=[VMEM_FULL] * 3,
@@ -120,20 +121,25 @@
     out_ref, down_ref, gate_ref, up_ref, rows_ref, sems, down_sems = refs[5:]
     slots, width, hidden = gate_ref.shape
     local = gate_hbm.shape[0]
+    ahead = min(AHEAD, slots)
+    columns = down_ref.shape[1]
 
     def copies(e):
-        slot = e % slots
+        slot = lax.rem(e, slots)
         return [
             pltpu.make_async_copy(gate_hbm.at[e], gate_ref.at[slot], sems.at[0, slot]),
             pltpu.make_async_copy(up_hbm.at[e], up_ref.at[slot], sems.at[1, slot]),
         ]
 
     def down_copy(e):
-        at = slice(e * hidden, (e + 1) * hidden)
-        return pltpu.make_async_copy(down_hbm.at[at], down_ref.at[at], down_sems.at[e])
-
-    down_copy(0).start()
-    down_copy(1).start()
+        at = pl.ds(pl.multiple_of(e * hidden, hidden), hidden)
+        return pltpu.make_async_copy(down_hbm.at[at, :columns], down_ref.at[at], down_sems.at[e])
+
+    for e in range(ahead, slots):
+        for copy in copies(e):
+            copy.start()
+    for e in range(local):
+        down_copy(e).start()
     at = 0
     for piece in pieces:
         rows_ref[at : at + piece.shape[0]] = piece[...]
@@ -142,25 +148,29 @@
     row = lax.broadcasted_iota(jnp.int32, (EXTRA, hidden), 0)
     number = lax.axis_index("exp") * local
 
-    def finish(e, both):
+    def one(e, carry):
+        @pl.when((e >= 1) & (e <= local - slots))
+        def _():
+            for copy in copies(e - 1 + slots):
+                copy.start()
+
+        @pl.when(e >= ahead)
+        def _():
+            for copy in copies(e):
+                copy.wait()
+
+        slot = lax.rem(e, slots)
+        weights = jnp.concatenate([gate_ref[slot], up_ref[slot]], axis=1)
+        both = jnp.dot(rows_ref[:, :width], weights, preferred_element_type=F32)
         gate, up = both[:, :hidden], both[:, hidden:]
         pick = jnp.where((row % expert_count == number + e) & (row < 3 * expert_count), 1.0, 0.0)
         mixing = jnp.dot(rows_ref[:, width:], pick.astype(BF16), preferred_element_type=F32)
         value = gate / (1.0 + jnp.exp(-gate)) * up * mixing
-        out_ref[:, e * hidden : (e + 1) * hidden] = value.astype(BF16)
-
-    for e in range(local):
-        if e >= slots:
-            for copy in copies(e):
-                copy.wait()
-        weights = jnp.concatenate([gate_ref[e % slots], up_ref[e % slots]], axis=1)
-        both = jnp.dot(rows_ref[:, :width], weights, preferred_element_type=F32)
-        if e + slots < local:
-            for copy in copies(e + slots):
-                copy.start()
-        if e + 2 < local:
-            down_copy(e + 2).start()
-        finish(e, both)
+        at = pl.ds(pl.multiple_of(e * hidden, hidden), hidden)
+        out_ref[:, at] = value.astype(BF16)
+        return carry
+
+    lax.fori_loop(0, local, one, 0)
     for e in range(local):
         down_copy(e).wait()
 
@@ -174,7 +184,7 @@
     shape = pltpu.VMEM(gate_slots.shape, BF16)
     return pl.pallas_call(
         functools.partial(gate_up_body, expert_count, count),
-        out_shape=[pltpu.VMEM((rows, depth), BF16), pltpu.VMEM((depth, width), BF16), shape, shape],
+        out_shape=[pltpu.VMEM((rows, depth), BF16), pltpu.VMEM((depth, 3 * width // 4), BF16), shape, shape],
         in_specs=[VMEM_FULL] * (count + 2) + [ANY_FULL] * 3,
         out_specs=[VMEM_FULL] * 4,
         scratch_shapes=[
@@ -191,27 +201,61 @@
     )[:2]
 
 
-def down_body(half, start, hidden_ref, weight_ref, keep_ref, send_ref):
+def down_body(half, start, more, hidden_ref, *refs):
+    if more:
+        weight_ref, down_hbm, keep_ref, send_ref, rest_ref, sems = refs
+        parts = sems.shape[0]
+        step = rest_ref.shape[0] // parts
+        skip = down_hbm.shape[1] - rest_ref.shape[1]
+        copies = []
+        for i in range(parts):
+            at = slice(i * step, (i + 1) * step)
+            copies.append(
+                pltpu.make_async_copy(down_hbm.at[at, skip:], rest_ref.at[at], sems.at[i])
+            )
+    else:
+        weight_ref, rest_ref, keep_ref, send_ref = refs
+        copies = []
+    for copy in copies:
+        copy.start()
+    ready = weight_ref.shape[1]
     block = 512
-    for at in range(0, keep_ref.shape[1], block):
-        to = slice(at, at + block)
-        weights = weight_ref[:, start + at : start + at + block]
-        out = jnp.dot(hidden_ref[...], weights, preferred_element_type=F32).astype(BF16)
-        keep_ref[:, to] = out[:half]
-        send_ref[:, to] = out[half:]
-
-
-def down_call(hidden, weight, start, step, scoped):
+
+    def run(ref, skip, first, stop):
+        def one(i, carry):
+            to = pl.ds(pl.multiple_of(i * block, block), block)
+            at = pl.ds(pl.multiple_of(skip + i * block, block), block)
+            out = jnp.dot(hidden_ref[...], ref[:, at], preferred_element_type=F32).astype(BF16)
+            keep_ref[:, to] = out[:half]
+            send_ref[:, to] = out[half:]
+            return carry
+
+        lax.fori_loop(first, stop, one, 0)
+
+    stop = keep_ref.shape[1]
+    middle = min(stop, ready - start)
+    run(weight_ref, start, 0, middle // block)
+    if middle < stop:
+        run(rest_ref, start - ready, middle // block, stop // block)
+    for copy in copies:
+        copy.wait()
+
+
+def down_call(start, step, hidden, weight, w_down, rest, scoped):
     rows, depth = hidden.shape
     half = rows // 2
-    return pl.pallas_call(
-        functools.partial(down_body, half, start),
-        out_shape=[pltpu.VMEM((half, step), BF16)] * 2,
-        in_specs=[VMEM_FULL] * 2,
-        out_specs=[VMEM_FULL] * 2,
+    more = rest is None
+    last = w_down.shape[1] - weight.shape[1]
+    return pl.pallas_call(
+        functools.partial(down_body, half, start, more),
+        out_shape=[pltpu.VMEM((half, step), BF16)] * 2
+        + ([pltpu.VMEM((depth, last), BF16)] if more else []),
+        in_specs=[VMEM_FULL] * 2 + [ANY_FULL if more else VMEM_FULL],
+        out_specs=[VMEM_FULL] * (3 if more else 2),
+        scratch_shapes=[pltpu.SemaphoreType.DMA((8,))] if more else [],
         compiler_params=scoped,
         cost_estimate=cost(2 * rows * depth * step, 2 * depth * step),
-    )(in_vmem(hidden), in_vmem(weight))
+    )(in_vmem(hidden), in_vmem(weight), in_hbm(w_down) if more else in_vmem(rest))
 
 
 def pair_body(keep_ref, got_ref, *outs):
@@ -270,13 +314,15 @@
     mixed_hidden, weight = gate_up_call(
         pieces, gate_slots, up_slots, w_gate, w_up, w_rows, expert_count, scoped
     )
-    step = width // OUT_CHUNKS
+    step = width // 2
+    keep_a, send_a, rest = down_call(0, step, mixed_hidden, weight, w_rows, None, scoped)
+    keep_b, send_b = down_call(step, step, mixed_hidden, weight, w_rows, rest, scoped)
     parts = []
-    for j in range(OUT_CHUNKS):
-        keep, send = down_call(mixed_hidden, weight, j * step, step, scoped)
+    for keep, send in ((keep_a, send_a), (keep_b, send_b)):
         blocks = pair_call(keep, exchange(send, size, 1), rows, scoped)
-        parts += [blocks[0]] + [exchange(b, size, mask) for b, mask in zip(blocks[1:], far)]
-    return finish_call(parts, OUT_CHUNKS, rows, width, scoped)
+        parts += [exchange(b, size, mask) for b, mask in zip(blocks[:0:-1], far[::-1])]
+        parts.append(blocks[0])
+    return finish_call(parts, 2, rows, width, scoped)
 
 
 def solution(mesh):

time: 61.5 us -> 60.2 us (0.979)
  waiting for transfers between devices: 12.1 us -> 9.89 us
  Pallas kernels: 35.7 us -> 36.4 us
    pallas_call x3, Pallas kernels: 15.7 us -> 18.7 us  [the longest x1 10.7 us: fetch_call(): pl.pallas_call(functools.partial(fetch_body, ahead), out_shape=[pltpu.VME...]
    pallas_call x1, Pallas kernels: 17.7 us -> 15.5 us  [gate_up_call(): pl.pallas_call(functools.partial(gate_up_body, expert_count, count), out_...]
    ppermute x15, waiting for transfers between devices: 12.1 us -> 9.89 us  [exchange(): return lax.ppermute(value, GROUP, [(i, i ^ mask) for i in range(size)])]
  transfers between devices with their start and end apart: 15 -> 15, of which waited for: 8 -> 9; matrix products, arithmetic and copies ran while one was open for 0% -> 0% of each run, Pallas kernels for 20% -> 25%
where the time goes in v4:
time: 60.2 us; the launch traced here: 60.1 us
  Pallas kernels  36.4 us (60%)
  starting transfers between devices  13.7 us (23%)
  waiting for transfers between devices  9.89 us (16%)
    pallas_call x1, Pallas kernels, gate_up_call(): pl.pallas_call(functools.partial(gate_up_body, expert_count, count), out_...  15.5 us
    ppermute x15, starting transfers between devices, exchange(): return lax.ppermute(value, GROUP, [(i, i ^ mask) for i in range(size)])  13.7 us
    pallas_call x1, Pallas kernels, fetch_call(): pl.pallas_call(functools.partial(fetch_body, ahead), out_shape=[pltpu.VME...  10.7 us
    ppermute x15, waiting for transfers between devices, exchange(): return lax.ppermute(value, GROUP, [(i, i ^ mask) for i in range(size)])  9.89 us
    pallas_call x2, Pallas kernels, down_call(): pl.pallas_call(functools.partial(down_body, half, start, more), out_shape...  8 us
  transfers between devices with their start and end apart: 15, of which 9 were waited for; matrix products, arithmetic and copies ran while one was open for 0% of the time, Pallas kernels for 25%

profile of v4, /device:TPU:0, one launch (start us, length us, event | category | flops | bytes accessed | tf_op | source)
XLA Modules:
  0.0 60.1 jit_solution(12688557143416808357)
XLA Ops:
  0.0 1.2 %shard_map.73.order_ref.refs_0_ = bf16[32,4224]{1,0:T(8,128)(2,1)S(1)} custom-call(bf16[32,4096]{1,0:T(8,128)(2,1)} %refs_0_.1, f32[1,4096]{1,0:T(1,128)} %bitcast.6, s32[8,32]{1,0:T(8,128)} %bitcast.7, f32[8,32]{1,0:T(8,128)} %bitcast.8), custom_call_target="tpu_custom_call" | custom-call | tf_op jit(solution)/shard_map/pallas_call | solution.py:79
  1.2 4.0 %collective-permute-start.2 = (bf16[32,4224]{1,0:T(8,128)(2,1)S(1)}, bf16[32,4224]{1,0:T(8,128)(2,1)S(1)}, u32[]{:S(2)}, u32[]{:S(2)}) collective-permute-start(bf16[32,4224]{1,0:T(8,128)(2,1)S(1)} %shard_map.73.order_ref.refs_0_), channel_id=1, source_target_pairs={{0,6},{1,7},{2,4},{3,5},{4,2},{5,3},{6,0},{7,1},{8,14},{9,15},{10,... | collective-permute-start | bytes 811016 | tf_op jit(solution)/shard_map/ppermute | solution.py:38
  5.1 0.5 collective-permute-start.1
  5.8 10.7 %shard_map.74 = (bf16[5,4096,384]{2,1,0:T(8,128)(2,1)S(1)}, bf16[5,4096,384]{2,1,0:T(8,128)(2,1)S(1)}, f32[8,128]{1,0:T(8,128)}) custom-call(bf16[32,4224]{1,0:T(8,128)(2,1)S(1)} %shard_map.73.order_ref.refs_0_, bf16[8,4096,384]{2,1,0:T(8,128)(2,1)} %refs_10_.1, bf16[8,4096,384]{2,1,0:T(8,128)(2,1)} %refs_11_.1), custom_call_target="tpu_custom_call" | custom-call | bytes 62914560 | tf_op jit(solution)/shard_map/pallas_call | solution.py:107
  16.5 1.2 %collective-permute-done.1.refs_2_ = bf16[32,4224]{1,0:T(8,128)(2,1)S(1)} collective-permute-done((bf16[32,4224]{1,0:T(8,128)(2,1)S(1)}, bf16[32,4224]{1,0:T(8,128)(2,1)S(1)}, u32[]{:S(2)}, u32[]{:S(2)}) %collective-permute-start.1) | collective-permute-done | bytes 270368 | tf_op jit(solution)/shard_map/ppermute | solution.py:38
  17.7 0.5 collective-permute-start.5
  18.2 1.0 %collective-permute-done.4.refs_5_ = bf16[32,4224]{1,0:T(8,128)(2,1)S(1)} collective-permute-done((bf16[32,4224]{1,0:T(8,128)(2,1)S(1)}, bf16[32,4224]{1,0:T(8,128)(2,1)S(1)}, u32[]{:S(2)}, u32[]{:S(2)}) %collective-permute-start.4) | collective-permute-done | bytes 270368 | tf_op jit(solution)/shard_map/ppermute | solution.py:38
  19.3 0.4 collective-permute-done.5.refs_6_
  20.0 15.5 %shard_map.75 = (bf16[256,3072]{1,0:T(8,128)(2,1)S(1)}, bf16[3072,3072]{1,0:T(8,128)(2,1)S(1)}, bf16[5,4096,384]{2,1,0:T(8,128)(2,1)S(1)}, bf16[5,4096,384]{2,1,0:T(8,128)(2,1)S(1)}) custom-call(bf16[32,4224]{1,0:T(8,128)(2,1)S(1)} %shard_map.73.order_ref.refs_0_, ...), custom_call_target="tpu_custom_call", output_to_operand_aliasing={{2}: (8, {}), {3}: (9, {})} | custom-call | flops 12884901888 | bytes 75497472 | tf_op jit(solution)/shard_map/pallas_call | solution.py:185
  35.5 4.1 %shard_map.76 = (bf16[128,2048]{1,0:T(8,128)(2,1)S(1)}, bf16[128,2048]{1,0:T(8,128)(2,1)S(1)}, bf16[3072,1024]{1,0:T(8,128)(2,1)S(1)}) custom-call(bf16[256,3072]{1,0:T(8,128)(2,1)S(1)} %get-tuple-element.32.hidden_ref, bf16[3072,3072]{1,0:T(8,128)(2,1)S(1)} %get-tuple-element.33.refs_0_, bf16[3072,4096]{1,0:T(8,128)(2,1)} %bitcast.5), custom_call_target="tpu_custom_call" | custom-call | flops 3221225472 | bytes 12582912 | tf_op jit(solution)/shard_map/pallas_call | solution.py:249
  39.8 3.9 %shard_map.78 = (bf16[128,2048]{1,0:T(8,128)(2,1)S(1)}, bf16[128,2048]{1,0:T(8,128)(2,1)S(1)}) custom-call(bf16[256,3072]{1,0:T(8,128)(2,1)S(1)} %get-tuple-element.32.hidden_ref, bf16[3072,3072]{1,0:T(8,128)(2,1)S(1)} %get-tuple-element.33.refs_0_, bf16[3072,1024]{1,0:T(8,128)(2,1)S(1)} %get-tuple-element.40.refs_1_), custom_call_target="tpu_custom_call" | custom-call | flops 3221225472 | bytes 12582912 | tf_op jit(solution)/shard_map/pallas_call | solution.py:249
  43.7 0.4 collective-permute-start.11
  44.3 2.4 %collective-permute-start.8 = (bf16[32,2048]{1,0:T(8,128)(2,1)S(1)}, bf16[32,2048]{1,0:T(8,128)(2,1)S(1)}, u32[]{:S(2)}, u32[]{:S(2)}) collective-permute-start(bf16[32,2048]{1,0:T(8,128)(2,1)S(1)} %get-tuple-element.36), channel_id=1, source_target_pairs={{0,6},{1,7},{2,4},{3,5},{4,2},{5,3},{6,0},{7,1},{8,14},{9,15},{10,... | collective-permute-start | bytes 393224 | tf_op jit(solution)/shard_map/ppermute | solution.py:38
  46.7 0.5 collective-permute-start.9
  47.3 0.6 collective-permute-start.10
  48.0 2.4 %collective-permute-start.12 = (bf16[32,2048]{1,0:T(8,128)(2,1)S(1)}, bf16[32,2048]{1,0:T(8,128)(2,1)S(1)}, u32[]{:S(2)}, u32[]{:S(2)}) collective-permute-start(bf16[32,2048]{1,0:T(8,128)(2,1)S(1)} %get-tuple-element.43), channel_id=1, source_target_pairs={{0,6},{1,7},{2,4},{3,5},{4,2},{5,3},{6,0},{7,1},{8,14},{9,15},{10,... | collective-permute-start | bytes 393224 | tf_op jit(solution)/shard_map/ppermute | solution.py:38
  50.4 0.5 collective-permute-start.13
  50.9 0.7 %collective-permute-done.8.refs_0_ = bf16[32,2048]{1,0:T(8,128)(2,1)S(1)} collective-permute-done((bf16[32,2048]{1,0:T(8,128)(2,1)S(1)}, bf16[32,2048]{1,0:T(8,128)(2,1)S(1)}, u32[]{:S(2)}, u32[]{:S(2)}) %collective-permute-start.8) | collective-permute-done | bytes 131104 | tf_op jit(solution)/shard_map/ppermute | solution.py:38
  51.6 1.4 %collective-permute-start.14 = (bf16[32,2048]{1,0:T(8,128)(2,1)S(1)}, bf16[32,2048]{1,0:T(8,128)(2,1)S(1)}, u32[]{:S(2)}, u32[]{:S(2)}) collective-permute-start(bf16[32,2048]{1,0:T(8,128)(2,1)S(1)} %get-tuple-element.45), channel_id=1, source_target_pairs={{0,2},{1,3},{2,0},{3,1},{4,6},{5,7},{6,4},{7,5},{8,10},{9,11},{10,... | collective-permute-start | bytes 393224 | tf_op jit(solution)/shard_map/ppermute | solution.py:38
  53.0 1.3 %collective-permute-done.9.refs_1_ = bf16[32,2048]{1,0:T(8,128)(2,1)S(1)} collective-permute-done((bf16[32,2048]{1,0:T(8,128)(2,1)S(1)}, bf16[32,2048]{1,0:T(8,128)(2,1)S(1)}, u32[]{:S(2)}, u32[]{:S(2)}) %collective-permute-start.9) | collective-permute-done | bytes 131104 | tf_op jit(solution)/shard_map/ppermute | solution.py:38
  54.4 2.1 %collective-permute-done.10.refs_2_ = bf16[32,2048]{1,0:T(8,128)(2,1)S(1)} collective-permute-done((bf16[32,2048]{1,0:T(8,128)(2,1)S(1)}, bf16[32,2048]{1,0:T(8,128)(2,1)S(1)}, u32[]{:S(2)}, u32[]{:S(2)}) %collective-permute-start.10) | collective-permute-done | bytes 131104 | tf_op jit(solution)/shard_map/ppermute | solution.py:38
  56.5 0.8 %collective-permute-done.12.refs_4_ = bf16[32,2048]{1,0:T(8,128)(2,1)S(1)} collective-permute-done((bf16[32,2048]{1,0:T(8,128)(2,1)S(1)}, bf16[32,2048]{1,0:T(8,128)(2,1)S(1)}, u32[]{:S(2)}, u32[]{:S(2)}) %collective-permute-start.12) | collective-permute-done | bytes 131104 | tf_op jit(solution)/shard_map/ppermute | solution.py:38
  57.3 2.0 %collective-permute-done.13.refs_5_ = bf16[32,2048]{1,0:T(8,128)(2,1)S(1)} collective-permute-done((bf16[32,2048]{1,0:T(8,128)(2,1)S(1)}, bf16[32,2048]{1,0:T(8,128)(2,1)S(1)}, u32[]{:S(2)}, u32[]{:S(2)}) %collective-permute-start.13) | collective-permute-done | bytes 131104 | tf_op jit(solution)/shard_map/ppermute | solution.py:38
  59.2 0.8 %shard_map.80 = bf16[32,4096]{1,0:T(8,128)(2,1)} custom-call(bf16[32,2048]{1,0:T(8,128)(2,1)S(1)} %collective-permute-done.8.refs_0_, bf16[32,2048]{1,0:T(8,128)(2,1)S(1)} %collective-permute-done.9.refs_1_, bf16[32,2048]{1,0:T(8,128)(2,1)S(1)} %collective-permute-done.10.refs_2_, bf16[32,2048]{1,0:T(8,128)(2,1)S(1)} %get-tuple-element.39.refs_3_, ...), custom_call_target="tpu_custom_call" | custom-call | tf_op jit(solution)/shard_map/pallas_call | solution.py:291
  (14 shorter events, 1.0 us)
Async XLA Ops:
  1.2 15.3 %collective-permute-start.2 = (bf16[32,4224]{1,0:T(8,128)(2,1)S(1)}, bf16[32,4224]{1,0:T(8,128)(2,1)S(1)}, u32[]{:S(2)}, u32[]{:S(2)}) collective-permute-start(bf16[32,4224]{1,0:T(8,128)(2,1)S(1)} %shard_map.73.order_ref.refs_0_), channel_id=1, source_target_pairs={{0,6},{1,7},{2,4},{3,5},{4,2},{5,3},{6,0},{7,1},{8,14},{9,15},{10,... | collective-permute-start | bytes 811016 | tf_op jit(solution)/shard_map/ppermute | solution.py:38
  5.1 12.6 %collective-permute-start.1 = (bf16[32,4224]{1,0:T(8,128)(2,1)S(1)}, bf16[32,4224]{1,0:T(8,128)(2,1)S(1)}, u32[]{:S(2)}, u32[]{:S(2)}) collective-permute-start(bf16[32,4224]{1,0:T(8,128)(2,1)S(1)} %shard_map.73.order_ref.refs_0_), channel_id=1, source_target_pairs={{0,4},{1,5},{2,6},{3,7},{4,0},{5,1},{6,2},{7,3},{8,12},{9,13},{10,... | collective-permute-start | bytes 811016 | tf_op jit(solution)/shard_map/ppermute | solution.py:38
  5.7 12.0 %collective-permute-start = (bf16[32,4224]{1,0:T(8,128)(2,1)S(1)}, bf16[32,4224]{1,0:T(8,128)(2,1)S(1)}, u32[]{:S(2)}, u32[]{:S(2)}) collective-permute-start(bf16[32,4224]{1,0:T(8,128)(2,1)S(1)} %shard_map.73.order_ref.refs_0_), channel_id=1, source_target_pairs={{0,2},{1,3},{2,0},{3,1},{4,6},{5,7},{6,4},{7,5},{8,10},{9,11},{10,... | collective-permute-start | bytes 811016 | tf_op jit(solution)/shard_map/ppermute | solution.py:38
  5.8 12.4 %collective-permute-start.3 = (bf16[32,4224]{1,0:T(8,128)(2,1)S(1)}, bf16[32,4224]{1,0:T(8,128)(2,1)S(1)}, u32[]{:S(2)}, u32[]{:S(2)}) collective-permute-start(bf16[32,4224]{1,0:T(8,128)(2,1)S(1)} %shard_map.73.order_ref.refs_0_), channel_id=1, source_target_pairs={{0,1},{1,0},{2,3},{3,2},{4,5},{5,4},{6,7},{7,6},{8,9},{9,8},{10,11... | collective-permute-start | bytes 811016 | tf_op jit(solution)/shard_map/ppermute | solution.py:38
  17.7 1.5 %collective-permute-start.4 = (bf16[32,4224]{1,0:T(8,128)(2,1)S(1)}, bf16[32,4224]{1,0:T(8,128)(2,1)S(1)}, u32[]{:S(2)}, u32[]{:S(2)}) collective-permute-start(bf16[32,4224]{1,0:T(8,128)(2,1)S(1)} %collective-permute-done.refs_1_), channel_id=1, source_target_pairs={{0,1},{1,0},{2,3},{3,2},{4,5},{5,4},{6,7},{7,6},{8,9},{9,8},{10,11... | collective-permute-start | bytes 811016 | tf_op jit(solution)/shard_map/ppermute | solution.py:38
  17.7 1.9 %collective-permute-start.5 = (bf16[32,4224]{1,0:T(8,128)(2,1)S(1)}, bf16[32,4224]{1,0:T(8,128)(2,1)S(1)}, u32[]{:S(2)}, u32[]{:S(2)}) collective-permute-start(bf16[32,4224]{1,0:T(8,128)(2,1)S(1)} %collective-permute-done.1.refs_2_), channel_id=1, source_target_pairs={{0,1},{1,0},{2,3},{3,2},{4,5},{5,4},{6,7},{7,6},{8,9},{9,8},{10,11... | collective-permute-start | bytes 811016 | tf_op jit(solution)/shard_map/ppermute | solution.py:38
  18.2 1.8 %collective-permute-start.6 = (bf16[32,4224]{1,0:T(8,128)(2,1)S(1)}, bf16[32,4224]{1,0:T(8,128)(2,1)S(1)}, u32[]{:S(2)}, u32[]{:S(2)}) collective-permute-start(bf16[32,4224]{1,0:T(8,128)(2,1)S(1)} %collective-permute-done.2.refs_3_), channel_id=1, source_target_pairs={{0,1},{1,0},{2,3},{3,2},{4,5},{5,4},{6,7},{7,6},{8,9},{9,8},{10,11... | collective-permute-start | bytes 811016 | tf_op jit(solution)/shard_map/ppermute | solution.py:38
  39.6 4.6 %collective-permute-start.7 = (bf16[128,2048]{1,0:T(8,128)(2,1)S(1)}, bf16[128,2048]{1,0:T(8,128)(2,1)S(1)}, u32[]{:S(2)}, u32[]{:S(2)}) collective-permute-start(bf16[128,2048]{1,0:T(8,128)(2,1)S(1)} %get-tuple-element.35), channel_id=1, source_target_pairs={{0,1},{1,0},{2,3},{3,2},{4,5},{5,4},{6,7},{7,6},{8,9},{9,8},{10,11... | collective-permute-start | bytes 1572872 | tf_op jit(solution)/shard_map/ppermute | solution.py:38
  43.7 4.1 %collective-permute-start.11 = (bf16[128,2048]{1,0:T(8,128)(2,1)S(1)}, bf16[128,2048]{1,0:T(8,128)(2,1)S(1)}, u32[]{:S(2)}, u32[]{:S(2)}) collective-permute-start(bf16[128,2048]{1,0:T(8,128)(2,1)S(1)} %get-tuple-element.42), channel_id=1, source_target_pairs={{0,1},{1,0},{2,3},{3,2},{4,5},{5,4},{6,7},{7,6},{8,9},{9,8},{10,11... | collective-permute-start | bytes 1572872 | tf_op jit(solution)/shard_map/ppermute | solution.py:38
  44.3 7.3 %collective-permute-start.8 = (bf16[32,2048]{1,0:T(8,128)(2,1)S(1)}, bf16[32,2048]{1,0:T(8,128)(2,1)S(1)}, u32[]{:S(2)}, u32[]{:S(2)}) collective-permute-start(bf16[32,2048]{1,0:T(8,128)(2,1)S(1)} %get-tuple-element.36), channel_id=1, source_target_pairs={{0,6},{1,7},{2,4},{3,5},{4,2},{5,3},{6,0},{7,1},{8,14},{9,15},{10,... | collective-permute-start | bytes 393224 | tf_op jit(solution)/shard_map/ppermute | solution.py:38
  46.7 7.7 %collective-permute-start.9 = (bf16[32,2048]{1,0:T(8,128)(2,1)S(1)}, bf16[32,2048]{1,0:T(8,128)(2,1)S(1)}, u32[]{:S(2)}, u32[]{:S(2)}) collective-permute-start(bf16[32,2048]{1,0:T(8,128)(2,1)S(1)} %get-tuple-element.37), channel_id=1, source_target_pairs={{0,4},{1,5},{2,6},{3,7},{4,0},{5,1},{6,2},{7,3},{8,12},{9,13},{10,... | collective-permute-start | bytes 393224 | tf_op jit(solution)/shard_map/ppermute | solution.py:38
  47.3 9.2 %collective-permute-start.10 = (bf16[32,2048]{1,0:T(8,128)(2,1)S(1)}, bf16[32,2048]{1,0:T(8,128)(2,1)S(1)}, u32[]{:S(2)}, u32[]{:S(2)}) collective-permute-start(bf16[32,2048]{1,0:T(8,128)(2,1)S(1)} %get-tuple-element.38), channel_id=1, source_target_pairs={{0,2},{1,3},{2,0},{3,1},{4,6},{5,7},{6,4},{7,5},{8,10},{9,11},{10,... | collective-permute-start | bytes 393224 | tf_op jit(solution)/shard_map/ppermute | solution.py:38
  48.0 9.3 %collective-permute-start.12 = (bf16[32,2048]{1,0:T(8,128)(2,1)S(1)}, bf16[32,2048]{1,0:T(8,128)(2,1)S(1)}, u32[]{:S(2)}, u32[]{:S(2)}) collective-permute-start(bf16[32,2048]{1,0:T(8,128)(2,1)S(1)} %get-tuple-element.43), channel_id=1, source_target_pairs={{0,6},{1,7},{2,4},{3,5},{4,2},{5,3},{6,0},{7,1},{8,14},{9,15},{10,... | collective-permute-start | bytes 393224 | tf_op jit(solution)/shard_map/ppermute | solution.py:38
  50.4 8.8 %collective-permute-start.13 = (bf16[32,2048]{1,0:T(8,128)(2,1)S(1)}, bf16[32,2048]{1,0:T(8,128)(2,1)S(1)}, u32[]{:S(2)}, u32[]{:S(2)}) collective-permute-start(bf16[32,2048]{1,0:T(8,128)(2,1)S(1)} %get-tuple-element.44), channel_id=1, source_target_pairs={{0,4},{1,5},{2,6},{3,7},{4,0},{5,1},{6,2},{7,3},{8,12},{9,13},{10,... | collective-permute-start | bytes 393224 | tf_op jit(solution)/shard_map/ppermute | solution.py:38
  51.6 7.6 %collective-permute-start.14 = (bf16[32,2048]{1,0:T(8,128)(2,1)S(1)}, bf16[32,2048]{1,0:T(8,128)(2,1)S(1)}, u32[]{:S(2)}, u32[]{:S(2)}) collective-permute-start(bf16[32,2048]{1,0:T(8,128)(2,1)S(1)} %get-tuple-element.45), channel_id=1, source_target_pairs={{0,2},{1,3},{2,0},{3,1},{4,6},{5,7},{6,4},{7,5},{8,10},{9,11},{10,... | collective-permute-start | bytes 393224 | tf_op jit(solution)/shard_map/ppermute | solution.py:38

commit v5 on v4

--- a/solution.py
+++ b/solution.py
@@ -14,6 +14,7 @@
 EXTRA = 128
 SLOTS = 5
 AHEAD = 5
+BLOCK = 1024
 VMEM_FULL = pl.BlockSpec(memory_space=pltpu.VMEM)
 ANY_FULL = pl.BlockSpec(memory_space=pl.ANY)
 
@@ -219,24 +220,25 @@
     for copy in copies:
         copy.start()
     ready = weight_ref.shape[1]
-    block = 512
 
     def run(ref, skip, first, stop):
+        block = BLOCK if (stop - first) % BLOCK == 0 else 512
+
         def one(i, carry):
-            to = pl.ds(pl.multiple_of(i * block, block), block)
-            at = pl.ds(pl.multiple_of(skip + i * block, block), block)
+            to = pl.ds(pl.multiple_of(first + i * block, 128), block)
+            at = pl.ds(pl.multiple_of(skip + first + i * block, 128), block)
             out = jnp.dot(hidden_ref[...], ref[:, at], preferred_element_type=F32).astype(BF16)
             keep_ref[:, to] = out[:half]
             send_ref[:, to] = out[half:]
             return carry
 
-        lax.fori_loop(first, stop, one, 0)
+        lax.fori_loop(0, (stop - first) // block, one, 0, unroll=not more)
 
     stop = keep_ref.shape[1]
     middle = min(stop, ready - start)
-    run(weight_ref, start, 0, middle // block)
+    run(weight_ref, start, 0, middle)
     if middle < stop:
-        run(rest_ref, start - ready, middle // block, stop // block)
+        run(rest_ref, start - ready, middle, stop)
     for copy in copies:
         copy.wait()
 
@@ -276,20 +278,37 @@
     )(in_vmem(keep), in_vmem(got))
 
 
-def finish_body(chunks, *refs):
+def add_body(left_ref, right_ref, out_ref):
+    out_ref[...] = (left_ref[...].astype(F32) + right_ref[...].astype(F32)).astype(BF16)
+
+
+def add_call(left, right, scoped):
+    return pl.pallas_call(
+        add_body,
+        out_shape=pltpu.VMEM(left.shape, BF16),
+        in_specs=[VMEM_FULL] * 2,
+        out_specs=VMEM_FULL,
+        compiler_params=scoped,
+    )(in_vmem(left), in_vmem(right))
+
+
+def finish_body(counts, *refs):
     ins, out_ref = refs[:-1], refs[-1]
-    count = len(ins) // chunks
-    step = ins[0].shape[1]
-    for j in range(chunks):
-        total = ins[j * count][...].astype(F32)
-        for ref in ins[j * count + 1 : (j + 1) * count]:
+    start = 0
+    for count in counts:
+        terms, ins = ins[:count], ins[count:]
+        stop = start + terms[0].shape[1]
+        total = terms[0][...].astype(F32)
+        for ref in terms[1:]:
             total = total + ref[...].astype(F32)
-        out_ref[:, j * step : (j + 1) * step] = total.astype(BF16)
-
-
-def finish_call(parts, chunks, rows, width, scoped):
-    return pl.pallas_call(
-        functools.partial(finish_body, chunks),
+        out_ref[:, start:stop] = total.astype(BF16)
+        start = stop
+
+
+def finish_call(chunks, rows, width, scoped):
+    parts = [p for chunk in chunks for p in chunk]
+    return pl.pallas_call(
+        functools.partial(finish_body, [len(chunk) for chunk in chunks]),
         out_shape=jax.ShapeDtypeStruct((rows, width), BF16),
         in_specs=[VMEM_FULL] * len(parts),
         out_specs=VMEM_FULL,
@@ -316,13 +335,30 @@
     )
     step = width // 2
     keep_a, send_a, rest = down_call(0, step, mixed_hidden, weight, w_rows, None, scoped)
-    keep_b, send_b = down_call(step, step, mixed_hidden, weight, w_rows, rest, scoped)
-    parts = []
-    for keep, send in ((keep_a, send_a), (keep_b, send_b)):
-        blocks = pair_call(keep, exchange(send, size, 1), rows, scoped)
-        parts += [exchange(b, size, mask) for b, mask in zip(blocks[:0:-1], far[::-1])]
-        parts.append(blocks[0])
-    return finish_call(parts, 2, rows, width, scoped)
+    keep_b, send_b = down_call(step, width - step, mixed_hidden, weight, w_rows, rest, scoped)
+    got_a, got_b = exchange(send_a, size, 1), exchange(send_b, size, 1)
+    blocks_a = pair_call(keep_a, got_a, rows, scoped)
+    blocks_b = pair_call(keep_b, got_b, rows, scoped)
+    if len(blocks_a) != 4:
+        chunks = []
+        for blocks in (blocks_a, blocks_b):
+            sent = [exchange(b, size, mask) for b, mask in zip(blocks[1:], far)]
+            chunks.append([blocks[0], *sent])
+        return finish_call(chunks, rows, width, scoped)
+
+    def over(block, axis):
+        return exchange(block, size, far[axis])
+
+    own_a, first_a, second_a, both_a = blocks_a
+    own_b, first_b, second_b, both_b = blocks_b
+    passed_a = over(both_a, 1)
+    direct_a = over(second_a, 1)
+    passed_b = over(both_b, 0)
+    direct_b = over(first_b, 0)
+    summed_a = over(add_call(first_a, passed_a, scoped), 0)
+    summed_b = over(add_call(second_b, passed_b, scoped), 1)
+    chunks = [[own_a, direct_a, summed_a], [own_b, direct_b, summed_b]]
+    return finish_call(chunks, rows, width, scoped)
 
 
 def solution(mesh):

time: 60.2 us -> 57.3 us (0.952)
  waiting for transfers between devices: 9.89 us -> 6.95 us
  starting transfers between devices: 13.7 us -> 14.6 us
  Pallas kernels: 36.4 us -> 35.5 us
    ppermute x15, waiting for transfers between devices: 9.89 us -> 6.95 us  [exchange(): return lax.ppermute(value, GROUP, [(i, i ^ mask) for i in range(size)])]
    ppermute x15, starting transfers between devices: 13.7 us -> 14.6 us  [exchange(): return lax.ppermute(value, GROUP, [(i, i ^ mask) for i in range(size)])]
    pallas_call x2, Pallas kernels: 8 us -> 7.08 us  [down_call(): pl.pallas_call(functools.partial(down_body, half, start, more), out_shape...]
  transfers between devices with their start and end apart: 15 -> 15, of which waited for: 9 -> 7; matrix products, arithmetic and copies ran while one was open for 0% -> 0% of each run, Pallas kernels for 25% -> 25%
where the time goes in v5:
time: 57.3 us; the launch traced here: 57.2 us
  Pallas kernels  35.5 us (62%)
  starting transfers between devices  14.6 us (25%)
  waiting for transfers between devices  6.95 us (12%)
    pallas_call x1, Pallas kernels, gate_up_call(): pl.pallas_call(functools.partial(gate_up_body, expert_count, count), out_...  15.5 us
    ppermute x15, starting transfers between devices, exchange(): return lax.ppermute(value, GROUP, [(i, i ^ mask) for i in range(size)])  14.6 us
    pallas_call x1, Pallas kernels, fetch_call(): pl.pallas_call(functools.partial(fetch_body, ahead), out_shape=[pltpu.VME...  10.7 us
    pallas_call x2, Pallas kernels, down_call(): pl.pallas_call(functools.partial(down_body, half, start, more), out_shape...  7.08 us
    ppermute x15, waiting for transfers between devices, exchange(): return lax.ppermute(value, GROUP, [(i, i ^ mask) for i in range(size)])  6.95 us
    pallas_call x1, Pallas kernels, norm_call(): pl.pallas_call(functools.partial(norm_body, expert_count), out_shape=pltp...  1.17 us
  transfers between devices with their start and end apart: 15, of which 7 were waited for; matrix products, arithmetic and copies ran while one was open for 0% of the time, Pallas kernels for 25%

profile of v5, /device:TPU:0, one launch (start us, length us, event | category | flops | bytes accessed | tf_op | source)
XLA Modules:
  0.0 57.2 jit_solution(6442483114316276864)
XLA Ops:
  0.0 1.2 %shard_map.73.order_ref.refs_0_ = bf16[32,4224]{1,0:T(8,128)(2,1)S(1)} custom-call(bf16[32,4096]{1,0:T(8,128)(2,1)} %refs_0_.1, f32[1,4096]{1,0:T(1,128)} %bitcast.6, s32[8,32]{1,0:T(8,128)} %bitcast.7, f32[8,32]{1,0:T(8,128)} %bitcast.8), custom_call_target="tpu_custom_call" | custom-call | tf_op jit(solution)/shard_map/pallas_call | solution.py:80
  1.2 4.0 %collective-permute-start.2 = (bf16[32,4224]{1,0:T(8,128)(2,1)S(1)}, bf16[32,4224]{1,0:T(8,128)(2,1)S(1)}, u32[]{:S(2)}, u32[]{:S(2)}) collective-permute-start(bf16[32,4224]{1,0:T(8,128)(2,1)S(1)} %shard_map.73.order_ref.refs_0_), channel_id=1, source_target_pairs={{0,6},{1,7},{2,4},{3,5},{4,2},{5,3},{6,0},{7,1},{8,14},{9,15},{10,... | collective-permute-start | bytes 811016 | tf_op jit(solution)/shard_map/ppermute | solution.py:39
  5.1 0.5 collective-permute-start.1
  5.8 10.7 %shard_map.74 = (bf16[5,4096,384]{2,1,0:T(8,128)(2,1)S(1)}, bf16[5,4096,384]{2,1,0:T(8,128)(2,1)S(1)}, f32[8,128]{1,0:T(8,128)}) custom-call(bf16[32,4224]{1,0:T(8,128)(2,1)S(1)} %shard_map.73.order_ref.refs_0_, bf16[8,4096,384]{2,1,0:T(8,128)(2,1)} %refs_10_.1, bf16[8,4096,384]{2,1,0:T(8,128)(2,1)} %refs_11_.1), custom_call_target="tpu_custom_call" | custom-call | bytes 62914560 | tf_op jit(solution)/shard_map/pallas_call | solution.py:108
  16.5 1.2 %collective-permute-done.1.refs_2_ = bf16[32,4224]{1,0:T(8,128)(2,1)S(1)} collective-permute-done((bf16[32,4224]{1,0:T(8,128)(2,1)S(1)}, bf16[32,4224]{1,0:T(8,128)(2,1)S(1)}, u32[]{:S(2)}, u32[]{:S(2)}) %collective-permute-start.1) | collective-permute-done | bytes 270368 | tf_op jit(solution)/shard_map/ppermute | solution.py:39
  17.7 0.5 collective-permute-start.5
  18.2 1.0 %collective-permute-done.4.refs_5_ = bf16[32,4224]{1,0:T(8,128)(2,1)S(1)} collective-permute-done((bf16[32,4224]{1,0:T(8,128)(2,1)S(1)}, bf16[32,4224]{1,0:T(8,128)(2,1)S(1)}, u32[]{:S(2)}, u32[]{:S(2)}) %collective-permute-start.4) | collective-permute-done | bytes 270368 | tf_op jit(solution)/shard_map/ppermute | solution.py:39
  19.3 0.4 collective-permute-done.5.refs_6_
  19.6 0.4 collective-permute-done.6.refs_7_
  20.0 15.5 %shard_map.75 = (bf16[256,3072]{1,0:T(8,128)(2,1)S(1)}, bf16[3072,3072]{1,0:T(8,128)(2,1)S(1)}, bf16[5,4096,384]{2,1,0:T(8,128)(2,1)S(1)}, bf16[5,4096,384]{2,1,0:T(8,128)(2,1)S(1)}) custom-call(bf16[32,4224]{1,0:T(8,128)(2,1)S(1)} %shard_map.73.order_ref.refs_0_, ...), custom_call_target="tpu_custom_call", output_to_operand_aliasing={{2}: (8, {}), {3}: (9, {})} | custom-call | flops 12884901888 | bytes 75497472 | tf_op jit(solution)/shard_map/pallas_call | solution.py:186
  35.5 3.7 %shard_map.76 = (bf16[128,2048]{1,0:T(8,128)(2,1)S(1)}, bf16[128,2048]{1,0:T(8,128)(2,1)S(1)}, bf16[3072,1024]{1,0:T(8,128)(2,1)S(1)}) custom-call(bf16[256,3072]{1,0:T(8,128)(2,1)S(1)} %get-tuple-element.32.hidden_ref, bf16[3072,3072]{1,0:T(8,128)(2,1)S(1)} %get-tuple-element.33.refs_0_, bf16[3072,4096]{1,0:T(8,128)(2,1)} %bitcast.5), custom_call_target="tpu_custom_call" | custom-call | flops 3221225472 | bytes 12582912 | tf_op jit(solution)/shard_map/pallas_call | solution.py:251
  39.2 0.2 collective-permute-start.7
  39.4 3.4 %shard_map.79 = (bf16[128,2048]{1,0:T(8,128)(2,1)S(1)}, bf16[128,2048]{1,0:T(8,128)(2,1)S(1)}) custom-call(bf16[256,3072]{1,0:T(8,128)(2,1)S(1)} %get-tuple-element.32.hidden_ref, bf16[3072,3072]{1,0:T(8,128)(2,1)S(1)} %get-tuple-element.33.refs_0_, bf16[3072,1024]{1,0:T(8,128)(2,1)S(1)} %get-tuple-element.40.refs_1_), custom_call_target="tpu_custom_call" | custom-call | flops 3221225472 | bytes 12582912 | tf_op jit(solution)/shard_map/pallas_call | solution.py:251
  42.8 0.4 collective-permute-start.11
  43.4 1.6 %collective-permute-start.9 = (bf16[32,2048]{1,0:T(8,128)(2,1)S(1)}, bf16[32,2048]{1,0:T(8,128)(2,1)S(1)}, u32[]{:S(2)}, u32[]{:S(2)}) collective-permute-start(bf16[32,2048]{1,0:T(8,128)(2,1)S(1)} %get-tuple-element.39), channel_id=1, source_target_pairs={{0,4},{1,5},{2,6},{3,7},{4,0},{5,1},{6,2},{7,3},{8,12},{9,13},{10,... | collective-permute-start | bytes 393224 | tf_op jit(solution)/shard_map/ppermute | solution.py:39
  45.1 1.5 %collective-permute-start.13 = (bf16[32,2048]{1,0:T(8,128)(2,1)S(1)}, bf16[32,2048]{1,0:T(8,128)(2,1)S(1)}, u32[]{:S(2)}, u32[]{:S(2)}) collective-permute-start(bf16[32,2048]{1,0:T(8,128)(2,1)S(1)} %get-tuple-element.46), channel_id=1, source_target_pairs={{0,2},{1,3},{2,0},{3,1},{4,6},{5,7},{6,4},{7,5},{8,10},{9,11},{10,... | collective-permute-start | bytes 393224 | tf_op jit(solution)/shard_map/ppermute | solution.py:39
  46.6 1.4 %collective-permute-start.8 = (bf16[32,2048]{1,0:T(8,128)(2,1)S(1)}, bf16[32,2048]{1,0:T(8,128)(2,1)S(1)}, u32[]{:S(2)}, u32[]{:S(2)}) collective-permute-start(bf16[32,2048]{1,0:T(8,128)(2,1)S(1)} %get-tuple-element.37), channel_id=1, source_target_pairs={{0,4},{1,5},{2,6},{3,7},{4,0},{5,1},{6,2},{7,3},{8,12},{9,13},{10,... | collective-permute-start | bytes 393224 | tf_op jit(solution)/shard_map/ppermute | solution.py:39
  47.9 0.6 %collective-permute-start.12 = (bf16[32,2048]{1,0:T(8,128)(2,1)S(1)}, bf16[32,2048]{1,0:T(8,128)(2,1)S(1)}, u32[]{:S(2)}, u32[]{:S(2)}) collective-permute-start(bf16[32,2048]{1,0:T(8,128)(2,1)S(1)} %get-tuple-element.44), channel_id=1, source_target_pairs={{0,2},{1,3},{2,0},{3,1},{4,6},{5,7},{6,4},{7,5},{8,10},{9,11},{10,... | collective-permute-start | bytes 393224 | tf_op jit(solution)/shard_map/ppermute | solution.py:39
  48.5 0.5 collective-permute-done.9.right_ref
  49.0 2.2 %collective-permute-start.10 = (bf16[32,2048]{1,0:T(8,128)(2,1)S(1)}, bf16[32,2048]{1,0:T(8,128)(2,1)S(1)}, u32[]{:S(2)}, u32[]{:S(2)}) collective-permute-start(bf16[32,2048]{1,0:T(8,128)(2,1)S(1)} %shard_map.78), channel_id=1, source_target_pairs={{0,2},{1,3},{2,0},{3,1},{4,6},{5,7},{6,4},{7,5},{8,10},{9,11},{10,... | collective-permute-start | bytes 393224 | tf_op jit(solution)/shard_map/ppermute | solution.py:39
  51.2 1.7 %collective-permute-start.14 = (bf16[32,2048]{1,0:T(8,128)(2,1)S(1)}, bf16[32,2048]{1,0:T(8,128)(2,1)S(1)}, u32[]{:S(2)}, u32[]{:S(2)}) collective-permute-start(bf16[32,2048]{1,0:T(8,128)(2,1)S(1)} %shard_map.81), channel_id=1, source_target_pairs={{0,4},{1,5},{2,6},{3,7},{4,0},{5,1},{6,2},{7,3},{8,12},{9,13},{10,... | collective-permute-start | bytes 393224 | tf_op jit(solution)/shard_map/ppermute | solution.py:39
  52.9 1.4 %collective-permute-done.12.refs_4_ = bf16[32,2048]{1,0:T(8,128)(2,1)S(1)} collective-permute-done((bf16[32,2048]{1,0:T(8,128)(2,1)S(1)}, bf16[32,2048]{1,0:T(8,128)(2,1)S(1)}, u32[]{:S(2)}, u32[]{:S(2)}) %collective-permute-start.12) | collective-permute-done | bytes 131104 | tf_op jit(solution)/shard_map/ppermute | solution.py:39
  54.3 2.1 %collective-permute-done.10.refs_2_ = bf16[32,2048]{1,0:T(8,128)(2,1)S(1)} collective-permute-done((bf16[32,2048]{1,0:T(8,128)(2,1)S(1)}, bf16[32,2048]{1,0:T(8,128)(2,1)S(1)}, u32[]{:S(2)}, u32[]{:S(2)}) %collective-permute-start.10) | collective-permute-done | bytes 131104 | tf_op jit(solution)/shard_map/ppermute | solution.py:39
  56.4 0.8 %shard_map.82 = bf16[32,4096]{1,0:T(8,128)(2,1)} custom-call(bf16[32,2048]{1,0:T(8,128)(2,1)S(1)} %get-tuple-element.36.refs_0_, bf16[32,2048]{1,0:T(8,128)(2,1)S(1)} %collective-permute-done.8.refs_1_, bf16[32,2048]{1,0:T(8,128)(2,1)S(1)} %collective-permute-done.10.refs_2_, bf16[32,2048]{1,0:T(8,128)(2,1)S(1)} %get-tuple-element.43.refs_3_, ...), custom_call_target="tpu_custom_call" | custom-call | tf_op jit(solution)/shard_map/pallas_call | solution.py:310
  (16 shorter events, 0.4 us)
Async XLA Ops:
  1.2 15.3 %collective-permute-start.2 = (bf16[32,4224]{1,0:T(8,128)(2,1)S(1)}, bf16[32,4224]{1,0:T(8,128)(2,1)S(1)}, u32[]{:S(2)}, u32[]{:S(2)}) collective-permute-start(bf16[32,4224]{1,0:T(8,128)(2,1)S(1)} %shard_map.73.order_ref.refs_0_), channel_id=1, source_target_pairs={{0,6},{1,7},{2,4},{3,5},{4,2},{5,3},{6,0},{7,1},{8,14},{9,15},{10,... | collective-permute-start | bytes 811016 | tf_op jit(solution)/shard_map/ppermute | solution.py:39
  5.1 12.6 %collective-permute-start.1 = (bf16[32,4224]{1,0:T(8,128)(2,1)S(1)}, bf16[32,4224]{1,0:T(8,128)(2,1)S(1)}, u32[]{:S(2)}, u32[]{:S(2)}) collective-permute-start(bf16[32,4224]{1,0:T(8,128)(2,1)S(1)} %shard_map.73.order_ref.refs_0_), channel_id=1, source_target_pairs={{0,4},{1,5},{2,6},{3,7},{4,0},{5,1},{6,2},{7,3},{8,12},{9,13},{10,... | collective-permute-start | bytes 811016 | tf_op jit(solution)/shard_map/ppermute | solution.py:39
  5.7 12.0 %collective-permute-start = (bf16[32,4224]{1,0:T(8,128)(2,1)S(1)}, bf16[32,4224]{1,0:T(8,128)(2,1)S(1)}, u32[]{:S(2)}, u32[]{:S(2)}) collective-permute-start(bf16[32,4224]{1,0:T(8,128)(2,1)S(1)} %shard_map.73.order_ref.refs_0_), channel_id=1, source_target_pairs={{0,2},{1,3},{2,0},{3,1},{4,6},{5,7},{6,4},{7,5},{8,10},{9,11},{10,... | collective-permute-start | bytes 811016 | tf_op jit(solution)/shard_map/ppermute | solution.py:39
  5.8 12.4 %collective-permute-start.3 = (bf16[32,4224]{1,0:T(8,128)(2,1)S(1)}, bf16[32,4224]{1,0:T(8,128)(2,1)S(1)}, u32[]{:S(2)}, u32[]{:S(2)}) collective-permute-start(bf16[32,4224]{1,0:T(8,128)(2,1)S(1)} %shard_map.73.order_ref.refs_0_), channel_id=1, source_target_pairs={{0,1},{1,0},{2,3},{3,2},{4,5},{5,4},{6,7},{7,6},{8,9},{9,8},{10,11... | collective-permute-start | bytes 811016 | tf_op jit(solution)/shard_map/ppermute | solution.py:39
  17.7 1.5 %collective-permute-start.4 = (bf16[32,4224]{1,0:T(8,128)(2,1)S(1)}, bf16[32,4224]{1,0:T(8,128)(2,1)S(1)}, u32[]{:S(2)}, u32[]{:S(2)}) collective-permute-start(bf16[32,4224]{1,0:T(8,128)(2,1)S(1)} %collective-permute-done.refs_1_), channel_id=1, source_target_pairs={{0,1},{1,0},{2,3},{3,2},{4,5},{5,4},{6,7},{7,6},{8,9},{9,8},{10,11... | collective-permute-start | bytes 811016 | tf_op jit(solution)/shard_map/ppermute | solution.py:39
  17.7 1.9 %collective-permute-start.5 = (bf16[32,4224]{1,0:T(8,128)(2,1)S(1)}, bf16[32,4224]{1,0:T(8,128)(2,1)S(1)}, u32[]{:S(2)}, u32[]{:S(2)}) collective-permute-start(bf16[32,4224]{1,0:T(8,128)(2,1)S(1)} %collective-permute-done.1.refs_2_), channel_id=1, source_target_pairs={{0,1},{1,0},{2,3},{3,2},{4,5},{5,4},{6,7},{7,6},{8,9},{9,8},{10,11... | collective-permute-start | bytes 811016 | tf_op jit(solution)/shard_map/ppermute | solution.py:39
  18.2 1.8 %collective-permute-start.6 = (bf16[32,4224]{1,0:T(8,128)(2,1)S(1)}, bf16[32,4224]{1,0:T(8,128)(2,1)S(1)}, u32[]{:S(2)}, u32[]{:S(2)}) collective-permute-start(bf16[32,4224]{1,0:T(8,128)(2,1)S(1)} %collective-permute-done.2.refs_3_), channel_id=1, source_target_pairs={{0,1},{1,0},{2,3},{3,2},{4,5},{5,4},{6,7},{7,6},{8,9},{9,8},{10,11... | collective-permute-start | bytes 811016 | tf_op jit(solution)/shard_map/ppermute | solution.py:39
  39.2 4.1 %collective-permute-start.7 = (bf16[128,2048]{1,0:T(8,128)(2,1)S(1)}, bf16[128,2048]{1,0:T(8,128)(2,1)S(1)}, u32[]{:S(2)}, u32[]{:S(2)}) collective-permute-start(bf16[128,2048]{1,0:T(8,128)(2,1)S(1)} %get-tuple-element.35), channel_id=1, source_target_pairs={{0,1},{1,0},{2,3},{3,2},{4,5},{5,4},{6,7},{7,6},{8,9},{9,8},{10,11... | collective-permute-start | bytes 1572872 | tf_op jit(solution)/shard_map/ppermute | solution.py:39
  42.8 2.1 %collective-permute-start.11 = (bf16[128,2048]{1,0:T(8,128)(2,1)S(1)}, bf16[128,2048]{1,0:T(8,128)(2,1)S(1)}, u32[]{:S(2)}, u32[]{:S(2)}) collective-permute-start(bf16[128,2048]{1,0:T(8,128)(2,1)S(1)} %get-tuple-element.42), channel_id=1, source_target_pairs={{0,1},{1,0},{2,3},{3,2},{4,5},{5,4},{6,7},{7,6},{8,9},{9,8},{10,11... | collective-permute-start | bytes 1572872 | tf_op jit(solution)/shard_map/ppermute | solution.py:39
  43.4 5.6 %collective-permute-start.9 = (bf16[32,2048]{1,0:T(8,128)(2,1)S(1)}, bf16[32,2048]{1,0:T(8,128)(2,1)S(1)}, u32[]{:S(2)}, u32[]{:S(2)}) collective-permute-start(bf16[32,2048]{1,0:T(8,128)(2,1)S(1)} %get-tuple-element.39), channel_id=1, source_target_pairs={{0,4},{1,5},{2,6},{3,7},{4,0},{5,1},{6,2},{7,3},{8,12},{9,13},{10,... | collective-permute-start | bytes 393224 | tf_op jit(solution)/shard_map/ppermute | solution.py:39
  45.1 6.1 %collective-permute-start.13 = (bf16[32,2048]{1,0:T(8,128)(2,1)S(1)}, bf16[32,2048]{1,0:T(8,128)(2,1)S(1)}, u32[]{:S(2)}, u32[]{:S(2)}) collective-permute-start(bf16[32,2048]{1,0:T(8,128)(2,1)S(1)} %get-tuple-element.46), channel_id=1, source_target_pairs={{0,2},{1,3},{2,0},{3,1},{4,6},{5,7},{6,4},{7,5},{8,10},{9,11},{10,... | collective-permute-start | bytes 393224 | tf_op jit(solution)/shard_map/ppermute | solution.py:39
  46.6 6.4 %collective-permute-start.8 = (bf16[32,2048]{1,0:T(8,128)(2,1)S(1)}, bf16[32,2048]{1,0:T(8,128)(2,1)S(1)}, u32[]{:S(2)}, u32[]{:S(2)}) collective-permute-start(bf16[32,2048]{1,0:T(8,128)(2,1)S(1)} %get-tuple-element.37), channel_id=1, source_target_pairs={{0,4},{1,5},{2,6},{3,7},{4,0},{5,1},{6,2},{7,3},{8,12},{9,13},{10,... | collective-permute-start | bytes 393224 | tf_op jit(solution)/shard_map/ppermute | solution.py:39
  47.9 6.4 %collective-permute-start.12 = (bf16[32,2048]{1,0:T(8,128)(2,1)S(1)}, bf16[32,2048]{1,0:T(8,128)(2,1)S(1)}, u32[]{:S(2)}, u32[]{:S(2)}) collective-permute-start(bf16[32,2048]{1,0:T(8,128)(2,1)S(1)} %get-tuple-element.44), channel_id=1, source_target_pairs={{0,2},{1,3},{2,0},{3,1},{4,6},{5,7},{6,4},{7,5},{8,10},{9,11},{10,... | collective-permute-start | bytes 393224 | tf_op jit(solution)/shard_map/ppermute | solution.py:39
  49.0 7.4 %collective-permute-start.10 = (bf16[32,2048]{1,0:T(8,128)(2,1)S(1)}, bf16[32,2048]{1,0:T(8,128)(2,1)S(1)}, u32[]{:S(2)}, u32[]{:S(2)}) collective-permute-start(bf16[32,2048]{1,0:T(8,128)(2,1)S(1)} %shard_map.78), channel_id=1, source_target_pairs={{0,2},{1,3},{2,0},{3,1},{4,6},{5,7},{6,4},{7,5},{8,10},{9,11},{10,... | collective-permute-start | bytes 393224 | tf_op jit(solution)/shard_map/ppermute | solution.py:39
  51.2 5.1 %collective-permute-start.14 = (bf16[32,2048]{1,0:T(8,128)(2,1)S(1)}, bf16[32,2048]{1,0:T(8,128)(2,1)S(1)}, u32[]{:S(2)}, u32[]{:S(2)}) collective-permute-start(bf16[32,2048]{1,0:T(8,128)(2,1)S(1)} %shard_map.81), channel_id=1, source_target_pairs={{0,4},{1,5},{2,6},{3,7},{4,0},{5,1},{6,2},{7,3},{8,12},{9,13},{10,... | collective-permute-start | bytes 393224 | tf_op jit(solution)/shard_map/ppermute | solution.py:39

commit v6 on v5

--- a/solution.py
+++ b/solution.py
@@ -12,7 +12,7 @@
 MIB = 2**20
 GROUP = ("exp", "ten")
 EXTRA = 128
-SLOTS = 5
+SLOTS = 6
 AHEAD = 5
 BLOCK = 1024
 VMEM_FULL = pl.BlockSpec(memory_space=pltpu.VMEM)
@@ -88,42 +88,82 @@
     )(*[in_hbm(v) for v in args])
 
 
-def fetch_body(ahead, order_ref, gate_hbm, up_hbm, gate_out, up_out, done_ref, sems):
-    del order_ref
-    copies = []
+def assemble(pieces, rows_ref):
+    at = 0
+    for piece in pieces:
+        rows_ref[at : at + piece.shape[0]] = piece[...]
+        at += piece.shape[0]
+
+
+def hidden_of(rows_ref, first, gate_weight, up_weight, expert, expert_count):
+    width, hidden = gate_weight.shape
+    weights = jnp.concatenate([gate_weight, up_weight], axis=1)
+    both = jnp.dot(rows_ref[first:, :width], weights, preferred_element_type=F32)
+    gate, up = both[:, :hidden], both[:, hidden:]
+    row = lax.broadcasted_iota(jnp.int32, (EXTRA, hidden), 0)
+    pick = jnp.where((row % expert_count == expert) & (row < 3 * expert_count), 1.0, 0.0)
+    mixing = jnp.dot(rows_ref[first:, width:], pick.astype(BF16), preferred_element_type=F32)
+    return (gate / (1.0 + jnp.exp(-gate)) * up * mixing).astype(BF16)
+
+
+def fetch_body(ahead, expert_count, parts, *refs):
+    pieces, refs = refs[:parts], refs[parts:]
+    gate_hbm, up_hbm, gate_ref, up_ref, early_ref, done_ref, rows_ref, sems = refs
+    local, _, hidden = gate_hbm.shape
+
+    def copies(e):
+        return [
+            pltpu.make_async_copy(gate_hbm.at[e], gate_ref.at[e], sems.at[0, e]),
+            pltpu.make_async_copy(up_hbm.at[e], up_ref.at[e], sems.at[1, e]),
+        ]
+
     for e in range(ahead):
-        copies.append(pltpu.make_async_copy(gate_hbm.at[e], gate_out.at[e], sems.at[0, e]))
-        copies.append(pltpu.make_async_copy(up_hbm.at[e], up_out.at[e], sems.at[1, e]))
-    for copy in copies:
-        copy.start()
+        for copy in copies(e):
+            copy.start()
     done_ref[...] = jnp.zeros_like(done_ref)
-    for copy in copies:
-        copy.wait()
-
-
-def fetch_call(order, w_gate, w_up, scoped):
+    assemble(pieces, rows_ref)
+    number = lax.axis_index("exp") * local
+
+    def one(e, carry):
+        for copy in copies(e):
+            copy.wait()
+        at = pl.ds(pl.multiple_of(e * hidden, hidden), hidden)
+        early_ref[:, at] = hidden_of(
+            rows_ref, 0, gate_ref[e], up_ref[e], number + e, expert_count
+        )
+        return carry
+
+    lax.fori_loop(0, ahead, one, 0)
+
+
+def fetch_call(pieces, w_gate, w_up, expert_count, scoped):
     local, width, hidden = w_gate.shape
-    slots = min(SLOTS, local)
-    ahead = min(AHEAD, local)
-    return pl.pallas_call(
-        functools.partial(fetch_body, ahead),
-        out_shape=[pltpu.VMEM((slots, width, hidden), BF16)] * 2 + [pltpu.VMEM((8, 128), F32)],
-        in_specs=[ANY_FULL] * 3,
-        out_specs=[VMEM_FULL] * 3,
-        scratch_shapes=[pltpu.SemaphoreType.DMA((2, slots))],
-        compiler_params=scoped,
-        cost_estimate=cost(0, 8 * slots * width * hidden),
-    )(order, in_hbm(w_gate), in_hbm(w_up))
+    slots, ahead = min(SLOTS, local), min(AHEAD, local)
+    rows = sum(p.shape[0] for p in pieces)
+    return pl.pallas_call(
+        functools.partial(fetch_body, ahead, expert_count, len(pieces)),
+        out_shape=[pltpu.VMEM((slots, width, hidden), BF16)] * 2
+        + [pltpu.VMEM((rows, ahead * hidden), BF16), pltpu.VMEM((8, 128), F32)],
+        in_specs=[VMEM_FULL] * len(pieces) + [ANY_FULL] * 2,
+        out_specs=[VMEM_FULL] * 4,
+        scratch_shapes=[
+            pltpu.VMEM((rows, width + EXTRA), BF16),
+            pltpu.SemaphoreType.DMA((2, ahead)),
+        ],
+        compiler_params=scoped,
+        cost_estimate=cost(0, 8 * ahead * width * hidden),
+    )(*[in_vmem(p) for p in pieces], in_hbm(w_gate), in_hbm(w_up))
 
 
 def gate_up_body(expert_count, parts, *refs):
     pieces, refs = refs[:parts], refs[parts:]
-    gate_hbm, up_hbm, down_hbm = refs[2:5]
-    out_ref, down_ref, gate_ref, up_ref, rows_ref, sems, down_sems = refs[5:]
+    early_ref, gate_hbm, up_hbm, down_hbm = refs[0], *refs[3:6]
+    out_ref, down_ref, gate_ref, up_ref, rows_ref, sems, down_sems = refs[6:]
     slots, width, hidden = gate_ref.shape
     local = gate_hbm.shape[0]
     ahead = min(AHEAD, slots)
     columns = down_ref.shape[1]
+    first, ready = early_ref.shape
 
     def copies(e):
         slot = lax.rem(e, slots)
@@ -141,15 +181,11 @@
             copy.start()
     for e in range(local):
         down_copy(e).start()
-    at = 0
-    for piece in pieces:
-        rows_ref[at : at + piece.shape[0]] = piece[...]
-        at += piece.shape[0]
-
-    row = lax.broadcasted_iota(jnp.int32, (EXTRA, hidden), 0)
+    assemble(pieces, rows_ref)
+    out_ref[:first, :ready] = early_ref[...]
     number = lax.axis_index("exp") * local
 
-    def one(e, carry):
+    def run(skip, e, carry):
         @pl.when((e >= 1) & (e <= local - slots))
         def _():
             for copy in copies(e - 1 + slots):
@@ -161,22 +197,19 @@
                 copy.wait()
 
         slot = lax.rem(e, slots)
-        weights = jnp.concatenate([gate_ref[slot], up_ref[slot]], axis=1)
-        both = jnp.dot(rows_ref[:, :width], weights, preferred_element_type=F32)
-        gate, up = both[:, :hidden], both[:, hidden:]
-        pick = jnp.where((row % expert_count == number + e) & (row < 3 * expert_count), 1.0, 0.0)
-        mixing = jnp.dot(rows_ref[:, width:], pick.astype(BF16), preferred_element_type=F32)
-        value = gate / (1.0 + jnp.exp(-gate)) * up * mixing
         at = pl.ds(pl.multiple_of(e * hidden, hidden), hidden)
-        out_ref[:, at] = value.astype(BF16)
+        out_ref[skip:, at] = hidden_of(
+            rows_ref, skip, gate_ref[slot], up_ref[slot], number + e, expert_count
+        )
         return carry
 
-    lax.fori_loop(0, local, one, 0)
+    lax.fori_loop(0, ready // hidden, functools.partial(run, first), 0)
+    lax.fori_loop(ready // hidden, local, functools.partial(run, 0), 0)
     for e in range(local):
         down_copy(e).wait()
 
 
-def gate_up_call(pieces, gate_slots, up_slots, w_gate, w_up, w_down, expert_count, scoped):
+def gate_up_call(pieces, early, gate_slots, up_slots, w_gate, w_up, w_down, expert_count, scoped):
     slots, width, hidden = gate_slots.shape
     local = w_gate.shape[0]
     depth = w_down.shape[0]
@@ -185,24 +218,24 @@
     shape = pltpu.VMEM(gate_slots.shape, BF16)
     return pl.pallas_call(
         functools.partial(gate_up_body, expert_count, count),
-        out_shape=[pltpu.VMEM((rows, depth), BF16), pltpu.VMEM((depth, 3 * width // 4), BF16), shape, shape],
-        in_specs=[VMEM_FULL] * (count + 2) + [ANY_FULL] * 3,
+        out_shape=[pltpu.VMEM((rows, depth), BF16), pltpu.VMEM((depth, 5 * width // 8), BF16), shape, shape],
+        in_specs=[VMEM_FULL] * (count + 3) + [ANY_FULL] * 3,
         out_specs=[VMEM_FULL] * 4,
         scratch_shapes=[
             pltpu.VMEM((rows, width + EXTRA), BF16),
             pltpu.SemaphoreType.DMA((2, slots)),
             pltpu.SemaphoreType.DMA((local,)),
         ],
-        input_output_aliases={count: 2, count + 1: 3},
+        input_output_aliases={count + 1: 2, count + 2: 3},
         compiler_params=scoped,
         cost_estimate=cost(4 * rows * width * hidden * local, 6 * width * hidden * local),
     )(
-        *[in_vmem(v) for v in (*pieces, gate_slots, up_slots)],
+        *[in_vmem(v) for v in (*pieces, early, gate_slots, up_slots)],
         *[in_hbm(v) for v in (w_gate, w_up, w_down)],
     )[:2]
 
 
-def down_body(half, start, more, hidden_ref, *refs):
+def down_body(order, rows, start, more, hidden_ref, *refs):
     if more:
         weight_ref, down_hbm, keep_ref, send_ref, rest_ref, sems = refs
         parts = sems.shape[0]
@@ -228,8 +261,10 @@
             to = pl.ds(pl.multiple_of(first + i * block, 128), block)
             at = pl.ds(pl.multiple_of(skip + first + i * block, 128), block)
             out = jnp.dot(hidden_ref[...], ref[:, at], preferred_element_type=F32).astype(BF16)
-            keep_ref[:, to] = out[:half]
-            send_ref[:, to] = out[half:]
+            for k, (near, other) in enumerate(order):
+                block_rows = slice(k * rows, (k + 1) * rows)
+                keep_ref[block_rows, to] = out[near * rows : (near + 1) * rows]
+                send_ref[block_rows, to] = out[other * rows : (other + 1) * rows]
             return carry
 
         lax.fori_loop(0, (stop - first) // block, one, 0, unroll=not more)
@@ -243,13 +278,14 @@
         copy.wait()
 
 
-def down_call(start, step, hidden, weight, w_down, rest, scoped):
+def down_call(start, step, hidden, weight, w_down, rest, order, scoped):
     rows, depth = hidden.shape
     half = rows // 2
+    block = half // len(order)
     more = rest is None
     last = w_down.shape[1] - weight.shape[1]
     return pl.pallas_call(
-        functools.partial(down_body, half, start, more),
+        functools.partial(down_body, order, block, start, more),
         out_shape=[pltpu.VMEM((half, step), BF16)] * 2
         + ([pltpu.VMEM((depth, last), BF16)] if more else []),
         in_specs=[VMEM_FULL] * 2 + [ANY_FULL if more else VMEM_FULL],
@@ -327,15 +363,17 @@
     scoped = params(size * rows, width)
 
     own = norm_call(tokens, norm_gain, expert_ids, gate_prob, expert_count, scoped)
-    gate_slots, up_slots, fetched = fetch_call(own, w_gate, w_up, scoped)
-    near = [own] + [after(exchange(own, size, mask), fetched) for mask in far]
-    pieces = near + [exchange(piece, size, 1) for piece in near]
+    ours = [own, exchange(own, size, 1)]
+    *slots, early, fetched = fetch_call(ours, w_gate, w_up, expert_count, scoped)
+    near = [after(exchange(own, size, mask), fetched) for mask in far]
+    pieces = ours + near + [exchange(piece, size, 1) for piece in near]
+    order = [(0, 1)] + [(2 + i, 2 + len(far) + i) for i in range(len(far))]
     mixed_hidden, weight = gate_up_call(
-        pieces, gate_slots, up_slots, w_gate, w_up, w_rows, expert_count, scoped
+        pieces, early, *slots, w_gate, w_up, w_rows, expert_count, scoped
     )
     step = width // 2
-    keep_a, send_a, rest = down_call(0, step, mixed_hidden, weight, w_rows, None, scoped)
-    keep_b, send_b = down_call(step, width - step, mixed_hidden, weight, w_rows, rest, scoped)
+    keep_a, send_a, rest = down_call(0, step, mixed_hidden, weight, w_rows, None, order, scoped)
+    keep_b, send_b = down_call(step, width - step, mixed_hidden, weight, w_rows, rest, order, scoped)
     got_a, got_b = exchange(send_a, size, 1), exchange(send_b, size, 1)
     blocks_a = pair_call(keep_a, got_a, rows, scoped)
     blocks_b = pair_call(keep_b, got_b, rows, scoped)

time: 57.3 us -> 55.9 us (0.976)
  Pallas kernels: 35.5 us -> 34.1 us
    pallas_call x1, Pallas kernels: 15.5 us -> 13.3 us  [gate_up_call(): pl.pallas_call(functools.partial(gate_up_body, expert_count, count), out_...]
    pallas_call x3, Pallas kernels: 17.8 us -> 18.6 us  [the longest x1 11.3 us: fetch_call(): pl.pallas_call(functools.partial(fetch_body, ahead, expert_count, len(pie...]
  transfers between devices with their start and end apart: 15 -> 15, of which waited for: 7 -> 7; matrix products, arithmetic and copies ran while one was open for 0% -> 0% of each run, Pallas kernels for 25% -> 27%
where the time goes in v6:
time: 55.9 us; the launch traced here: 55.8 us
  Pallas kernels  34.1 us (61%)
  starting transfers between devices  14.7 us (26%)
  waiting for transfers between devices  6.93 us (12%)
    ppermute x15, starting transfers between devices, exchange(): return lax.ppermute(value, GROUP, [(i, i ^ mask) for i in range(size)])  14.7 us
    pallas_call x1, Pallas kernels, gate_up_call(): pl.pallas_call(functools.partial(gate_up_body, expert_count, count), out_...  13.3 us
    pallas_call x1, Pallas kernels, fetch_call(): pl.pallas_call(functools.partial(fetch_body, ahead, expert_count, len(pie...  11.3 us
    pallas_call x2, Pallas kernels, down_call(): pl.pallas_call(functools.partial(down_body, order, block, start, more), o...  7.21 us
    ppermute x15, waiting for transfers between devices, exchange(): return lax.ppermute(value, GROUP, [(i, i ^ mask) for i in range(size)])  6.93 us
    pallas_call x1, Pallas kernels, norm_call(): pl.pallas_call(functools.partial(norm_body, expert_count), out_shape=pltp...  1.17 us
  transfers between devices with their start and end apart: 15, of which 7 were waited for; matrix products, arithmetic and copies ran while one was open for 0% of the time, Pallas kernels for 27%

profile of v6, /device:TPU:0, one launch (start us, length us, event | category | flops | bytes accessed | tf_op | source)
XLA Modules:
  0.0 55.8 jit_solution(3539187284406523728)
XLA Ops:
  0.0 1.2 %shard_map.73.refs_0_ = bf16[32,4224]{1,0:T(8,128)(2,1)S(1)} custom-call(bf16[32,4096]{1,0:T(8,128)(2,1)} %refs_0_.1, f32[1,4096]{1,0:T(1,128)} %bitcast.6, s32[8,32]{1,0:T(8,128)} %bitcast.7, f32[8,32]{1,0:T(8,128)} %bitcast.8), custom_call_target="tpu_custom_call" | custom-call | tf_op jit(solution)/shard_map/pallas_call | solution.py:80
  1.2 0.5 collective-permute-start
  1.7 3.5 %collective-permute-start.3 = (bf16[32,4224]{1,0:T(8,128)(2,1)S(1)}, bf16[32,4224]{1,0:T(8,128)(2,1)S(1)}, u32[]{:S(2)}, u32[]{:S(2)}) collective-permute-start(bf16[32,4224]{1,0:T(8,128)(2,1)S(1)} %shard_map.73.refs_0_), channel_id=1, source_target_pairs={{0,6},{1,7},{2,4},{3,5},{4,2},{5,3},{6,0},{7,1},{8,14},{9,15},{10,... | collective-permute-start | bytes 811016 | tf_op jit(solution)/shard_map/ppermute | solution.py:39
  5.2 0.5 collective-permute-start.2
  5.9 11.3 %shard_map.74 = (bf16[6,4096,384]{2,1,0:T(8,128)(2,1)S(1)}, bf16[6,4096,384]{2,1,0:T(8,128)(2,1)S(1)}, bf16[64,1920]{1,0:T(8,128)(2,1)S(1)}, f32[8,128]{1,0:T(8,128)}) custom-call(bf16[32,4224]{1,0:T(8,128)(2,1)S(1)} %shard_map.73.refs_0_, bf16[32,4224]{1,0:T(8,128)(2,1)S(1)} %collective-permute-done.refs_1_, bf16[8,4096,384]{2,1,0:T(8,128)(2,1)} %refs_11_.1, ...), custom_call_target="tpu_custom_call" | custom-call | bytes 62914560 | tf_op jit(solution)/shard_map/pallas_call | solution.py:143
  17.2 1.2 %collective-permute-done.2.refs_3_ = bf16[32,4224]{1,0:T(8,128)(2,1)S(1)} collective-permute-done((bf16[32,4224]{1,0:T(8,128)(2,1)S(1)}, bf16[32,4224]{1,0:T(8,128)(2,1)S(1)}, u32[]{:S(2)}, u32[]{:S(2)}) %collective-permute-start.2) | collective-permute-done | bytes 270368 | tf_op jit(solution)/shard_map/ppermute | solution.py:39
  18.4 0.5 collective-permute-start.5
  18.9 1.0 %collective-permute-done.4.refs_5_ = bf16[32,4224]{1,0:T(8,128)(2,1)S(1)} collective-permute-done((bf16[32,4224]{1,0:T(8,128)(2,1)S(1)}, bf16[32,4224]{1,0:T(8,128)(2,1)S(1)}, u32[]{:S(2)}, u32[]{:S(2)}) %collective-permute-start.4) | collective-permute-done | bytes 270368 | tf_op jit(solution)/shard_map/ppermute | solution.py:39
  20.0 0.4 collective-permute-done.5.refs_6_
  20.3 0.4 collective-permute-done.6.refs_7_
  20.7 13.3 %shard_map.75 = (bf16[256,3072]{1,0:T(8,128)(2,1)S(1)}, bf16[3072,2560]{1,0:T(8,128)(2,1)S(1)}, bf16[6,4096,384]{2,1,0:T(8,128)(2,1)S(1)}, bf16[6,4096,384]{2,1,0:T(8,128)(2,1)S(1)}) custom-call(bf16[32,4224]{1,0:T(8,128)(2,1)S(1)} %shard_map.73.refs_0_, ...), custom_call_target="tpu_custom_call", output_to_operand_aliasing={{2}: (9, {}), {3}: (10, {})} | custom-call | flops 12884901888 | bytes 75497472 | tf_op jit(solution)/shard_map/pallas_call | solution.py:219
  34.0 3.8 %shard_map.76 = (bf16[128,2048]{1,0:T(8,128)(2,1)S(1)}, bf16[128,2048]{1,0:T(8,128)(2,1)S(1)}, bf16[3072,1536]{1,0:T(8,128)(2,1)S(1)}) custom-call(bf16[256,3072]{1,0:T(8,128)(2,1)S(1)} %get-tuple-element.34.hidden_ref, bf16[3072,2560]{1,0:T(8,128)(2,1)S(1)} %get-tuple-element.35.refs_0_, bf16[3072,4096]{1,0:T(8,128)(2,1)} %bitcast.5), custom_call_target="tpu_custom_call" | custom-call | flops 3221225472 | bytes 12582912 | tf_op jit(solution)/shard_map/pallas_call | solution.py:287
  38.0 3.4 %shard_map.79 = (bf16[128,2048]{1,0:T(8,128)(2,1)S(1)}, bf16[128,2048]{1,0:T(8,128)(2,1)S(1)}) custom-call(bf16[256,3072]{1,0:T(8,128)(2,1)S(1)} %get-tuple-element.34.hidden_ref, bf16[3072,2560]{1,0:T(8,128)(2,1)S(1)} %get-tuple-element.35.refs_0_, bf16[3072,1536]{1,0:T(8,128)(2,1)S(1)} %get-tuple-element.42.refs_1_), custom_call_target="tpu_custom_call" | custom-call | flops 3221225472 | bytes 12582912 | tf_op jit(solution)/shard_map/pallas_call | solution.py:287
  41.4 0.4 collective-permute-start.11
  42.0 1.6 %collective-permute-start.9 = (bf16[32,2048]{1,0:T(8,128)(2,1)S(1)}, bf16[32,2048]{1,0:T(8,128)(2,1)S(1)}, u32[]{:S(2)}, u32[]{:S(2)}) collective-permute-start(bf16[32,2048]{1,0:T(8,128)(2,1)S(1)} %get-tuple-element.41), channel_id=1, source_target_pairs={{0,4},{1,5},{2,6},{3,7},{4,0},{5,1},{6,2},{7,3},{8,12},{9,13},{10,... | collective-permute-start | bytes 393224 | tf_op jit(solution)/shard_map/ppermute | solution.py:39
  43.7 1.5 %collective-permute-start.13 = (bf16[32,2048]{1,0:T(8,128)(2,1)S(1)}, bf16[32,2048]{1,0:T(8,128)(2,1)S(1)}, u32[]{:S(2)}, u32[]{:S(2)}) collective-permute-start(bf16[32,2048]{1,0:T(8,128)(2,1)S(1)} %get-tuple-element.48), channel_id=1, source_target_pairs={{0,2},{1,3},{2,0},{3,1},{4,6},{5,7},{6,4},{7,5},{8,10},{9,11},{10,... | collective-permute-start | bytes 393224 | tf_op jit(solution)/shard_map/ppermute | solution.py:39
  45.1 1.4 %collective-permute-start.8 = (bf16[32,2048]{1,0:T(8,128)(2,1)S(1)}, bf16[32,2048]{1,0:T(8,128)(2,1)S(1)}, u32[]{:S(2)}, u32[]{:S(2)}) collective-permute-start(bf16[32,2048]{1,0:T(8,128)(2,1)S(1)} %get-tuple-element.39), channel_id=1, source_target_pairs={{0,4},{1,5},{2,6},{3,7},{4,0},{5,1},{6,2},{7,3},{8,12},{9,13},{10,... | collective-permute-start | bytes 393224 | tf_op jit(solution)/shard_map/ppermute | solution.py:39
  46.5 0.6 %collective-permute-start.12 = (bf16[32,2048]{1,0:T(8,128)(2,1)S(1)}, bf16[32,2048]{1,0:T(8,128)(2,1)S(1)}, u32[]{:S(2)}, u32[]{:S(2)}) collective-permute-start(bf16[32,2048]{1,0:T(8,128)(2,1)S(1)} %get-tuple-element.46), channel_id=1, source_target_pairs={{0,2},{1,3},{2,0},{3,1},{4,6},{5,7},{6,4},{7,5},{8,10},{9,11},{10,... | collective-permute-start | bytes 393224 | tf_op jit(solution)/shard_map/ppermute | solution.py:39
  47.1 0.5 collective-permute-done.9.right_ref
  47.6 2.1 %collective-permute-start.10 = (bf16[32,2048]{1,0:T(8,128)(2,1)S(1)}, bf16[32,2048]{1,0:T(8,128)(2,1)S(1)}, u32[]{:S(2)}, u32[]{:S(2)}) collective-permute-start(bf16[32,2048]{1,0:T(8,128)(2,1)S(1)} %shard_map.78), channel_id=1, source_target_pairs={{0,2},{1,3},{2,0},{3,1},{4,6},{5,7},{6,4},{7,5},{8,10},{9,11},{10,... | collective-permute-start | bytes 393224 | tf_op jit(solution)/shard_map/ppermute | solution.py:39
  49.8 1.7 %collective-permute-start.14 = (bf16[32,2048]{1,0:T(8,128)(2,1)S(1)}, bf16[32,2048]{1,0:T(8,128)(2,1)S(1)}, u32[]{:S(2)}, u32[]{:S(2)}) collective-permute-start(bf16[32,2048]{1,0:T(8,128)(2,1)S(1)} %shard_map.81), channel_id=1, source_target_pairs={{0,4},{1,5},{2,6},{3,7},{4,0},{5,1},{6,2},{7,3},{8,12},{9,13},{10,... | collective-permute-start | bytes 393224 | tf_op jit(solution)/shard_map/ppermute | solution.py:39
  51.5 1.4 %collective-permute-done.12.refs_4_ = bf16[32,2048]{1,0:T(8,128)(2,1)S(1)} collective-permute-done((bf16[32,2048]{1,0:T(8,128)(2,1)S(1)}, bf16[32,2048]{1,0:T(8,128)(2,1)S(1)}, u32[]{:S(2)}, u32[]{:S(2)}) %collective-permute-start.12) | collective-permute-done | bytes 131104 | tf_op jit(solution)/shard_map/ppermute | solution.py:39
  52.9 2.1 %collective-permute-done.10.refs_2_ = bf16[32,2048]{1,0:T(8,128)(2,1)S(1)} collective-permute-done((bf16[32,2048]{1,0:T(8,128)(2,1)S(1)}, bf16[32,2048]{1,0:T(8,128)(2,1)S(1)}, u32[]{:S(2)}, u32[]{:S(2)}) %collective-permute-start.10) | collective-permute-done | bytes 131104 | tf_op jit(solution)/shard_map/ppermute | solution.py:39
  55.0 0.8 %shard_map.82 = bf16[32,4096]{1,0:T(8,128)(2,1)} custom-call(bf16[32,2048]{1,0:T(8,128)(2,1)S(1)} %get-tuple-element.38.refs_0_, bf16[32,2048]{1,0:T(8,128)(2,1)S(1)} %collective-permute-done.8.refs_1_, bf16[32,2048]{1,0:T(8,128)(2,1)S(1)} %collective-permute-done.10.refs_2_, bf16[32,2048]{1,0:T(8,128)(2,1)S(1)} %get-tuple-element.45.refs_3_, ...), custom_call_target="tpu_custom_call" | custom-call | tf_op jit(solution)/shard_map/pallas_call | solution.py:346
  (16 shorter events, 0.6 us)
Async XLA Ops:
  1.2 4.7 %collective-permute-start = (bf16[32,4224]{1,0:T(8,128)(2,1)S(1)}, bf16[32,4224]{1,0:T(8,128)(2,1)S(1)}, u32[]{:S(2)}, u32[]{:S(2)}) collective-permute-start(bf16[32,4224]{1,0:T(8,128)(2,1)S(1)} %shard_map.73.refs_0_), channel_id=1, source_target_pairs={{0,1},{1,0},{2,3},{3,2},{4,5},{5,4},{6,7},{7,6},{8,9},{9,8},{10,11... | collective-permute-start | bytes 811016 | tf_op jit(solution)/shard_map/ppermute | solution.py:39
  1.7 15.5 %collective-permute-start.3 = (bf16[32,4224]{1,0:T(8,128)(2,1)S(1)}, bf16[32,4224]{1,0:T(8,128)(2,1)S(1)}, u32[]{:S(2)}, u32[]{:S(2)}) collective-permute-start(bf16[32,4224]{1,0:T(8,128)(2,1)S(1)} %shard_map.73.refs_0_), channel_id=1, source_target_pairs={{0,6},{1,7},{2,4},{3,5},{4,2},{5,3},{6,0},{7,1},{8,14},{9,15},{10,... | collective-permute-start | bytes 811016 | tf_op jit(solution)/shard_map/ppermute | solution.py:39
  5.2 13.2 %collective-permute-start.2 = (bf16[32,4224]{1,0:T(8,128)(2,1)S(1)}, bf16[32,4224]{1,0:T(8,128)(2,1)S(1)}, u32[]{:S(2)}, u32[]{:S(2)}) collective-permute-start(bf16[32,4224]{1,0:T(8,128)(2,1)S(1)} %shard_map.73.refs_0_), channel_id=1, source_target_pairs={{0,4},{1,5},{2,6},{3,7},{4,0},{5,1},{6,2},{7,3},{8,12},{9,13},{10,... | collective-permute-start | bytes 811016 | tf_op jit(solution)/shard_map/ppermute | solution.py:39
  5.8 12.6 %collective-permute-start.1 = (bf16[32,4224]{1,0:T(8,128)(2,1)S(1)}, bf16[32,4224]{1,0:T(8,128)(2,1)S(1)}, u32[]{:S(2)}, u32[]{:S(2)}) collective-permute-start(bf16[32,4224]{1,0:T(8,128)(2,1)S(1)} %shard_map.73.refs_0_), channel_id=1, source_target_pairs={{0,2},{1,3},{2,0},{3,1},{4,6},{5,7},{6,4},{7,5},{8,10},{9,11},{10,... | collective-permute-start | bytes 811016 | tf_op jit(solution)/shard_map/ppermute | solution.py:39
  18.4 1.5 %collective-permute-start.4 = (bf16[32,4224]{1,0:T(8,128)(2,1)S(1)}, bf16[32,4224]{1,0:T(8,128)(2,1)S(1)}, u32[]{:S(2)}, u32[]{:S(2)}) collective-permute-start(bf16[32,4224]{1,0:T(8,128)(2,1)S(1)} %collective-permute-done.1.refs_2_), channel_id=1, source_target_pairs={{0,1},{1,0},{2,3},{3,2},{4,5},{5,4},{6,7},{7,6},{8,9},{9,8},{10,11... | collective-permute-start | bytes 811016 | tf_op jit(solution)/shard_map/ppermute | solution.py:39
  18.4 1.9 %collective-permute-start.5 = (bf16[32,4224]{1,0:T(8,128)(2,1)S(1)}, bf16[32,4224]{1,0:T(8,128)(2,1)S(1)}, u32[]{:S(2)}, u32[]{:S(2)}) collective-permute-start(bf16[32,4224]{1,0:T(8,128)(2,1)S(1)} %collective-permute-done.2.refs_3_), channel_id=1, source_target_pairs={{0,1},{1,0},{2,3},{3,2},{4,5},{5,4},{6,7},{7,6},{8,9},{9,8},{10,11... | collective-permute-start | bytes 811016 | tf_op jit(solution)/shard_map/ppermute | solution.py:39
  18.9 1.8 %collective-permute-start.6 = (bf16[32,4224]{1,0:T(8,128)(2,1)S(1)}, bf16[32,4224]{1,0:T(8,128)(2,1)S(1)}, u32[]{:S(2)}, u32[]{:S(2)}) collective-permute-start(bf16[32,4224]{1,0:T(8,128)(2,1)S(1)} %collective-permute-done.3.refs_4_), channel_id=1, source_target_pairs={{0,1},{1,0},{2,3},{3,2},{4,5},{5,4},{6,7},{7,6},{8,9},{9,8},{10,11... | collective-permute-start | bytes 811016 | tf_op jit(solution)/shard_map/ppermute | solution.py:39
  37.8 4.1 %collective-permute-start.7 = (bf16[128,2048]{1,0:T(8,128)(2,1)S(1)}, bf16[128,2048]{1,0:T(8,128)(2,1)S(1)}, u32[]{:S(2)}, u32[]{:S(2)}) collective-permute-start(bf16[128,2048]{1,0:T(8,128)(2,1)S(1)} %get-tuple-element.37), channel_id=1, source_target_pairs={{0,1},{1,0},{2,3},{3,2},{4,5},{5,4},{6,7},{7,6},{8,9},{9,8},{10,11... | collective-permute-start | bytes 1572872 | tf_op jit(solution)/shard_map/ppermute | solution.py:39
  41.4 2.1 %collective-permute-start.11 = (bf16[128,2048]{1,0:T(8,128)(2,1)S(1)}, bf16[128,2048]{1,0:T(8,128)(2,1)S(1)}, u32[]{:S(2)}, u32[]{:S(2)}) collective-permute-start(bf16[128,2048]{1,0:T(8,128)(2,1)S(1)} %get-tuple-element.44), channel_id=1, source_target_pairs={{0,1},{1,0},{2,3},{3,2},{4,5},{5,4},{6,7},{7,6},{8,9},{9,8},{10,11... | collective-permute-start | bytes 1572872 | tf_op jit(solution)/shard_map/ppermute | solution.py:39
  42.0 5.6 %collective-permute-start.9 = (bf16[32,2048]{1,0:T(8,128)(2,1)S(1)}, bf16[32,2048]{1,0:T(8,128)(2,1)S(1)}, u32[]{:S(2)}, u32[]{:S(2)}) collective-permute-start(bf16[32,2048]{1,0:T(8,128)(2,1)S(1)} %get-tuple-element.41), channel_id=1, source_target_pairs={{0,4},{1,5},{2,6},{3,7},{4,0},{5,1},{6,2},{7,3},{8,12},{9,13},{10,... | collective-permute-start | bytes 393224 | tf_op jit(solution)/shard_map/ppermute | solution.py:39
  43.7 6.1 %collective-permute-start.13 = (bf16[32,2048]{1,0:T(8,128)(2,1)S(1)}, bf16[32,2048]{1,0:T(8,128)(2,1)S(1)}, u32[]{:S(2)}, u32[]{:S(2)}) collective-permute-start(bf16[32,2048]{1,0:T(8,128)(2,1)S(1)} %get-tuple-element.48), channel_id=1, source_target_pairs={{0,2},{1,3},{2,0},{3,1},{4,6},{5,7},{6,4},{7,5},{8,10},{9,11},{10,... | collective-permute-start | bytes 393224 | tf_op jit(solution)/shard_map/ppermute | solution.py:39
  45.1 6.4 %collective-permute-start.8 = (bf16[32,2048]{1,0:T(8,128)(2,1)S(1)}, bf16[32,2048]{1,0:T(8,128)(2,1)S(1)}, u32[]{:S(2)}, u32[]{:S(2)}) collective-permute-start(bf16[32,2048]{1,0:T(8,128)(2,1)S(1)} %get-tuple-element.39), channel_id=1, source_target_pairs={{0,4},{1,5},{2,6},{3,7},{4,0},{5,1},{6,2},{7,3},{8,12},{9,13},{10,... | collective-permute-start | bytes 393224 | tf_op jit(solution)/shard_map/ppermute | solution.py:39
  46.5 6.4 %collective-permute-start.12 = (bf16[32,2048]{1,0:T(8,128)(2,1)S(1)}, bf16[32,2048]{1,0:T(8,128)(2,1)S(1)}, u32[]{:S(2)}, u32[]{:S(2)}) collective-permute-start(bf16[32,2048]{1,0:T(8,128)(2,1)S(1)} %get-tuple-element.46), channel_id=1, source_target_pairs={{0,2},{1,3},{2,0},{3,1},{4,6},{5,7},{6,4},{7,5},{8,10},{9,11},{10,... | collective-permute-start | bytes 393224 | tf_op jit(solution)/shard_map/ppermute | solution.py:39
  47.6 7.4 %collective-permute-start.10 = (bf16[32,2048]{1,0:T(8,128)(2,1)S(1)}, bf16[32,2048]{1,0:T(8,128)(2,1)S(1)}, u32[]{:S(2)}, u32[]{:S(2)}) collective-permute-start(bf16[32,2048]{1,0:T(8,128)(2,1)S(1)} %shard_map.78), channel_id=1, source_target_pairs={{0,2},{1,3},{2,0},{3,1},{4,6},{5,7},{6,4},{7,5},{8,10},{9,11},{10,... | collective-permute-start | bytes 393224 | tf_op jit(solution)/shard_map/ppermute | solution.py:39
  49.8 5.2 %collective-permute-start.14 = (bf16[32,2048]{1,0:T(8,128)(2,1)S(1)}, bf16[32,2048]{1,0:T(8,128)(2,1)S(1)}, u32[]{:S(2)}, u32[]{:S(2)}) collective-permute-start(bf16[32,2048]{1,0:T(8,128)(2,1)S(1)} %shard_map.81), channel_id=1, source_target_pairs={{0,4},{1,5},{2,6},{3,7},{4,0},{5,1},{6,2},{7,3},{8,12},{9,13},{10,... | collective-permute-start | bytes 393224 | tf_op jit(solution)/shard_map/ppermute | solution.py:39

commit v7 on v6

--- a/solution.py
+++ b/solution.py
@@ -179,8 +179,6 @@
     for e in range(ahead, slots):
         for copy in copies(e):
             copy.start()
-    for e in range(local):
-        down_copy(e).start()
     assemble(pieces, rows_ref)
     out_ref[:first, :ready] = early_ref[...]
     number = lax.axis_index("exp") * local
@@ -190,6 +188,11 @@
         def _():
             for copy in copies(e - 1 + slots):
                 copy.start()
+
+        @pl.when(e == local - slots)
+        def _():
+            for k in range(local):
+                down_copy(k).start()
 
         @pl.when(e >= ahead)
         def _():
@@ -315,13 +318,14 @@
 
 
 def add_body(left_ref, right_ref, out_ref):
-    out_ref[...] = (left_ref[...].astype(F32) + right_ref[...].astype(F32)).astype(BF16)
-
-
-def add_call(left, right, scoped):
+    total = left_ref[...].astype(F32) + right_ref[...].astype(F32)
+    out_ref[...] = total.astype(out_ref.dtype)
+
+
+def add_call(left, right, scoped, kind=BF16):
     return pl.pallas_call(
         add_body,
-        out_shape=pltpu.VMEM(left.shape, BF16),
+        out_shape=pltpu.VMEM(left.shape, kind),
         in_specs=[VMEM_FULL] * 2,
         out_specs=VMEM_FULL,
         compiler_params=scoped,
@@ -395,7 +399,10 @@
     direct_b = over(first_b, 0)
     summed_a = over(add_call(first_a, passed_a, scoped), 0)
     summed_b = over(add_call(second_b, passed_b, scoped), 1)
-    chunks = [[own_a, direct_a, summed_a], [own_b, direct_b, summed_b]]
+    chunks = [
+        [add_call(own_a, direct_a, scoped, F32), summed_a],
+        [add_call(own_b, direct_b, scoped, F32), summed_b],
+    ]
     return finish_call(chunks, rows, width, scoped)
 
 

time: 55.9 us -> 55.8 us (level)
  no operation moved by 1% of the time
where the time goes in v7:
time: 55.8 us; the launch traced here: 55.7 us
  Pallas kernels  34.1 us (61%)
  starting transfers between devices  14.7 us (26%)
  waiting for transfers between devices  6.87 us (12%)
    ppermute x15, starting transfers between devices, exchange(): return lax.ppermute(value, GROUP, [(i, i ^ mask) for i in range(size)])  14.7 us
    pallas_call x1, Pallas kernels, gate_up_call(): pl.pallas_call(functools.partial(gate_up_body, expert_count, count), out_...  13.2 us
    pallas_call x1, Pallas kernels, fetch_call(): pl.pallas_call(functools.partial(fetch_body, ahead, expert_count, len(pie...  11.3 us
    pallas_call x2, Pallas kernels, down_call(): pl.pallas_call(functools.partial(down_body, order, block, start, more), o...  7.21 us
    ppermute x15, waiting for transfers between devices, exchange(): return lax.ppermute(value, GROUP, [(i, i ^ mask) for i in range(size)])  6.87 us
    pallas_call x1, Pallas kernels, norm_call(): pl.pallas_call(functools.partial(norm_body, expert_count), out_shape=pltp...  1.17 us
  transfers between devices with their start and end apart: 15, of which 7 were waited for; matrix products, arithmetic and copies ran while one was open for 0% of the time, Pallas kernels for 27%

profile of v7, /device:TPU:0, one launch (start us, length us, event | category | flops | bytes accessed | tf_op | source)
XLA Modules:
  0.0 55.7 jit_solution(10986635942566825320)
XLA Ops:
  0.0 1.2 %shard_map.73.refs_0_ = bf16[32,4224]{1,0:T(8,128)(2,1)S(1)} custom-call(bf16[32,4096]{1,0:T(8,128)(2,1)} %refs_0_.1, f32[1,4096]{1,0:T(1,128)} %bitcast.6, s32[8,32]{1,0:T(8,128)} %bitcast.7, f32[8,32]{1,0:T(8,128)} %bitcast.8), custom_call_target="tpu_custom_call" | custom-call | tf_op jit(solution)/shard_map/pallas_call | solution.py:80
  1.2 0.5 collective-permute-start
  1.7 3.5 %collective-permute-start.3 = (bf16[32,4224]{1,0:T(8,128)(2,1)S(1)}, bf16[32,4224]{1,0:T(8,128)(2,1)S(1)}, u32[]{:S(2)}, u32[]{:S(2)}) collective-permute-start(bf16[32,4224]{1,0:T(8,128)(2,1)S(1)} %shard_map.73.refs_0_), channel_id=1, source_target_pairs={{0,6},{1,7},{2,4},{3,5},{4,2},{5,3},{6,0},{7,1},{8,14},{9,15},{10,... | collective-permute-start | bytes 811016 | tf_op jit(solution)/shard_map/ppermute | solution.py:39
  5.2 0.5 collective-permute-start.2
  5.9 11.3 %shard_map.74 = (bf16[6,4096,384]{2,1,0:T(8,128)(2,1)S(1)}, bf16[6,4096,384]{2,1,0:T(8,128)(2,1)S(1)}, bf16[64,1920]{1,0:T(8,128)(2,1)S(1)}, f32[8,128]{1,0:T(8,128)}) custom-call(bf16[32,4224]{1,0:T(8,128)(2,1)S(1)} %shard_map.73.refs_0_, bf16[32,4224]{1,0:T(8,128)(2,1)S(1)} %collective-permute-done.refs_1_, bf16[8,4096,384]{2,1,0:T(8,128)(2,1)} %refs_11_.1, ...), custom_call_target="tpu_custom_call" | custom-call | bytes 62914560 | tf_op jit(solution)/shard_map/pallas_call | solution.py:143
  17.2 1.2 %collective-permute-done.2.refs_3_ = bf16[32,4224]{1,0:T(8,128)(2,1)S(1)} collective-permute-done((bf16[32,4224]{1,0:T(8,128)(2,1)S(1)}, bf16[32,4224]{1,0:T(8,128)(2,1)S(1)}, u32[]{:S(2)}, u32[]{:S(2)}) %collective-permute-start.2) | collective-permute-done | bytes 270368 | tf_op jit(solution)/shard_map/ppermute | solution.py:39
  18.4 0.5 collective-permute-start.5
  18.9 1.0 %collective-permute-done.4.refs_5_ = bf16[32,4224]{1,0:T(8,128)(2,1)S(1)} collective-permute-done((bf16[32,4224]{1,0:T(8,128)(2,1)S(1)}, bf16[32,4224]{1,0:T(8,128)(2,1)S(1)}, u32[]{:S(2)}, u32[]{:S(2)}) %collective-permute-start.4) | collective-permute-done | bytes 270368 | tf_op jit(solution)/shard_map/ppermute | solution.py:39
  20.0 0.4 collective-permute-done.5.refs_6_
  20.3 0.4 collective-permute-done.6.refs_7_
  20.7 13.2 %shard_map.75 = (bf16[256,3072]{1,0:T(8,128)(2,1)S(1)}, bf16[3072,2560]{1,0:T(8,128)(2,1)S(1)}, bf16[6,4096,384]{2,1,0:T(8,128)(2,1)S(1)}, bf16[6,4096,384]{2,1,0:T(8,128)(2,1)S(1)}) custom-call(bf16[32,4224]{1,0:T(8,128)(2,1)S(1)} %shard_map.73.refs_0_, ...), custom_call_target="tpu_custom_call", output_to_operand_aliasing={{2}: (9, {}), {3}: (10, {})} | custom-call | flops 12884901888 | bytes 75497472 | tf_op jit(solution)/shard_map/pallas_call | solution.py:222
  34.0 3.8 %shard_map.76 = (bf16[128,2048]{1,0:T(8,128)(2,1)S(1)}, bf16[128,2048]{1,0:T(8,128)(2,1)S(1)}, bf16[3072,1536]{1,0:T(8,128)(2,1)S(1)}) custom-call(bf16[256,3072]{1,0:T(8,128)(2,1)S(1)} %get-tuple-element.34.hidden_ref, bf16[3072,2560]{1,0:T(8,128)(2,1)S(1)} %get-tuple-element.35.refs_0_, bf16[3072,4096]{1,0:T(8,128)(2,1)} %bitcast.5), custom_call_target="tpu_custom_call" | custom-call | flops 3221225472 | bytes 12582912 | tf_op jit(solution)/shard_map/pallas_call | solution.py:290
  38.0 3.4 %shard_map.80 = (bf16[128,2048]{1,0:T(8,128)(2,1)S(1)}, bf16[128,2048]{1,0:T(8,128)(2,1)S(1)}) custom-call(bf16[256,3072]{1,0:T(8,128)(2,1)S(1)} %get-tuple-element.34.hidden_ref, bf16[3072,2560]{1,0:T(8,128)(2,1)S(1)} %get-tuple-element.35.refs_0_, bf16[3072,1536]{1,0:T(8,128)(2,1)S(1)} %get-tuple-element.42.refs_1_), custom_call_target="tpu_custom_call" | custom-call | flops 3221225472 | bytes 12582912 | tf_op jit(solution)/shard_map/pallas_call | solution.py:290
  41.4 0.4 collective-permute-start.11
  42.0 1.6 %collective-permute-start.9 = (bf16[32,2048]{1,0:T(8,128)(2,1)S(1)}, bf16[32,2048]{1,0:T(8,128)(2,1)S(1)}, u32[]{:S(2)}, u32[]{:S(2)}) collective-permute-start(bf16[32,2048]{1,0:T(8,128)(2,1)S(1)} %get-tuple-element.41), channel_id=1, source_target_pairs={{0,4},{1,5},{2,6},{3,7},{4,0},{5,1},{6,2},{7,3},{8,12},{9,13},{10,... | collective-permute-start | bytes 393224 | tf_op jit(solution)/shard_map/ppermute | solution.py:39
  43.6 1.5 %collective-permute-start.13 = (bf16[32,2048]{1,0:T(8,128)(2,1)S(1)}, bf16[32,2048]{1,0:T(8,128)(2,1)S(1)}, u32[]{:S(2)}, u32[]{:S(2)}) collective-permute-start(bf16[32,2048]{1,0:T(8,128)(2,1)S(1)} %get-tuple-element.48), channel_id=1, source_target_pairs={{0,2},{1,3},{2,0},{3,1},{4,6},{5,7},{6,4},{7,5},{8,10},{9,11},{10,... | collective-permute-start | bytes 393224 | tf_op jit(solution)/shard_map/ppermute | solution.py:39
  45.1 1.4 %collective-permute-start.8 = (bf16[32,2048]{1,0:T(8,128)(2,1)S(1)}, bf16[32,2048]{1,0:T(8,128)(2,1)S(1)}, u32[]{:S(2)}, u32[]{:S(2)}) collective-permute-start(bf16[32,2048]{1,0:T(8,128)(2,1)S(1)} %get-tuple-element.39), channel_id=1, source_target_pairs={{0,4},{1,5},{2,6},{3,7},{4,0},{5,1},{6,2},{7,3},{8,12},{9,13},{10,... | collective-permute-start | bytes 393224 | tf_op jit(solution)/shard_map/ppermute | solution.py:39
  46.5 0.6 %collective-permute-start.12 = (bf16[32,2048]{1,0:T(8,128)(2,1)S(1)}, bf16[32,2048]{1,0:T(8,128)(2,1)S(1)}, u32[]{:S(2)}, u32[]{:S(2)}) collective-permute-start(bf16[32,2048]{1,0:T(8,128)(2,1)S(1)} %get-tuple-element.46), channel_id=1, source_target_pairs={{0,2},{1,3},{2,0},{3,1},{4,6},{5,7},{6,4},{7,5},{8,10},{9,11},{10,... | collective-permute-start | bytes 393224 | tf_op jit(solution)/shard_map/ppermute | solution.py:39
  47.1 0.5 collective-permute-done.9.right_ref
  47.6 2.2 %collective-permute-start.10 = (bf16[32,2048]{1,0:T(8,128)(2,1)S(1)}, bf16[32,2048]{1,0:T(8,128)(2,1)S(1)}, u32[]{:S(2)}, u32[]{:S(2)}) collective-permute-start(bf16[32,2048]{1,0:T(8,128)(2,1)S(1)} %shard_map.79), channel_id=1, source_target_pairs={{0,2},{1,3},{2,0},{3,1},{4,6},{5,7},{6,4},{7,5},{8,10},{9,11},{10,... | collective-permute-start | bytes 393224 | tf_op jit(solution)/shard_map/ppermute | solution.py:39
  49.8 1.7 %collective-permute-start.14 = (bf16[32,2048]{1,0:T(8,128)(2,1)S(1)}, bf16[32,2048]{1,0:T(8,128)(2,1)S(1)}, u32[]{:S(2)}, u32[]{:S(2)}) collective-permute-start(bf16[32,2048]{1,0:T(8,128)(2,1)S(1)} %shard_map.83), channel_id=1, source_target_pairs={{0,4},{1,5},{2,6},{3,7},{4,0},{5,1},{6,2},{7,3},{8,12},{9,13},{10,... | collective-permute-start | bytes 393224 | tf_op jit(solution)/shard_map/ppermute | solution.py:39
  51.5 1.4 %collective-permute-done.12.right_ref = bf16[32,2048]{1,0:T(8,128)(2,1)S(1)} collective-permute-done((bf16[32,2048]{1,0:T(8,128)(2,1)S(1)}, bf16[32,2048]{1,0:T(8,128)(2,1)S(1)}, u32[]{:S(2)}, u32[]{:S(2)}) %collective-permute-start.12) | collective-permute-done | bytes 131104 | tf_op jit(solution)/shard_map/ppermute | solution.py:39
  52.9 2.0 %collective-permute-done.10.refs_1_ = bf16[32,2048]{1,0:T(8,128)(2,1)S(1)} collective-permute-done((bf16[32,2048]{1,0:T(8,128)(2,1)S(1)}, bf16[32,2048]{1,0:T(8,128)(2,1)S(1)}, u32[]{:S(2)}, u32[]{:S(2)}) %collective-permute-start.10) | collective-permute-done | bytes 131104 | tf_op jit(solution)/shard_map/ppermute | solution.py:39
  55.0 0.7 %shard_map.84 = bf16[32,4096]{1,0:T(8,128)(2,1)} custom-call(f32[32,2048]{1,0:T(8,128)S(1)} %shard_map.78.refs_0_, bf16[32,2048]{1,0:T(8,128)(2,1)S(1)} %collective-permute-done.10.refs_1_, f32[32,2048]{1,0:T(8,128)S(1)} %shard_map.82.refs_2_, bf16[32,2048]{1,0:T(8,128)(2,1)S(1)} %collective-permute-done.14.refs_3_), custom_call_target="tpu_custom_call" | custom-call | tf_op jit(solution)/shard_map/pallas_call | solution.py:350
  (18 shorter events, 0.7 us)
Async XLA Ops:
  1.2 4.7 %collective-permute-start = (bf16[32,4224]{1,0:T(8,128)(2,1)S(1)}, bf16[32,4224]{1,0:T(8,128)(2,1)S(1)}, u32[]{:S(2)}, u32[]{:S(2)}) collective-permute-start(bf16[32,4224]{1,0:T(8,128)(2,1)S(1)} %shard_map.73.refs_0_), channel_id=1, source_target_pairs={{0,1},{1,0},{2,3},{3,2},{4,5},{5,4},{6,7},{7,6},{8,9},{9,8},{10,11... | collective-permute-start | bytes 811016 | tf_op jit(solution)/shard_map/ppermute | solution.py:39
  1.7 15.5 %collective-permute-start.3 = (bf16[32,4224]{1,0:T(8,128)(2,1)S(1)}, bf16[32,4224]{1,0:T(8,128)(2,1)S(1)}, u32[]{:S(2)}, u32[]{:S(2)}) collective-permute-start(bf16[32,4224]{1,0:T(8,128)(2,1)S(1)} %shard_map.73.refs_0_), channel_id=1, source_target_pairs={{0,6},{1,7},{2,4},{3,5},{4,2},{5,3},{6,0},{7,1},{8,14},{9,15},{10,... | collective-permute-start | bytes 811016 | tf_op jit(solution)/shard_map/ppermute | solution.py:39
  5.2 13.2 %collective-permute-start.2 = (bf16[32,4224]{1,0:T(8,128)(2,1)S(1)}, bf16[32,4224]{1,0:T(8,128)(2,1)S(1)}, u32[]{:S(2)}, u32[]{:S(2)}) collective-permute-start(bf16[32,4224]{1,0:T(8,128)(2,1)S(1)} %shard_map.73.refs_0_), channel_id=1, source_target_pairs={{0,4},{1,5},{2,6},{3,7},{4,0},{5,1},{6,2},{7,3},{8,12},{9,13},{10,... | collective-permute-start | bytes 811016 | tf_op jit(solution)/shard_map/ppermute | solution.py:39
  5.8 12.6 %collective-permute-start.1 = (bf16[32,4224]{1,0:T(8,128)(2,1)S(1)}, bf16[32,4224]{1,0:T(8,128)(2,1)S(1)}, u32[]{:S(2)}, u32[]{:S(2)}) collective-permute-start(bf16[32,4224]{1,0:T(8,128)(2,1)S(1)} %shard_map.73.refs_0_), channel_id=1, source_target_pairs={{0,2},{1,3},{2,0},{3,1},{4,6},{5,7},{6,4},{7,5},{8,10},{9,11},{10,... | collective-permute-start | bytes 811016 | tf_op jit(solution)/shard_map/ppermute | solution.py:39
  18.4 1.5 %collective-permute-start.4 = (bf16[32,4224]{1,0:T(8,128)(2,1)S(1)}, bf16[32,4224]{1,0:T(8,128)(2,1)S(1)}, u32[]{:S(2)}, u32[]{:S(2)}) collective-permute-start(bf16[32,4224]{1,0:T(8,128)(2,1)S(1)} %collective-permute-done.1.refs_2_), channel_id=1, source_target_pairs={{0,1},{1,0},{2,3},{3,2},{4,5},{5,4},{6,7},{7,6},{8,9},{9,8},{10,11... | collective-permute-start | bytes 811016 | tf_op jit(solution)/shard_map/ppermute | solution.py:39
  18.4 1.9 %collective-permute-start.5 = (bf16[32,4224]{1,0:T(8,128)(2,1)S(1)}, bf16[32,4224]{1,0:T(8,128)(2,1)S(1)}, u32[]{:S(2)}, u32[]{:S(2)}) collective-permute-start(bf16[32,4224]{1,0:T(8,128)(2,1)S(1)} %collective-permute-done.2.refs_3_), channel_id=1, source_target_pairs={{0,1},{1,0},{2,3},{3,2},{4,5},{5,4},{6,7},{7,6},{8,9},{9,8},{10,11... | collective-permute-start | bytes 811016 | tf_op jit(solution)/shard_map/ppermute | solution.py:39
  18.9 1.8 %collective-permute-start.6 = (bf16[32,4224]{1,0:T(8,128)(2,1)S(1)}, bf16[32,4224]{1,0:T(8,128)(2,1)S(1)}, u32[]{:S(2)}, u32[]{:S(2)}) collective-permute-start(bf16[32,4224]{1,0:T(8,128)(2,1)S(1)} %collective-permute-done.3.refs_4_), channel_id=1, source_target_pairs={{0,1},{1,0},{2,3},{3,2},{4,5},{5,4},{6,7},{7,6},{8,9},{9,8},{10,11... | collective-permute-start | bytes 811016 | tf_op jit(solution)/shard_map/ppermute | solution.py:39
  37.8 4.1 %collective-permute-start.7 = (bf16[128,2048]{1,0:T(8,128)(2,1)S(1)}, bf16[128,2048]{1,0:T(8,128)(2,1)S(1)}, u32[]{:S(2)}, u32[]{:S(2)}) collective-permute-start(bf16[128,2048]{1,0:T(8,128)(2,1)S(1)} %get-tuple-element.37), channel_id=1, source_target_pairs={{0,1},{1,0},{2,3},{3,2},{4,5},{5,4},{6,7},{7,6},{8,9},{9,8},{10,11... | collective-permute-start | bytes 1572872 | tf_op jit(solution)/shard_map/ppermute | solution.py:39
  41.4 2.1 %collective-permute-start.11 = (bf16[128,2048]{1,0:T(8,128)(2,1)S(1)}, bf16[128,2048]{1,0:T(8,128)(2,1)S(1)}, u32[]{:S(2)}, u32[]{:S(2)}) collective-permute-start(bf16[128,2048]{1,0:T(8,128)(2,1)S(1)} %get-tuple-element.44), channel_id=1, source_target_pairs={{0,1},{1,0},{2,3},{3,2},{4,5},{5,4},{6,7},{7,6},{8,9},{9,8},{10,11... | collective-permute-start | bytes 1572872 | tf_op jit(solution)/shard_map/ppermute | solution.py:39
  42.0 5.6 %collective-permute-start.9 = (bf16[32,2048]{1,0:T(8,128)(2,1)S(1)}, bf16[32,2048]{1,0:T(8,128)(2,1)S(1)}, u32[]{:S(2)}, u32[]{:S(2)}) collective-permute-start(bf16[32,2048]{1,0:T(8,128)(2,1)S(1)} %get-tuple-element.41), channel_id=1, source_target_pairs={{0,4},{1,5},{2,6},{3,7},{4,0},{5,1},{6,2},{7,3},{8,12},{9,13},{10,... | collective-permute-start | bytes 393224 | tf_op jit(solution)/shard_map/ppermute | solution.py:39
  43.6 6.1 %collective-permute-start.13 = (bf16[32,2048]{1,0:T(8,128)(2,1)S(1)}, bf16[32,2048]{1,0:T(8,128)(2,1)S(1)}, u32[]{:S(2)}, u32[]{:S(2)}) collective-permute-start(bf16[32,2048]{1,0:T(8,128)(2,1)S(1)} %get-tuple-element.48), channel_id=1, source_target_pairs={{0,2},{1,3},{2,0},{3,1},{4,6},{5,7},{6,4},{7,5},{8,10},{9,11},{10,... | collective-permute-start | bytes 393224 | tf_op jit(solution)/shard_map/ppermute | solution.py:39
  45.1 6.4 %collective-permute-start.8 = (bf16[32,2048]{1,0:T(8,128)(2,1)S(1)}, bf16[32,2048]{1,0:T(8,128)(2,1)S(1)}, u32[]{:S(2)}, u32[]{:S(2)}) collective-permute-start(bf16[32,2048]{1,0:T(8,128)(2,1)S(1)} %get-tuple-element.39), channel_id=1, source_target_pairs={{0,4},{1,5},{2,6},{3,7},{4,0},{5,1},{6,2},{7,3},{8,12},{9,13},{10,... | collective-permute-start | bytes 393224 | tf_op jit(solution)/shard_map/ppermute | solution.py:39
  46.5 6.4 %collective-permute-start.12 = (bf16[32,2048]{1,0:T(8,128)(2,1)S(1)}, bf16[32,2048]{1,0:T(8,128)(2,1)S(1)}, u32[]{:S(2)}, u32[]{:S(2)}) collective-permute-start(bf16[32,2048]{1,0:T(8,128)(2,1)S(1)} %get-tuple-element.46), channel_id=1, source_target_pairs={{0,2},{1,3},{2,0},{3,1},{4,6},{5,7},{6,4},{7,5},{8,10},{9,11},{10,... | collective-permute-start | bytes 393224 | tf_op jit(solution)/shard_map/ppermute | solution.py:39
  47.6 7.3 %collective-permute-start.10 = (bf16[32,2048]{1,0:T(8,128)(2,1)S(1)}, bf16[32,2048]{1,0:T(8,128)(2,1)S(1)}, u32[]{:S(2)}, u32[]{:S(2)}) collective-permute-start(bf16[32,2048]{1,0:T(8,128)(2,1)S(1)} %shard_map.79), channel_id=1, source_target_pairs={{0,2},{1,3},{2,0},{3,1},{4,6},{5,7},{6,4},{7,5},{8,10},{9,11},{10,... | collective-permute-start | bytes 393224 | tf_op jit(solution)/shard_map/ppermute | solution.py:39
  49.8 5.2 %collective-permute-start.14 = (bf16[32,2048]{1,0:T(8,128)(2,1)S(1)}, bf16[32,2048]{1,0:T(8,128)(2,1)S(1)}, u32[]{:S(2)}, u32[]{:S(2)}) collective-permute-start(bf16[32,2048]{1,0:T(8,128)(2,1)S(1)} %shard_map.83), channel_id=1, source_target_pairs={{0,4},{1,5},{2,6},{3,7},{4,0},{5,1},{6,2},{7,3},{8,12},{9,13},{10,... | collective-permute-start | bytes 393224 | tf_op jit(solution)/shard_map/ppermute | solution.py:39
